TPU v7x, 32 devices: a whole 2x2x4 slice. The times are simulated.
32 devices in a mesh: gx: 4 (over y, x), gy: 8 (over z, core).
Axes of the slice: x: 2, y: 2, z: 4, core: 2. Of those that a mesh axis runs over, the one named last changes fastest.
Arguments:
- layer_in: bfloat16 [2, 2048, 1024], P(None, ('gx', 'gy')), may hold values from -6 to 6
- first_layer_value: bfloat16 [2, 2048, 1024], P(None, ('gx', 'gy')), may hold values from -6 to 6
- v1_acc: float32 [2, 2048, 1024], P(None, ('gx', 'gy')), may hold values from -6 to 6
- cotangent: bfloat16 [2, 2048, 1024], P(None, ('gx', 'gy')), may hold values from -6 to 6
- seq_starts: int32 [2, 11], replicated, may hold values from 0 to 1920, as said below
- norm1_gain: bfloat16 [1024], P(('gx', 'gy')), may hold values from 0.5 to 1.5
- w_query: bfloat16 [1024, 1024], P(('gx', 'gy')), may hold values from -0.1875 to 0.1875
- w_key: bfloat16 [1024, 1024], P(('gx', 'gy')), may hold values from -0.1875 to 0.1875
- w_value: bfloat16 [1024, 1024], P(('gx', 'gy')), may hold values from -0.1875 to 0.1875
- w_out: bfloat16 [1024, 1024], P(('gx', 'gy')), may hold values from -1.5 to 1.5
- norm2_gain: bfloat16 [1024], P(('gx', 'gy')), may hold values from 0.5 to 1.5
- w_gate: bfloat16 [1024, 2816], P(('gx', 'gy')), may hold values from -0.1875 to 0.1875
- w_up: bfloat16 [1024, 2816], P(('gx', 'gy')), may hold values from -0.1875 to 0.1875
- w_down: bfloat16 [2816, 1024], P(('gx', 'gy')), may hold values from -0.109375 to 0.109375
Outputs:
- layer_out: bfloat16 [2, 2048, 1024], P(None, ('gx', 'gy'))
- input_grad: float32 [2, 2048, 1024], P(None, ('gx', 'gy'))
- v1_acc_out: float32 [2, 2048, 1024], P(None, ('gx', 'gy'))
- norm1_gain_grad: float32 [1024], P(('gx', 'gy'))
- w_query_grad: float32 [1024, 1024], P(('gx', 'gy'))
- w_key_grad: float32 [1024, 1024], P(('gx', 'gy'))
- w_value_grad: float32 [1024, 1024], P(('gx', 'gy'))
- output_weight_gradient: float32 [1024, 1024], P(('gx', 'gy'))
- norm2_gain_grad: float32 [1024], P(('gx', 'gy'))
- w_gate_grad: float32 [1024, 2816], P(('gx', 'gy'))
- w_up_grad: float32 [1024, 2816], P(('gx', 'gy'))
- w_down_grad: float32 [2816, 1024], P(('gx', 'gy'))
Inputs may be any that keep to these rules, and one draw needn't show every extreme that they name: `seq_starts`: sorted ascending within each micro-batch; each sequence runs to the next start or to the end of the micro-batch. Every block of 512 rows holds whole sequences: one of 512, two of 256, or four of 128, in 1, 1 and 2 of the blocks of each micro-batch.
All inputs are finite; a program needn't handle non-finite values.
Results may differ from a plain program's by a relative error of at most 0.03.
Values may be sent and summed in bfloat16 or wider, within the bound.
No kernel may reach another device: no remote copies, remote signals or barrier semaphores. Data moves between devices by JAX's collectives and lax.ppermute only.
A program may use at most 320 MiB of HBM per device.

v0:
```python
import jax
import jax.numpy as jnp
from jax import lax
from jax.sharding import PartitionSpec as P

D = 1024
H = 16
HD = 64
MICRO = 2


EPS = 1e-05
NEG = -1e30
SCORE_SCALE = 0.125


def shortened(value):

    def short(part):
        return part.astype(jnp.bfloat16) if part.dtype == jnp.float32 else part

    return jax.tree.map(short, value)


def norm_apply(hidden_in, gain):
    return (
        hidden_in * lax.rsqrt(jnp.mean(hidden_in * hidden_in, axis=-1, keepdims=True) + EPS) * gain
    )


def rotary(values, positions):
    half_dim = values.shape[-1] // 2
    frequency = 10000.0 ** (-(jnp.arange(half_dim, dtype=jnp.float32) * 2.0 / values.shape[-1]))
    angles = positions.astype(jnp.float32)[:, None] * frequency[None, :]
    cosine = jnp.cos(angles)[:, None, :]
    sine_part = jnp.sin(angles)[:, None, :]
    first_half = values[..., :half_dim]
    second_half = values[..., half_dim:]
    return jnp.concatenate(
        [
            first_half * cosine - second_half * sine_part,
            second_half * cosine + first_half * sine_part,
        ],
        axis=-1,
    )


def seq_start_of(positions, starts):
    return jnp.max(jnp.where(starts[None, :] <= positions[:, None], starts[None, :], 0), axis=1)


def dot_rows(left, right):
    return lax.dot_general(
        left, right, (((0,), (0,)), ((), ())), preferred_element_type=jnp.float32
    )


def dot_cols(left, right):
    return lax.dot_general(
        left, right, (((1,), (1,)), ((), ())), preferred_element_type=jnp.float32
    )


def fetch_attention(shards):
    return jax.tree.map(
        lambda part, own: part.astype(own.dtype),
        lax.all_gather(shortened(shards), ("gx", "gy"), axis=0, tiled=True),
        shards,
    )


def fetch_feed(shards):
    return jax.tree.map(
        lambda part, own: part.astype(own.dtype),
        lax.all_gather(shortened(shards), ("gx", "gy"), axis=0, tiled=True),
        shards,
    )


def reduce_grads(full_grads):
    gain_one_g, query_g, key_g, value_g, out_g, gain_two_g, gate_g, up_g, down_g = full_grads
    half_cols = up_g.shape[1] // 2
    attn_part = (
        lax.psum_scatter(gain_one_g, ("gx", "gy"), scatter_dimension=0, tiled=True),
        lax.psum_scatter(query_g, ("gx", "gy"), scatter_dimension=0, tiled=True),
        lax.psum_scatter(key_g, ("gx", "gy"), scatter_dimension=0, tiled=True),
        lax.psum_scatter(value_g, ("gx", "gy"), scatter_dimension=0, tiled=True),
        lax.psum_scatter(out_g, ("gx", "gy"), scatter_dimension=0, tiled=True),
    )
    feed_first = (
        lax.psum_scatter(gain_two_g, ("gx", "gy"), scatter_dimension=0, tiled=True),
        lax.psum_scatter(gate_g, ("gx", "gy"), scatter_dimension=0, tiled=True),
        lax.psum_scatter(up_g[:, :half_cols], ("gx", "gy"), scatter_dimension=0, tiled=True),
    )
    feed_second = (
        lax.psum_scatter(up_g[:, half_cols:], ("gx", "gy"), scatter_dimension=0, tiled=True),
        lax.psum_scatter(down_g, ("gx", "gy"), scatter_dimension=0, tiled=True),
    )
    up_shard = jnp.concatenate([feed_first[2], feed_second[0]], axis=1)
    return tuple(attn_part) + (feed_first[0], feed_first[1], up_shard, feed_second[1])


def piece_visible(number_rows, row_base, starts, own_loc, own_seq, own_is_query):
    other_loc = jnp.arange(number_rows, dtype=jnp.int32)
    other_seq = seq_start_of(other_loc + row_base, starts)
    if own_is_query:
        return (other_seq[None, :] == own_seq[:, None]) & (other_loc[None, :] <= own_loc[:, None])
    return (own_seq[None, :] == other_seq[:, None]) & (own_loc[None, :] <= other_loc[:, None])


def attention_forward(heads_of_query, key_rows, value_rows, own_loc, own_seq, row_base, starts):
    local_rows = key_rows.shape[0]
    initial = (
        jnp.full((H, local_rows), NEG, jnp.float32),
        jnp.zeros((H, local_rows), jnp.float32),
        jnp.zeros((H, local_rows, HD), jnp.float32),
    )

    def absorb(running, pieces, offset):
        key_block, value_block = pieces
        number_rows = key_block.shape[0]
        visible = piece_visible(number_rows, row_base, starts, own_loc, own_seq, True)

        def work(state):
            row_max, denom_sum, accum = state
            scores = (
                jnp.einsum(
                    "htd,nhd->htn",
                    heads_of_query,
                    key_block.reshape(number_rows, H, HD),
                    preferred_element_type=jnp.float32,
                )
                * SCORE_SCALE
            )
            scores = jnp.where(visible[None], scores, NEG)
            new_max = jnp.maximum(row_max, jnp.max(scores, axis=-1))
            expo_vals = jnp.where(visible[None], jnp.exp(scores - new_max[..., None]), 0.0)
            denom_sum = jnp.sum(expo_vals, axis=-1)
            accum = jnp.einsum(
                "htn,nhd->htd",
                expo_vals.astype(jnp.bfloat16),
                value_block.reshape(number_rows, H, HD),
                preferred_element_type=jnp.float32,
            )
            return (new_max, denom_sum, accum)

        return lax.cond(jnp.any(visible), work, lambda state: state, running)

    return absorb(
        initial,
        (
            lax.all_gather(key_rows, "gy", axis=0, tiled=True),
            lax.all_gather(value_rows, "gy", axis=0, tiled=True),
        ),
        jnp.int32(0),
    )


def attention_queries(
    heads_of_query,
    head_gradient,
    log_norm,
    row_delta,
    key_rows,
    value_rows,
    own_loc,
    own_seq,
    row_base,
    starts,
):
    local_rows = key_rows.shape[0]
    initial = jnp.zeros((H, local_rows, HD), jnp.float32)

    def absorb(running, pieces, offset):
        key_block, value_block = pieces
        number_rows = key_block.shape[0]
        visible = piece_visible(number_rows, row_base, starts, own_loc, own_seq, True)

        def work(grad_query):
            heads_of_key = key_block.reshape(number_rows, H, HD)
            scores = (
                jnp.einsum(
                    "htd,nhd->htn", heads_of_query, heads_of_key, preferred_element_type=jnp.float32
                )
                * SCORE_SCALE
            )
            softmax_w = jnp.where(visible[None], jnp.exp(scores - log_norm[..., None]), 0.0)
            grad_probs = jnp.einsum(
                "htd,nhd->htn",
                head_gradient,
                value_block.reshape(number_rows, H, HD),
                preferred_element_type=jnp.float32,
            )
            score_gradient = (softmax_w * (grad_probs - row_delta[..., None])).astype(jnp.bfloat16)
            return (
                jnp.einsum(
                    "htn,nhd->htd", score_gradient, heads_of_key, preferred_element_type=jnp.float32
                )
                * SCORE_SCALE
            )

        return lax.cond(jnp.any(visible), work, lambda state: state, running)

    return absorb(
        initial,
        (
            lax.all_gather(key_rows, "gy", axis=0, tiled=True),
            lax.all_gather(value_rows, "gy", axis=0, tiled=True),
        ),
        jnp.int32(0),
    )


def attention_keys(
    heads_of_key,
    heads_of_value,
    query_rows,
    grad_rows,
    row_stats,
    own_loc,
    own_seq,
    row_base,
    starts,
):
    local_rows = query_rows.shape[0]
    initial = (
        jnp.zeros((H, local_rows, HD), jnp.float32),
        jnp.zeros((H, local_rows, HD), jnp.float32),
    )

    def absorb(running, pieces, offset):
        query_block, grad_block, stat_block = pieces
        number_rows = query_block.shape[0]
        visible = piece_visible(number_rows, row_base, starts, own_loc, own_seq, False)

        def work(state):
            stat_vals = stat_block.astype(jnp.float32)
            norm_piece = jnp.transpose(stat_vals[:, :H] + stat_vals[:, H : 2 * H])
            delta_piece = jnp.transpose(stat_vals[:, 2 * H : 3 * H] + stat_vals[:, 3 * H :])
            heads_of_query = query_block.reshape(number_rows, H, HD)
            head_gradient = grad_block.reshape(number_rows, H, HD)
            scores = (
                jnp.einsum(
                    "rli,lbi->lrb", heads_of_query, heads_of_key, preferred_element_type=jnp.float32
                )
                * SCORE_SCALE
            )
            softmax_w = jnp.where(visible[None], jnp.exp(scores - norm_piece[..., None]), 0.0)
            grad_value = jnp.einsum(
                "bfs,fbr->bsr",
                softmax_w.astype(jnp.bfloat16),
                head_gradient,
                preferred_element_type=jnp.float32,
            )
            grad_probs = jnp.einsum(
                "rli,lbi->lrb", head_gradient, heads_of_value, preferred_element_type=jnp.float32
            )
            score_gradient = (softmax_w * (grad_probs - delta_piece[..., None])).astype(
                jnp.bfloat16
            )
            grad_key = (
                jnp.einsum(
                    "bfs,fbr->bsr",
                    score_gradient,
                    heads_of_query,
                    preferred_element_type=jnp.float32,
                )
                * SCORE_SCALE
            )
            return (grad_key, grad_value)

        return lax.cond(jnp.any(visible), work, lambda state: state, running)

    return absorb(
        initial,
        (
            lax.all_gather(query_rows, "gy", axis=0, tiled=True),
            lax.all_gather(grad_rows, "gy", axis=0, tiled=True),
            lax.all_gather(row_stats, "gy", axis=0, tiled=True),
        ),
        jnp.int32(0),
    )


def split_pair(values):
    upper = values.astype(jnp.bfloat16)
    lower = (values - upper.astype(jnp.float32)).astype(jnp.bfloat16)
    return (upper, lower)


def local(
    layer_in,
    first_layer_value,
    v1_acc,
    cotangent,
    seq_starts,
    norm1_gain,
    w_query,
    w_key,
    w_value,
    w_out,
    norm2_gain,
    w_gate,
    w_up,
    w_down,
):
    local_rows = layer_in.shape[1]
    row_len = lax.axis_size("gy") * local_rows
    row_base = lax.axis_index("gx") * row_len
    own_loc = lax.axis_index("gy") * local_rows + jnp.arange(local_rows, dtype=jnp.int32)
    attn_shards = (norm1_gain, w_query, w_key, w_value, w_out)
    feed_shards = (norm2_gain, w_gate, w_up, w_down)
    attn_full = fetch_attention(attn_shards)
    feed_full = fetch_feed(feed_shards)
    outputs = []
    input_grads = []
    accums = []
    grad_total = None
    for micro_step in range(MICRO):
        starts = seq_starts[micro_step]
        own_seq = seq_start_of(own_loc + row_base, starts)
        own_rel = own_loc + row_base - own_seq
        gain_one, query_w, key_w, value_w, out_w = attn_full
        gain_two, gate_w, up_w, down_w = feed_full
        x_in = layer_in[micro_step].astype(jnp.float32)
        gain_one_f = gain_one.astype(jnp.float32)
        gain_two_f = gain_two.astype(jnp.float32)
        normed_one = norm_apply(x_in, gain_one_f).astype(jnp.bfloat16)
        query_pre = jnp.dot(normed_one, query_w, preferred_element_type=jnp.float32).reshape(
            local_rows, H, HD
        )
        key_pre = jnp.dot(normed_one, key_w, preferred_element_type=jnp.float32).reshape(
            local_rows, H, HD
        )
        value_pre = jnp.dot(normed_one, value_w, preferred_element_type=jnp.float32)
        query_rot = rotary(query_pre, own_rel).astype(jnp.bfloat16)
        key_rot = rotary(key_pre, own_rel).astype(jnp.bfloat16)
        blended = (
            0.5 * value_pre + 0.5 * first_layer_value[micro_step].astype(jnp.float32)
        ).astype(jnp.bfloat16)
        heads_of_query = jnp.transpose(query_rot, (1, 0, 2))
        key_rows = key_rot.reshape(local_rows, D)
        row_max, denom_sum, accum = attention_forward(
            heads_of_query, key_rows, blended, own_loc, own_seq, row_base, starts
        )
        log_norm = row_max + jnp.log(denom_sum)
        attn_f = accum / denom_sum[..., None]
        attn_low = jnp.transpose(attn_f, (1, 0, 2)).reshape(local_rows, D).astype(jnp.bfloat16)
        after_attn = x_in + jnp.dot(attn_low, out_w, preferred_element_type=jnp.float32)
        normed_two = norm_apply(after_attn, gain_two_f).astype(jnp.bfloat16)
        gate_pre = jnp.dot(normed_two, gate_w, preferred_element_type=jnp.float32)
        up_pre = jnp.dot(normed_two, up_w, preferred_element_type=jnp.float32)
        hidden = (jax.nn.silu(gate_pre) * up_pre).astype(jnp.bfloat16)
        result = after_attn + jnp.dot(hidden, down_w, preferred_element_type=jnp.float32)
        outputs.append(result.astype(jnp.bfloat16))
        gain_one, query_w, key_w, value_w, out_w = attn_full
        gain_two, gate_w, up_w, down_w = feed_full
        grad_out = cotangent[micro_step].astype(jnp.float32)
        grad_low = cotangent[micro_step]
        grad_down_w = dot_rows(hidden, grad_low)
        grad_hidden = dot_cols(grad_low, down_w)
        swiglu_out, swiglu_pull = jax.vjp(
            lambda gate_in, up_in: jax.nn.silu(gate_in) * up_in, gate_pre, up_pre
        )
        grad_gate, grad_up = swiglu_pull(grad_hidden)
        grad_gate = grad_gate.astype(jnp.bfloat16)
        grad_up = grad_up.astype(jnp.bfloat16)
        grad_gate_w = dot_rows(normed_two, grad_gate)
        grad_up_w = dot_rows(normed_two, grad_up)
        grad_normed_two = dot_cols(grad_gate, gate_w) + dot_cols(grad_up, up_w)
        norm_two_out, norm_two_pull = jax.vjp(norm_apply, after_attn, gain_two_f)
        grad_after_part, grad_gain_two = norm_two_pull(grad_normed_two)
        grad_after = grad_out + grad_after_part
        grad_branch = grad_after.astype(jnp.bfloat16)
        grad_out_w = dot_rows(attn_low, grad_branch)
        grad_attn = dot_cols(grad_branch, out_w).astype(jnp.bfloat16)
        head_gradient = jnp.transpose(grad_attn.reshape(local_rows, H, HD), (1, 0, 2))
        row_delta = jnp.sum(head_gradient.astype(jnp.float32) * attn_f, axis=-1)
        norm_upper, norm_lower = split_pair(jnp.transpose(log_norm))
        delta_upper, delta_lower = split_pair(jnp.transpose(row_delta))
        row_stats = jnp.concatenate([norm_upper, norm_lower, delta_upper, delta_lower], axis=1)
        grad_query = attention_queries(
            heads_of_query,
            head_gradient,
            log_norm,
            row_delta,
            key_rows,
            blended,
            own_loc,
            own_seq,
            row_base,
            starts,
        )
        heads_of_key = jnp.transpose(key_rot, (1, 0, 2))
        heads_of_value = jnp.transpose(blended.reshape(local_rows, H, HD), (1, 0, 2))
        grad_key, grad_blend = attention_keys(
            heads_of_key,
            heads_of_value,
            query_rot.reshape(local_rows, D),
            grad_attn,
            row_stats,
            own_loc,
            own_seq,
            row_base,
            starts,
        )
        rotary_out, rotary_pull = jax.vjp(lambda rotated_in: rotary(rotated_in, own_rel), query_pre)
        grad_query_pre = (
            rotary_pull(jnp.transpose(grad_query, (1, 0, 2)))[0]
            .reshape(local_rows, D)
            .astype(jnp.bfloat16)
        )
        grad_key_pre = (
            rotary_pull(jnp.transpose(grad_key, (1, 0, 2)))[0]
            .reshape(local_rows, D)
            .astype(jnp.bfloat16)
        )
        grad_blend_rows = jnp.transpose(grad_blend, (1, 0, 2)).reshape(local_rows, D)
        grad_value_pre = (0.5 * grad_blend_rows).astype(jnp.bfloat16)
        accums.append(v1_acc[micro_step] + 0.5 * grad_blend_rows)
        query_weight_gradient = dot_rows(normed_one, grad_query_pre)
        grad_key_w = dot_rows(normed_one, grad_key_pre)
        grad_value_w = dot_rows(normed_one, grad_value_pre)
        grad_normed_one = (
            dot_cols(grad_query_pre, query_w)
            + dot_cols(grad_key_pre, key_w)
            + dot_cols(grad_value_pre, value_w)
        )
        norm_one_out, norm_one_pull = jax.vjp(norm_apply, x_in, gain_one_f)
        grad_x_part, grad_gain_one = norm_one_pull(grad_normed_one)
        input_grads.append(grad_after + grad_x_part)
        full_grads = (
            grad_gain_one,
            query_weight_gradient,
            grad_key_w,
            grad_value_w,
            grad_out_w,
            grad_gain_two,
            grad_gate_w,
            grad_up_w,
            grad_down_w,
        )
        shard_grads = reduce_grads(full_grads)
        grad_total = (
            shard_grads
            if grad_total is None
            else tuple((old_g + new_g for old_g, new_g in zip(grad_total, shard_grads)))
        )
    return (
        jnp.stack(outputs),
        jnp.stack(input_grads),
        jnp.stack(accums),
        grad_total[0],
        grad_total[1],
        grad_total[2],
        grad_total[3],
        grad_total[4],
        grad_total[5],
        grad_total[6],
        grad_total[7],
        grad_total[8],
    )


def solution(mesh):
    return jax.shard_map(
        local,
        mesh=mesh,
        in_specs=(
            P(None, ("gx", "gy"), None),
            P(None, ("gx", "gy"), None),
            P(None, ("gx", "gy"), None),
            P(None, ("gx", "gy"), None),
            P(),
            P(("gx", "gy")),
            P(("gx", "gy"), None),
            P(("gx", "gy"), None),
            P(("gx", "gy"), None),
            P(("gx", "gy"), None),
            P(("gx", "gy")),
            P(("gx", "gy"), None),
            P(("gx", "gy"), None),
            P(("gx", "gy"), None),
        ),
        out_specs=(
            P(None, ("gx", "gy"), None),
            P(None, ("gx", "gy"), None),
            P(None, ("gx", "gy"), None),
            P(("gx", "gy")),
            P(("gx", "gy"), None),
            P(("gx", "gy"), None),
            P(("gx", "gy"), None),
            P(("gx", "gy"), None),
            P(("gx", "gy")),
            P(("gx", "gy"), None),
            P(("gx", "gy"), None),
            P(("gx", "gy"), None),
        ),
        check_vma=False,
    )
```

profile of v0, /device:TPU:0, one launch (start us, length us, event | category | flops | bytes accessed | tf_op | source)
XLA Modules:
  0.0 2124.3 jit_solution(6563933128141417355)
XLA Ops:
  11.1 42.1 %all-reduce.13 = (bf16[1024]{0:T(1024)(128)(2,1)S(1)}, bf16[1024]{0:T(1024)(128)(2,1)S(1)}) all-reduce(bf16[1024]{0:T(1024)(128)(2,1)S(1)} %dynamic-update-slice, bf16[1024]{0:T(1024)(128)(2,1)S(1)} %dynamic-update-slice.1), channel_id=1, replica_groups=mesh['gx'=4,'gy'=8] {'gx','gy'}, use_global_device_ids=true, to_apply=%add.8 | all-reduce | flops 2048 | bytes 8192
  56.0 14.2 all-gather.20.cloned.1.call-done
  73.1 55.5 %all-gather.16.cloned.1.call-done = bf16[1024,1024]{1,0:T(8,128)(2,1)} async-done(((bf16[32,1024]{1,0:T(8,128)(2,1)}), bf16[1024,1024]{1,0:T(8,128)(2,1)}) %all-gather.16.cloned.1.call-update) | async-done | bytes 2097168 | tf_op jit(solution)/shard_map/all_gather | solution.py:67
  136.7 50.3 %all-gather.22.cloned.1.call-done = bf16[1024,1024]{1,0:T(8,128)(2,1)} async-done(((bf16[32,1024]{1,0:T(8,128)(2,1)}), bf16[1024,1024]{1,0:T(8,128)(2,1)}) %all-gather.22.cloned.1.call-update) | async-done | bytes 2097168 | tf_op jit(solution)/shard_map/all_gather | solution.py:67
  210.0 23.7 %all-gather.36.cloned.1.call-done = bf16[512,1024]{1,0:T(8,128)(2,1)} async-done(((bf16[64,1024]{1,0:T(8,128)(2,1)}), bf16[512,1024]{1,0:T(8,128)(2,1)}) %all-gather.36.cloned.1.call-update) | async-done | bytes 1048592 | tf_op jit(solution)/shard_map/all_gather | solution.py:153
  257.6 23.9 %all-gather.24.cloned.1.call-done = bf16[512,1024]{1,0:T(8,128)(2,1)} async-done(((bf16[64,1024]{1,0:T(8,128)(2,1)}), bf16[512,1024]{1,0:T(8,128)(2,1)}) %all-gather.24.cloned.1.call-update) | async-done | bytes 1048592 | tf_op jit(solution)/shard_map/all_gather | solution.py:153
  298.9 41.8 %all-gather.26.cloned.1.call-done = bf16[1024,1024]{1,0:T(8,128)(2,1)} async-done(((bf16[32,1024]{1,0:T(8,128)(2,1)}), bf16[1024,1024]{1,0:T(8,128)(2,1)}) %all-gather.26.cloned.1.call-update) | async-done | bytes 2097168 | tf_op jit(solution)/shard_map/all_gather | solution.py:67
  344.8 64.8 %all-gather.28.cloned.1.call-done = bf16[1024,2816]{1,0:T(8,128)(2,1)} async-done(((bf16[32,2816]{1,0:T(8,128)(2,1)}), bf16[1024,2816]{1,0:T(8,128)(2,1)}) %all-gather.28.cloned.1.call-update) | async-done | bytes 5767184 | tf_op jit(solution)/shard_map/all_gather | solution.py:75
  414.3 64.4 %all-gather.30.cloned.1.call-done = bf16[1024,2816]{1,0:T(8,128)(2,1)} async-done(((bf16[32,2816]{1,0:T(8,128)(2,1)}), bf16[1024,2816]{1,0:T(8,128)(2,1)}) %all-gather.30.cloned.1.call-update) | async-done | bytes 5767184 | tf_op jit(solution)/shard_map/all_gather | solution.py:75
  483.3 64.6 %all-gather.32.cloned.1.call-done = bf16[2816,1024]{1,0:T(8,128)(2,1)} async-done(((bf16[88,1024]{1,0:T(8,128)(2,1)}), bf16[2816,1024]{1,0:T(8,128)(2,1)}) %all-gather.32.cloned.1.call-update) | async-done | bytes 5767184 | tf_op jit(solution)/shard_map/all_gather | solution.py:75
  665.8 15.4 all_gather.78
  681.2 15.3 all_gather.75
  696.5 15.5 conditional.11
  714.1 15.5 conditional.9
  799.3 38.9 %all-reduce.12 = (f32[1024]{0:T(1024)S(1)}, f32[1024]{0:T(1024)S(1)}) all-reduce(f32[1024]{0:T(1024)S(1)} %add.335, f32[1024]{0:T(1024)S(1)} %add.340), channel_id=10, replica_groups=mesh['gx'=4,'gy'=8] {'gx','gy'}, use_global_device_ids=true, to_apply=%region_35.36.clone | all-reduce | flops 2048 | bytes 16384
  841.4 94.2 %reduce-scatter.11.cloned.1.call-done = f32[32,1408]{1,0:T(8,128)} async-done(((f32[1024,1408]{1,0:T(8,128)}), f32[32,1408]{1,0:T(8,128)}) %reduce-scatter.11.cloned.1.call-update) | async-done | bytes 180240 | tf_op jit(solution)/shard_map/reduce_scatter | solution.py:93
  935.6 144.6 %reduce-scatter.17.cloned.1.call-done = f32[32,1408]{1,0:T(8,128)} async-done(((f32[1024,1408]{1,0:T(8,128)}), f32[32,1408]{1,0:T(8,128)}) %reduce-scatter.17.cloned.1.call-update) | async-done | bytes 180240 | tf_op jit(solution)/shard_map/reduce_scatter | solution.py:96
  1080.2 146.0 %reduce-scatter.15.cloned.1.call-done = f32[32,1408]{1,0:T(8,128)} async-done(((f32[1024,1408]{1,0:T(8,128)}), f32[32,1408]{1,0:T(8,128)}) %reduce-scatter.15.cloned.1.call-update) | async-done | bytes 180240 | tf_op jit(solution)/shard_map/reduce_scatter | solution.py:93
  1228.2 140.9 %reduce-scatter.25.cloned.1.call-done = f32[32,1024]{1,0:T(8,128)} async-done(((f32[1024,1024]{1,0:T(8,128)}), f32[32,1024]{1,0:T(8,128)}) %reduce-scatter.25.cloned.1.call-update) | async-done | bytes 131088 | tf_op jit(solution)/shard_map/reduce_scatter | solution.py:88
  1369.1 142.2 %reduce-scatter.19.cloned.1.call-done = f32[32,1024]{1,0:T(8,128)} async-done(((f32[1024,1024]{1,0:T(8,128)}), f32[32,1024]{1,0:T(8,128)}) %reduce-scatter.19.cloned.1.call-update) | async-done | bytes 131088 | tf_op jit(solution)/shard_map/reduce_scatter | solution.py:85
  1511.3 142.3 %reduce-scatter.21.cloned.1.call-done = f32[32,1024]{1,0:T(8,128)} async-done(((f32[1024,1024]{1,0:T(8,128)}), f32[32,1024]{1,0:T(8,128)}) %reduce-scatter.21.cloned.1.call-update) | async-done | bytes 131088 | tf_op jit(solution)/shard_map/reduce_scatter | solution.py:86
  1653.6 142.5 %reduce-scatter.23.cloned.1.call-done = f32[32,1024]{1,0:T(8,128)} async-done(((f32[1024,1024]{1,0:T(8,128)}), f32[32,1024]{1,0:T(8,128)}) %reduce-scatter.23.cloned.1.call-update) | async-done | bytes 131088 | tf_op jit(solution)/shard_map/reduce_scatter | solution.py:87
  1796.1 160.1 %reduce-scatter.27.cloned.1.call-done = f32[32,2816]{1,0:T(8,128)} async-done(((f32[1024,2816]{1,0:T(8,128)}), f32[32,2816]{1,0:T(8,128)}) %reduce-scatter.27.cloned.1.call-update) | async-done | bytes 360464 | tf_op jit(solution)/shard_map/reduce_scatter | solution.py:92
  1956.2 161.2 %reduce-scatter.29.cloned.1.call-done = f32[88,1024]{1,0:T(8,128)} async-done(((f32[2816,1024]{1,0:T(8,128)}), f32[88,1024]{1,0:T(8,128)}) %reduce-scatter.29.cloned.1.call-update) | async-done | bytes 360464 | tf_op jit(solution)/shard_map/reduce_scatter | solution.py:97
  (456 shorter events, 364.0 us)
Async XLA Ops:
  7.9 120.7 %all-gather.16.cloned.1.call-start = ((), (), s32[]{:S(2)}) async-start(), calls=%async_computation.10 | async-start | bytes 2162688 | tf_op jit(solution)/shard_map/all_gather | solution.py:67
  8.7 178.3 %all-gather.22.cloned.1.call-start = ((), (), s32[]{:S(2)}) async-start(), calls=%async_computation.13 | async-start | bytes 2162688 | tf_op jit(solution)/shard_map/all_gather | solution.py:67
  9.4 200.6 %all-gather.34.cloned.1.call-start = ((), (), s32[]{:S(2)}) async-start(), calls=%async_computation.19 | async-start | bytes 1179648 | tf_op jit(solution)/shard_map/all_gather | solution.py:152
  136.6 97.1 %all-gather.36.cloned.1.call-start = ((), (), s32[]{:S(2)}) async-start(), calls=%async_computation.20 | async-start | bytes 1179648 | tf_op jit(solution)/shard_map/all_gather | solution.py:153
  189.7 67.8 %all-gather.18.cloned.1.call-start = ((), (), s32[]{:S(2)}) async-start(), calls=%async_computation.11 | async-start | bytes 1179648 | tf_op jit(solution)/shard_map/all_gather | solution.py:152
  193.9 87.6 %all-gather.24.cloned.1.call-start = ((), (), s32[]{:S(2)}) async-start(), calls=%async_computation.14 | async-start | bytes 1179648 | tf_op jit(solution)/shard_map/all_gather | solution.py:153
  195.2 145.5 %all-gather.26.cloned.1.call-start = ((), (), s32[]{:S(2)}) async-start(), calls=%async_computation.15 | async-start | bytes 2162688 | tf_op jit(solution)/shard_map/all_gather | solution.py:67
  195.9 213.7 %all-gather.28.cloned.1.call-start = ((), (), s32[]{:S(2)}) async-start(), calls=%async_computation.16 | async-start | bytes 5947392 | tf_op jit(solution)/shard_map/all_gather | solution.py:75
  196.6 282.0 %all-gather.30.cloned.1.call-start = ((), (), s32[]{:S(2)}) async-start(), calls=%async_computation.17 | async-start | bytes 5947392 | tf_op jit(solution)/shard_map/all_gather | solution.py:75
  197.2 350.6 %all-gather.32.cloned.1.call-start = ((), (), s32[]{:S(2)}) async-start(), calls=%async_computation.18 | async-start | bytes 5947392 | tf_op jit(solution)/shard_map/all_gather | solution.py:75
  198.0 498.6 %all-gather.42.cloned.1.call-start = ((), (), s32[]{:S(2)}) async-start(), calls=%async_computation.23 | async-start | bytes 1179648 | tf_op jit(solution)/shard_map/all_gather | solution.py:277
  203.3 493.2 %all-gather.44.cloned.1.call-start = ((), (), s32[]{:S(2)}) async-start(), calls=%async_computation.24 | async-start | bytes 1179648 | tf_op jit(solution)/shard_map/all_gather | solution.py:278
  573.5 140.6 %all-gather.38.cloned.1.call-start = ((), (), s32[]{:S(2)}) async-start(), calls=%async_computation.21 | async-start | bytes 1179648 | tf_op jit(solution)/shard_map/all_gather | solution.py:277
  576.1 138.0 %all-gather.40.cloned.1.call-start = ((), (), s32[]{:S(2)}) async-start(), calls=%async_computation.22 | async-start | bytes 1179648 | tf_op jit(solution)/shard_map/all_gather | solution.py:278
  579.5 261.8 %reduce-scatter.13.cloned.1.call-start = ((), (), s32[]{:S(2)}) async-start(), calls=%async_computation.26 | async-start | bytes 5947392 | tf_op jit(solution)/shard_map/reduce_scatter | solution.py:96
  595.9 339.7 %reduce-scatter.11.cloned.1.call-start = ((), (), s32[]{:S(2)}) async-start(), calls=%async_computation.25 | async-start | bytes 5947392 | tf_op jit(solution)/shard_map/reduce_scatter | solution.py:93
  596.5 483.7 %reduce-scatter.17.cloned.1.call-start = ((), (), s32[]{:S(2)}) async-start(), calls=%async_computation.28 | async-start | bytes 5947392 | tf_op jit(solution)/shard_map/reduce_scatter | solution.py:96
  613.2 613.0 %reduce-scatter.15.cloned.1.call-start = ((), (), s32[]{:S(2)}) async-start(), calls=%async_computation.27 | async-start | bytes 5947392 | tf_op jit(solution)/shard_map/reduce_scatter | solution.py:93
  614.0 755.1 %reduce-scatter.25.cloned.1.call-start = ((), (), s32[]{:S(2)}) async-start(), calls=%async_computation.32 | async-start | bytes 4325376 | tf_op jit(solution)/shard_map/reduce_scatter | solution.py:88
  618.5 892.8 %reduce-scatter.19.cloned.1.call-start = ((), (), s32[]{:S(2)}) async-start(), calls=%async_computation.29 | async-start | bytes 4325376 | tf_op jit(solution)/shard_map/reduce_scatter | solution.py:85
  738.8 914.8 %reduce-scatter.21.cloned.1.call-start = ((), (), s32[]{:S(2)}) async-start(), calls=%async_computation.30 | async-start | bytes 4325376 | tf_op jit(solution)/shard_map/reduce_scatter | solution.py:86
  745.6 1050.4 %reduce-scatter.23.cloned.1.call-start = ((), (), s32[]{:S(2)}) async-start(), calls=%async_computation.31 | async-start | bytes 4325376 | tf_op jit(solution)/shard_map/reduce_scatter | solution.py:87
  757.5 1198.6 %reduce-scatter.27.cloned.1.call-start = ((), (), s32[]{:S(2)}) async-start(), calls=%async_computation.33 | async-start | bytes 11894784 | tf_op jit(solution)/shard_map/reduce_scatter | solution.py:92
  766.3 1351.0 %reduce-scatter.29.cloned.1.call-start = ((), (), s32[]{:S(2)}) async-start(), calls=%async_computation.34 | async-start | bytes 11894784 | tf_op jit(solution)/shard_map/reduce_scatter | solution.py:97
  (108 other events, 2396.4 us)
Sparse Core Ops, SparseCore 0:
  11.0 59.1 all-gather.19
  73.2 55.3 all-gather.15
  131.6 55.3 all-gather.21
  189.0 21.0 all-gather.33
  212.0 21.6 all-gather.35
  235.8 21.7 all-gather.17
  259.7 21.7 all-gather.23
  284.5 56.0 all-gather.25
  343.5 66.1 all-gather.27
  412.4 66.2 all-gather.29
  481.5 66.2 all-gather.31
  549.3 21.0 all-gather.41
  596.1 21.7 all-gather.37
  619.3 21.7 all-gather.39
  643.2 145.9 reduce-scatter.12
  791.4 144.1 reduce-scatter.10
  937.8 142.3 reduce-scatter.16
  1082.5 143.7 reduce-scatter.14
  1228.9 140.1 reduce-scatter.24
  1372.0 139.3 reduce-scatter.18
  1514.2 139.3 reduce-scatter.20
  1656.5 139.5 reduce-scatter.22
  1798.8 157.2 reduce-scatter.26
  1959.0 158.2 reduce-scatter.28
  (1 shorter events, 20.9 us)
where the time goes:
time: 2140 us; the launch traced here: 2120 us
  waiting for transfers between devices  1700 us (79%)
  matrix products  148 us (7%)
  blocking collectives  112 us (5%)
  local copies, waits for them, and re-layouts  102 us (5%)
  other arithmetic  42.4 us (2%)
    reduce_scatter x2, waiting for transfers between devices, reduce_grads(): lax.psum_scatter(up_g[:, :half_cols], ('gx', 'gy'), scatter_dimension=0,...  240 us
    all_gather x3, waiting for transfers between devices, fetch_feed(): lax.all_gather(shortened(shards), ('gx', 'gy'), axis=0, tiled=True)  194 us
    all_gather x4, waiting for transfers between devices, fetch_attention(): lax.all_gather(shortened(shards), ('gx', 'gy'), axis=0, tiled=True)  162 us
    reduce_scatter x1, waiting for transfers between devices, reduce_grads(): lax.psum_scatter(down_g, ('gx', 'gy'), scatter_dimension=0, tiled=True)  161 us
    reduce_scatter x1, waiting for transfers between devices, reduce_grads(): lax.psum_scatter(gate_g, ('gx', 'gy'), scatter_dimension=0, tiled=True)  160 us
    reduce_scatter x2, waiting for transfers between devices, reduce_grads(): lax.psum_scatter(up_g[:, half_cols:], ('gx', 'gy'), scatter_dimension=0,...  145 us
    reduce_scatter x1, waiting for transfers between devices, reduce_grads(): lax.psum_scatter(value_g, ('gx', 'gy'), scatter_dimension=0, tiled=True)  142 us
    reduce_scatter x1, waiting for transfers between devices, reduce_grads(): lax.psum_scatter(key_g, ('gx', 'gy'), scatter_dimension=0, tiled=True)  142 us
  transfers between devices with their start and end apart: 25, of which 20 were waited for; matrix products, arithmetic and copies ran while one was open for 13% of the time, Pallas kernels for 0%

commit v1 on v0

v1 whole, which is shorter than its diff:
```python
import functools

import jax
import jax.numpy as jnp
from jax import lax
from jax.sharding import PartitionSpec as P

H = 16
EPS = 1e-05
NEG = -1e30
SCALE = 0.125
ALL = ("gx", "gy")
F32 = jnp.float32
BF16 = jnp.bfloat16


class Plan:
    def __init__(self, n_gx, n_gy):
        self.n_gx, self.n_gy = n_gx, n_gy
        self.T, self.R = n_gy // 2, n_gx
        self.square = self.T == self.R
        every = [(t, r, c) for t in range(self.T) for r in range(self.R) for c in range(2)]
        at = self.device
        self.t_swap = {k: [(at(t, r, c), at(t ^ k, r, c)) for t, r, c in every] for k in range(1, self.T)}
        self.r_swap = {k: [(at(t, r, c), at(t, r ^ k, c)) for t, r, c in every] for k in range(1, self.R)}
        self.c_swap = [(at(t, r, c), at(t, r, 1 - c)) for t, r, c in every]
        self.inward = []
        for flip in range(2):
            self.inward.append([(self.home(self.chunk(t, r), r, c ^ flip), at(t, r, c)) for t, r, c in every])

    def device(self, t, r, c):
        return t * self.n_gy + r * 2 + c if self.square else r * self.n_gy + t * 2 + c

    def home(self, z, g, c):
        return g * self.n_gy + z * 2 + c

    def chunk(self, t, r):
        return t ^ r if self.square else t


def pick(array, index):
    return lax.dynamic_index_in_dim(array, index, 0, keepdims=False)


def send(array, pairs):
    if all(a == b for a, b in pairs):
        return array
    return lax.ppermute(array, ALL, pairs)


def dot(a, b):
    return lax.dot_general(a, b, (((1,), (0,)), ((), ())), preferred_element_type=F32)


def dot_rows(a, b):
    return lax.dot_general(a, b, (((0,), (0,)), ((), ())), preferred_element_type=F32)


def dot_cols(a, b):
    return lax.dot_general(a, b, (((1,), (1,)), ((), ())), preferred_element_type=F32)


def rotate(values, cosine, sine):
    half = values.shape[-1] // 2
    a, b = values[..., :half], values[..., half:]
    return jnp.concatenate([a * cosine - b * sine, b * cosine + a * sine], axis=-1)


def local(plan, layer_in, first_layer_value, v1_acc, cotangent, seq_starts, norm1_gain, w_query, w_key, w_value,
          w_out, norm2_gain, w_gate, w_up, w_down):
    T, R = plan.T, plan.R
    micro, L, D = layer_in.shape
    FF = w_gate.shape[1]
    HT, FT, heads = D // T, FF // T, H // T
    HD = D // H
    N = T * 2 * L
    gx, gy = lax.axis_index("gx"), lax.axis_index("gy")
    c = gy % 2
    t, r = (gx, gy // 2) if plan.square else (gy // 2, gx)
    swap_t = lambda array, k: send(array, plan.t_swap[k]) if k else array
    swap_r = lambda array, k: send(array, plan.r_swap[k]) if k else array

    def inward(array):
        parts = [send(pick(array, c ^ flip), plan.inward[flip]) for flip in range(2)]
        return jnp.concatenate(parts, axis=0)

    def outward(array):
        parts = [send(array[flip * L:(flip + 1) * L], [(b, a) for a, b in plan.inward[flip]]) for flip in range(2)]
        swapped = jnp.where(c == 0, parts[0], parts[1]), jnp.where(c == 0, parts[1], parts[0])
        return jnp.stack(swapped)

    def gather_t(array):
        return [swap_t(array, k) for k in range(T)]

    def reduce_t(partial):
        own = partial[:2 * L]
        for k in range(1, T):
            own = own + swap_t(partial[k * 2 * L:(k + 1) * 2 * L].astype(BF16), k).astype(F32)
        return own

    def gather_cols(shards):
        rows = shards[0].shape[0]
        if not plan.square:
            return [lax.dynamic_slice_in_dim(lax.all_gather(s, ALL, axis=0, tiled=True), t * (s.shape[1] // T), s.shape[1] // T, 1)
                    for s in shards]
        pieces = jnp.concatenate([s.reshape(rows, T, -1) for s in shards], axis=2).transpose(1, 0, 2)
        width = pieces.shape[2]
        block = jnp.stack([swap_t(pick(pieces, t ^ k), k) for k in range(T)])
        blocks = jnp.stack([swap_r(block, j) for j in range(R)])
        both = (blocks, send(blocks, plan.c_swap))
        full = jnp.zeros((T, R, 2, rows, width), BF16)
        for i in range(2):
            for j in range(R):
                for k in range(T):
                    full = lax.dynamic_update_slice(full, both[i][j, k][None, None, None], (t ^ k, r ^ j, c ^ i, 0, 0))
        full = full.reshape(T * R * 2 * rows, width)
        out, at = [], 0
        for s in shards:
            w = s.shape[1] // T
            out.append(full[:, at:at + w])
            at += w
        return out

    def gather_rows(shard):
        rows = shard.shape[0]
        if not plan.square:
            full = lax.all_gather(shard, ALL, axis=0, tiled=True)
            return lax.dynamic_slice_in_dim(full, t * (full.shape[0] // T), full.shape[0] // T, 0)
        blocks = jnp.stack([swap_r(shard, j) for j in range(R)])
        both = (blocks, send(blocks, plan.c_swap))
        full = jnp.zeros((R, 2) + shard.shape, shard.dtype)
        for i in range(2):
            for j in range(R):
                full = lax.dynamic_update_slice(full, both[i][j][None, None], (r ^ j, c ^ i) + (0,) * shard.ndim)
        return full.reshape((R * 2 * rows,) + shard.shape[1:])

    def reduce_r(grad):
        axis = grad.ndim - 4
        take = lambda a, i, ax: lax.dynamic_index_in_dim(a, i, ax, keepdims=False)
        kept = take(grad, c, axis + 1).astype(F32)
        kept = kept + send(take(grad, 1 - c, axis + 1), plan.c_swap).astype(F32)
        low = kept.astype(grad.dtype)
        total = take(kept, r, axis)
        for j in range(1, R):
            total = total + swap_r(take(low, r ^ j, axis), j).astype(F32)
        return total

    def scatter_cols(grad, widths):
        if not plan.square:
            out, at = [], 0
            for w in widths:
                full = lax.dynamic_update_slice(jnp.zeros((D, w * T), F32), grad[:, at:at + w].astype(F32), (0, t * w))
                out.append(lax.psum_scatter(full, ALL, scatter_dimension=0, tiled=True))
                at += w
            return out
        rows = D // (T * R * 2)
        total = reduce_r(grad.astype(BF16).reshape(T, R, 2, rows, -1))
        low = total.astype(BF16)
        parts = [swap_t(pick(low, t ^ k), k).astype(F32) if k else pick(total, t) for k in range(T)]
        parts = jnp.stack(parts)
        order = [pick(parts, s ^ t) for s in range(T)]
        out, at = [], 0
        for w in widths:
            out.append(jnp.concatenate([p[:, at:at + w] for p in order], axis=1))
            at += w
        return out

    def scatter_rows(grad):
        if not plan.square:
            full = lax.dynamic_update_slice(jnp.zeros((grad.shape[0] * T, D), F32), grad, (t * grad.shape[0], 0))
            return lax.psum_scatter(full, ALL, scatter_dimension=0, tiled=True)
        return reduce_r(grad.astype(BF16).reshape(R, 2, -1, D))

    def scatter_gains(grads):
        if not plan.square:
            return lax.psum_scatter(grads, ALL, scatter_dimension=1, tiled=True)
        rows = D // (T * R * 2)
        total = reduce_r(grads.reshape(2, T, R, 2, rows, 1).transpose(1, 2, 3, 0, 4, 5).reshape(T, R, 2, 2 * rows, 1))
        own = pick(total, t)
        for k in range(1, T):
            own = own + swap_t(pick(total, t ^ k), k)
        return own.reshape(2, rows)

    def gather_gains(gains):
        if not plan.square:
            return lax.all_gather(gains, ALL, axis=0, tiled=True).T
        rows = gains.shape[0]
        part = gather_rows(gains)
        full = jnp.zeros((T,) + part.shape, part.dtype)
        for k in range(T):
            full = lax.dynamic_update_slice(full, swap_t(part, k)[None], (t ^ k, 0, 0))
        return full.reshape(D, 2).T

    x_own = inward(layer_in)
    query_w, key_w, value_w = gather_cols([w_query, w_key, w_value])
    gains = gather_gains(jnp.stack([norm1_gain, norm2_gain], axis=1)).astype(F32)
    gain_one, gain_two = gains[0], gains[1]
    x_all = jnp.concatenate(gather_t(x_own), axis=0)
    v_own = inward(first_layer_value)
    v_cols = v_own.reshape(2 * L, T, HT).transpose(1, 0, 2)
    v_all = jnp.concatenate([swap_t(pick(v_cols, t ^ k), k) for k in range(T)], axis=0)
    out_rows = gather_rows(w_out)
    gate_w, up_w = gather_cols([w_gate, w_up])
    down_w = gather_rows(w_down)
    out_parts = gather_t(out_rows)
    c_own = inward(cotangent)
    c_all = jnp.concatenate(gather_t(c_own), axis=0)

    starts = pick(seq_starts, c)
    blocks = plan.chunk(t ^ jnp.arange(T, dtype=jnp.int32), r) if plan.square else (t ^ jnp.arange(T, dtype=jnp.int32))
    position = (blocks[:, None] * 2 + (c ^ jnp.arange(2, dtype=jnp.int32))[None, :])[:, :, None] * L
    position = (position + jnp.arange(L, dtype=jnp.int32)).reshape(N) + r * N
    begin = jnp.max(jnp.where(starts[None, :] <= position[:, None], starts[None, :], 0), axis=1)
    rel = (position - begin).astype(F32)
    visible = (begin[:, None] == begin[None, :]) & (position[None, :] <= position[:, None])
    frequency = 10000.0 ** (-(jnp.arange(HD // 2, dtype=F32) * 2.0 / HD))
    angles = rel[:, None] * frequency[None, :]
    cosine, sine = jnp.cos(angles)[:, None, :], jnp.sin(angles)[:, None, :]

    x = x_all.astype(F32)
    rstd_one = lax.rsqrt(jnp.mean(x * x, axis=-1, keepdims=True) + EPS)
    normed_one = (x * rstd_one * gain_one).astype(BF16)
    query = rotate(dot(normed_one, query_w).reshape(N, heads, HD), cosine, sine).astype(BF16)
    key = rotate(dot(normed_one, key_w).reshape(N, heads, HD), cosine, sine).astype(BF16)
    value = (0.5 * dot(normed_one, value_w) + 0.5 * v_all.astype(F32)).astype(BF16).reshape(N, heads, HD)
    scores = jnp.einsum("ihd,jhd->hij", query, key, preferred_element_type=F32) * SCALE
    scores = jnp.where(visible[None], scores, NEG)
    top = jnp.max(scores, axis=-1, keepdims=True)
    probs = jnp.exp(scores - top)
    denom = jnp.sum(probs, axis=-1, keepdims=True)
    probs = probs / denom
    probs_low = probs.astype(BF16)
    attn = jnp.einsum("hij,jhd->ihd", probs_low, value, preferred_element_type=F32)
    attn_low = attn.reshape(N, HT).astype(BF16)
    after = x
    for k in range(T):
        part = swap_t(attn_low, k).reshape(T, 2 * L, HT)
        part = jnp.concatenate([part[b ^ k] for b in range(T)], axis=0)
        after = after + dot(part, out_parts[k])
    rstd_two = lax.rsqrt(jnp.mean(after * after, axis=-1, keepdims=True) + EPS)
    hat_two = after * rstd_two
    normed_two = (hat_two * gain_two).astype(BF16)
    gate = dot(normed_two, gate_w)
    up = dot(normed_two, up_w)
    sig = jax.nn.sigmoid(gate)
    act = gate * sig
    hidden = (act * up).astype(BF16)
    result = reduce_t(dot(hidden, down_w)) + after[:2 * L]
    layer_out = outward(result.astype(BF16))

    grad_down = dot_rows(hidden, c_all)
    grad_hidden = dot_cols(c_all, down_w)
    grad_gate = (grad_hidden * up * (sig * (1.0 + gate * (1.0 - sig)))).astype(BF16)
    grad_up = (grad_hidden * act).astype(BF16)
    grad_gu = dot_rows(normed_two, jnp.concatenate([grad_gate, grad_up], axis=1))
    grad_two_part = dot_cols(grad_gate, gate_w) + dot_cols(grad_up, up_w)
    gain_two_grad = jnp.sum(grad_two_part * hat_two, axis=0)
    grad_two = reduce_t(grad_two_part) * gain_two
    hat_own = hat_two[:2 * L]
    grad_after = c_own.astype(F32) + rstd_two[:2 * L] * (
        grad_two - hat_own * jnp.mean(grad_two * hat_own, axis=-1, keepdims=True))
    grad_branch = jnp.concatenate(gather_t(grad_after.astype(BF16)), axis=0)
    grad_out = dot_rows(attn_low, grad_branch)
    grad_attn = dot_cols(grad_branch, out_rows).astype(BF16).reshape(N, heads, HD)
    delta = jnp.sum(grad_attn.astype(F32) * attn, axis=-1).T
    grad_probs = jnp.einsum("ihd,jhd->hij", grad_attn, value, preferred_element_type=F32)
    grad_scores = (probs * (grad_probs - delta[..., None])).astype(BF16)
    grad_query = jnp.einsum("hij,jhd->ihd", grad_scores, key, preferred_element_type=F32) * SCALE
    grad_key = jnp.einsum("hij,ihd->jhd", grad_scores, query, preferred_element_type=F32) * SCALE
    grad_blend = jnp.einsum("hij,ihd->jhd", probs_low, grad_attn, preferred_element_type=F32).reshape(N, HT)
    grad_query = rotate(grad_query, cosine, -sine).reshape(N, HT).astype(BF16)
    grad_key = rotate(grad_key, cosine, -sine).reshape(N, HT).astype(BF16)
    grad_value = (0.5 * grad_blend).astype(BF16)
    grad_qkv = dot_rows(normed_one, jnp.concatenate([grad_query, grad_key, grad_value], axis=1))
    grad_one_part = dot_cols(grad_query, query_w) + dot_cols(grad_key, key_w) + dot_cols(grad_value, value_w)
    hat_one = x * rstd_one
    gain_one_grad = jnp.sum(grad_one_part * hat_one, axis=0)
    grad_one = reduce_t(grad_one_part) * gain_one
    hat_own = hat_one[:2 * L]
    input_grad = grad_after + rstd_one[:2 * L] * (
        grad_one - hat_own * jnp.mean(grad_one * hat_own, axis=-1, keepdims=True))
    input_grad = outward(input_grad.astype(BF16)).astype(F32)
    v_parts = jnp.stack([swap_t(grad_value[k * 2 * L:(k + 1) * 2 * L], k) for k in range(T)])
    v_rows = jnp.concatenate([pick(v_parts, s ^ t) for s in range(T)], axis=1)
    v1_out = v1_acc + outward(v_rows).astype(F32)

    gate_g, up_g = scatter_cols(grad_gu, [FT, FT])
    down_g = scatter_rows(grad_down)
    out_g = scatter_rows(grad_out)
    query_g, key_g, value_g = scatter_cols(grad_qkv, [HT, HT, HT])
    gain_g = scatter_gains(jnp.stack([gain_one_grad, gain_two_grad]))
    return (layer_out, input_grad, v1_out, gain_g[0], query_g, key_g, value_g, out_g, gain_g[1], gate_g, up_g, down_g)


def solution(mesh):
    plan = Plan(mesh.shape["gx"], mesh.shape["gy"])
    tokens, rows, vector = P(None, ALL, None), P(ALL, None), P(ALL)
    return jax.shard_map(
        functools.partial(local, plan),
        mesh=mesh,
        in_specs=(tokens, tokens, tokens, tokens, P(), vector, rows, rows, rows, rows, vector, rows, rows, rows),
        out_specs=(tokens, tokens, tokens, vector, rows, rows, rows, rows, vector, rows, rows, rows),
        check_vma=False,
    )
```

time: 2140 us -> 458 us (0.21)
  waiting for transfers between devices: 1700 us -> 101 us
  starting transfers between devices: 1.62 us -> 200 us
  blocking collectives: 112 us -> 0 us
  matrix products: 148 us -> 50.5 us
  local copies, waits for them, and re-layouts: 102 us -> 66.2 us
    reduce_scatter x10 -> x0, waiting for transfers between devices: 1270 us -> none  [the longest x2 240 us: reduce_grads(): lax.psum_scatter(up_g[:, :half_cols], ('gx', 'gy'), scatter_dimension=0,...]
    all_gather x15 -> x0, waiting for transfers between devices: 420 us -> none  [the longest x3 194 us: fetch_feed(): lax.all_gather(shortened(shards), ('gx', 'gy'), axis=0, tiled=True)]
    ppermute x0 -> x100, starting transfers between devices: none -> 200 us  [send(): return lax.ppermute(array, ALL, pairs)]
    dot_general x56 -> x26, matrix products: 148 us -> 45.7 us  [the longest x10 17.6 us: dot(): lax.dot_general(a, b, (((1,), (0,)), ((), ())), preferred_element_type=F32)]
    ppermute x0 -> x100, waiting for transfers between devices: none -> 101 us  [send(): return lax.ppermute(array, ALL, pairs)]
    unnamed x2 -> x0, blocking collectives: 81 us -> none
    dynamic_update_slice x0 -> x92, local copies, waits for them, and re-layouts: none -> 34 us  [the longest x64 21.1 us: gather_cols(): lax.dynamic_update_slice(full, both[i][j, k][None, None, None], (t ^ k, r...]
    all_gather x2 -> x0, blocking collectives: 30.7 us -> none  [attention_keys(): lax.all_gather(row_stats, 'gy', axis=0, tiled=True)]
  transfers between devices with their start and end apart: 25 -> 100, of which waited for: 20 -> 35; matrix products, arithmetic and copies ran while one was open for 13% -> 26% of each run, Pallas kernels for 0% -> 0%
where the time goes in v1:
time: 458 us; the launch traced here: 451 us
  starting transfers between devices  200 us (44%)
  waiting for transfers between devices  101 us (22%)
  local copies, waits for them, and re-layouts  66.2 us (14%)
  matrix products  50.5 us (11%)
  other arithmetic  30.4 us (7%)
    ppermute x100, starting transfers between devices, send(): return lax.ppermute(array, ALL, pairs)  200 us
    ppermute x100, waiting for transfers between devices, send(): return lax.ppermute(array, ALL, pairs)  101 us
    dynamic_update_slice x64, local copies, waits for them, and re-layouts, gather_cols(): lax.dynamic_update_slice(full, both[i][j, k][None, None, None], (t ^ k, r...  21.1 us
    dot_general x10, matrix products, dot(): lax.dot_general(a, b, (((1,), (0,)), ((), ())), preferred_element_type=F32)  17.6 us
    dot_general x7, matrix products, dot_cols(): lax.dot_general(a, b, (((1,), (1,)), ((), ())), preferred_element_type=F32)  14.5 us
    dynamic_update_slice x24, local copies, waits for them, and re-layouts, gather_rows(): lax.dynamic_update_slice(full, both[i][j][None, None], (r ^ j, c ^ i) + (...  12.7 us
    dot_general x4, matrix products, dot_rows(): lax.dot_general(a, b, (((0,), (0,)), ((), ())), preferred_element_type=F32)  9.66 us
  transfers between devices with their start and end apart: 100, of which 35 were waited for; matrix products, arithmetic and copies ran while one was open for 26% of the time, Pallas kernels for 0%

profile of v1, /device:TPU:0, one launch (start us, length us, event | category | flops | bytes accessed | tf_op | source)
XLA Modules:
  0.0 451.5 jit_solution(8122439756727857165)
XLA Ops:
  7.6 3.9 collective-permute-start.7
  64.9 43.7 %collective-permute-start.15 = (bf16[4,32,768]{2,1,0:T(8,128)(2,1)}, bf16[4,32,768]{2,1,0:T(8,128)(2,1)S(1)}, u32[]{:S(2)}, u32[]{:S(2)}) collective-permute-start(bf16[4,32,768]{2,1,0:T(8,128)(2,1)} %get-tuple-element.125), channel_id=1, source_target_pairs={{0,2},{1,3},{2,0},{3,1},{4,6},{5,7},{6,4},{7,5},{8,10},{9,11},{10,... | collective-permute-start | bytes 589832 | tf_op jit(solution)/shard_map/ppermute | solution.py:48
  108.8 5.1 %collective-permute-start.17 = (bf16[4,32,768]{2,1,0:T(8,128)(2,1)}, bf16[4,32,768]{2,1,0:T(8,128)(2,1)S(1)}, u32[]{:S(2)}, u32[]{:S(2)}) collective-permute-start(bf16[4,32,768]{2,1,0:T(8,128)(2,1)} %get-tuple-element.125), channel_id=1, source_target_pairs={{0,6},{1,7},{2,4},{3,5},{4,2},{5,3},{6,0},{7,1},{8,14},{9,15},{10,... | collective-permute-start | bytes 589832 | tf_op jit(solution)/shard_map/ppermute | solution.py:48
  119.8 6.4 %collective-permute-done.16 = bf16[4,32,768]{2,1,0:T(8,128)(2,1)S(1)} collective-permute-done((bf16[4,32,768]{2,1,0:T(8,128)(2,1)}, bf16[4,32,768]{2,1,0:T(8,128)(2,1)S(1)}, u32[]{:S(2)}, u32[]{:S(2)}) %collective-permute-start.16) | collective-permute-done | bytes 196640 | tf_op jit(solution)/shard_map/ppermute | solution.py:48
  142.5 4.0 collective-permute-done.52
  147.2 3.6 collective-permute-done.53
  172.8 4.8 %fusion.221 = (f32[4,512]{1,0:T(4,128)S(1)}, f32[4,512,512]{1,2,0:T(8,128)}) fusion(pred[512,512]{0,1:T(8,128)(4,1)} %compare_and_fusion, bf16[512,4,32]{0,2,1:T(8,128)(2,1)S(1)} %get-tuple-element.145, bf16[512,4,32]{0,2,1:T(8,128)(2,1)S(1)} %get-tuple-element.146, bf16[512,4,32]{0,2,1:T(8,128)(2,1)S(1)} %get-tuple-element.63, ...), kind=kOutput, calls=%fused_computation.498 | convolution fusion | flops 139461120 | bytes 4988928 | tf_op jit(solution)/shard_map/sub | solution.py:229
  186.3 10.2 %collective-permute-done.30 = bf16[512,256]{0,1:T(8,128)(2,1)S(1)} collective-permute-done((bf16[512,256]{0,1:T(8,128)(2,1)S(1)}, bf16[512,256]{0,1:T(8,128)(2,1)S(1)}, u32[]{:S(2)}, u32[]{:S(2)}) %collective-permute-start.30) | collective-permute-done | bytes 262176 | tf_op jit(solution)/shard_map/ppermute | solution.py:48
  200.6 6.0 %collective-permute-done.32 = bf16[512,256]{0,1:T(8,128)(2,1)S(1)} collective-permute-done((bf16[512,256]{0,1:T(8,128)(2,1)S(1)}, bf16[512,256]{0,1:T(8,128)(2,1)S(1)}, u32[]{:S(2)}, u32[]{:S(2)}) %collective-permute-start.32) | collective-permute-done | bytes 262176 | tf_op jit(solution)/shard_map/ppermute | solution.py:48
  206.6 4.2 collective-permute-done.28
  233.4 3.7 fusion.223
  249.5 4.4 multiply_reduce_fusion
  272.3 6.5 %collective-permute-start.60 = (bf16[128,1024]{1,0:T(8,128)(2,1)S(1)}, bf16[128,1024]{1,0:T(8,128)(2,1)S(1)}, u32[]{:S(2)}, u32[]{:S(2)}) collective-permute-start(bf16[128,1024]{1,0:T(8,128)(2,1)S(1)} %get-tuple-element.24), channel_id=1, source_target_pairs={{0,24},{1,25},{2,26},{3,27},{4,28},{5,29},{6,30},{7,31},{8,16},{9,... | collective-permute-start | bytes 786440 | tf_op jit(solution)/shard_map/ppermute | solution.py:48
  278.8 7.1 %collective-permute-start.59 = (bf16[128,1024]{1,0:T(8,128)(2,1)S(1)}, bf16[128,1024]{1,0:T(8,128)(2,1)S(1)}, u32[]{:S(2)}, u32[]{:S(2)}) collective-permute-start(bf16[128,1024]{1,0:T(8,128)(2,1)S(1)} %get-tuple-element.24), channel_id=1, source_target_pairs={{0,16},{1,17},{2,18},{3,19},{4,20},{5,21},{6,22},{7,23},{8,24},{9,... | collective-permute-start | bytes 786440 | tf_op jit(solution)/shard_map/ppermute | solution.py:48
  286.7 7.0 %collective-permute-done.59 = bf16[128,1024]{1,0:T(8,128)(2,1)S(1)} collective-permute-done((bf16[128,1024]{1,0:T(8,128)(2,1)S(1)}, bf16[128,1024]{1,0:T(8,128)(2,1)S(1)}, u32[]{:S(2)}, u32[]{:S(2)}) %collective-permute-start.59) | collective-permute-done | bytes 262176 | tf_op jit(solution)/shard_map/ppermute | solution.py:48
  318.8 4.8 %collective-permute-start.77 = (f32[64,1]{0,1:T(1,128)S(1)}, f32[64,1]{0,1:T(1,128)S(1)}, u32[]{:S(2)}, u32[]{:S(2)}) collective-permute-start(f32[64,1]{0,1:T(1,128)S(1)} %get-tuple-element.174), channel_id=1, source_target_pairs={{0,24},{1,25},{2,26},{3,27},{4,28},{5,29},{6,30},{7,31},{8,16},{9,... | collective-permute-start | bytes 776 | tf_op jit(solution)/shard_map/ppermute | solution.py:48
  343.7 3.6 collective-permute-start.88
  353.5 4.8 %collective-permute-done.87 = bf16[32,1024]{1,0:T(8,128)(2,1)S(1)} collective-permute-done((bf16[32,1024]{1,0:T(8,128)(2,1)S(1)}, bf16[32,1024]{1,0:T(8,128)(2,1)S(1)}, u32[]{:S(2)}, u32[]{:S(2)}) %collective-permute-start.87) | collective-permute-done | bytes 65568 | tf_op jit(solution)/shard_map/ppermute | solution.py:48
  359.6 7.6 %collective-permute-done.98 = bf16[88,1024]{1,0:T(8,128)(2,1)S(1)} collective-permute-done((bf16[88,1024]{1,0:T(8,128)(2,1)S(1)}, bf16[88,1024]{1,0:T(8,128)(2,1)S(1)}, u32[]{:S(2)}, u32[]{:S(2)}) %collective-permute-start.98) | collective-permute-done | bytes 180256 | tf_op jit(solution)/shard_map/ppermute | solution.py:48
  371.6 21.5 %collective-permute-start.81 = (bf16[4,32,768]{2,1,0:T(8,128)(2,1)S(1)}, bf16[4,32,768]{2,1,0:T(8,128)(2,1)S(1)}, u32[]{:S(2)}, u32[]{:S(2)}) collective-permute-start(bf16[4,32,768]{2,1,0:T(8,128)(2,1)S(1)} %get-tuple-element.49), channel_id=1, source_target_pairs={{0,6},{1,7},{2,4},{3,5},{4,2},{5,3},{6,0},{7,1},{8,14},{9,15},{10,... | collective-permute-start | bytes 589832 | tf_op jit(solution)/shard_map/ppermute | solution.py:48
  395.7 3.8 collective-permute-start.92
  400.2 9.5 %collective-permute-done.80 = bf16[4,32,768]{2,1,0:T(8,128)(2,1)S(1)} collective-permute-done((bf16[4,32,768]{2,1,0:T(8,128)(2,1)S(1)}, bf16[4,32,768]{2,1,0:T(8,128)(2,1)S(1)}, u32[]{:S(2)}, u32[]{:S(2)}) %collective-permute-start.80) | collective-permute-done | bytes 196640 | tf_op jit(solution)/shard_map/ppermute | solution.py:48
  409.8 20.4 %collective-permute-start.84 = (bf16[32,768]{1,0:T(8,128)(2,1)S(1)}, bf16[32,768]{1,0:T(8,128)(2,1)S(1)}, u32[]{:S(2)}, u32[]{:S(2)}) collective-permute-start(bf16[32,768]{1,0:T(8,128)(2,1)S(1)} %get-tuple-element.123), channel_id=1, source_target_pairs={{0,24},{1,25},{2,26},{3,27},{4,28},{5,29},{6,30},{7,31},{8,16},{9,... | collective-permute-start | bytes 147464 | tf_op jit(solution)/shard_map/ppermute | solution.py:48
  438.9 5.4 %collective-permute-start.95 = (bf16[32,1408]{1,0:T(8,128)(2,1)S(1)}, bf16[32,1408]{1,0:T(8,128)(2,1)S(1)}, u32[]{:S(2)}, u32[]{:S(2)}) collective-permute-start(bf16[32,1408]{1,0:T(8,128)(2,1)S(1)} %get-tuple-element.75), channel_id=1, source_target_pairs={{0,24},{1,25},{2,26},{3,27},{4,28},{5,29},{6,30},{7,31},{8,16},{9,... | collective-permute-start | bytes 270344 | tf_op jit(solution)/shard_map/ppermute | solution.py:48
  (602 shorter events, 246.2 us)
Async XLA Ops:
  0.7 41.9 %collective-permute-start.24 = (bf16[32,1024]{1,0:T(8,128)(2,1)}, bf16[32,1024]{1,0:T(8,128)(2,1)S(1)}, u32[]{:S(2)}, u32[]{:S(2)}) collective-permute-start(bf16[32,1024]{1,0:T(8,128)(2,1)} %param.23), channel_id=1, source_target_pairs={{0,2},{1,3},{2,0},{3,1},{4,6},{5,7},{6,4},{7,5},{8,10},{9,11},{10,... | collective-permute-start | bytes 196616 | tf_op jit(solution)/shard_map/ppermute | solution.py:48
  3.8 42.0 %collective-permute-start.25 = (bf16[32,1024]{1,0:T(8,128)(2,1)}, bf16[32,1024]{1,0:T(8,128)(2,1)S(1)}, u32[]{:S(2)}, u32[]{:S(2)}) collective-permute-start(bf16[32,1024]{1,0:T(8,128)(2,1)} %param.23), channel_id=1, source_target_pairs={{0,4},{1,5},{2,6},{3,7},{4,0},{5,1},{6,2},{7,3},{8,12},{9,13},{10,... | collective-permute-start | bytes 196616 | tf_op jit(solution)/shard_map/ppermute | solution.py:48
  38.7 70.1 %collective-permute-start.41 = (bf16[88,1024]{1,0:T(8,128)(2,1)S(1)}, bf16[88,1024]{1,0:T(8,128)(2,1)S(1)}, u32[]{:S(2)}, u32[]{:S(2)}) collective-permute-start(bf16[88,1024]{1,0:T(8,128)(2,1)S(1)} %copy-done.16), channel_id=1, source_target_pairs={{0,2},{1,3},{2,0},{3,1},{4,6},{5,7},{6,4},{7,5},{8,10},{9,11},{10,... | collective-permute-start | bytes 540680 | tf_op jit(solution)/shard_map/ppermute | solution.py:48
  39.9 74.0 %collective-permute-start.42 = (bf16[88,1024]{1,0:T(8,128)(2,1)S(1)}, bf16[88,1024]{1,0:T(8,128)(2,1)}, u32[]{:S(2)}, u32[]{:S(2)}) collective-permute-start(bf16[88,1024]{1,0:T(8,128)(2,1)S(1)} %copy-done.16), channel_id=1, source_target_pairs={{0,4},{1,5},{2,6},{3,7},{4,0},{5,1},{6,2},{7,3},{8,12},{9,13},{10,... | collective-permute-start | bytes 540680 | tf_op jit(solution)/shard_map/ppermute | solution.py:48
  49.1 64.9 %collective-permute-start.43 = (bf16[88,1024]{1,0:T(8,128)(2,1)S(1)}, bf16[88,1024]{1,0:T(8,128)(2,1)}, u32[]{:S(2)}, u32[]{:S(2)}) collective-permute-start(bf16[88,1024]{1,0:T(8,128)(2,1)S(1)} %copy-done.16), channel_id=1, source_target_pairs={{0,6},{1,7},{2,4},{3,5},{4,2},{5,3},{6,0},{7,1},{8,14},{9,15},{10,... | collective-permute-start | bytes 540680 | tf_op jit(solution)/shard_map/ppermute | solution.py:48
  63.2 45.4 %collective-permute-start.51 = (bf16[64,1024]{1,0:T(8,128)(2,1)}, bf16[64,1024]{1,0:T(8,128)(2,1)S(1)}, u32[]{:S(2)}, u32[]{:S(2)}) collective-permute-start(bf16[64,1024]{1,0:T(8,128)(2,1)} %get-tuple-element.98), channel_id=1, source_target_pairs={{1,0},{0,1},{11,2},{10,3},{21,4},{20,5},{31,6},{30,7},{3,8},{2,9},... | collective-permute-start | bytes 393224 | tf_op jit(solution)/shard_map/ppermute | solution.py:48
  64.9 54.1 %collective-permute-start.15 = (bf16[4,32,768]{2,1,0:T(8,128)(2,1)}, bf16[4,32,768]{2,1,0:T(8,128)(2,1)S(1)}, u32[]{:S(2)}, u32[]{:S(2)}) collective-permute-start(bf16[4,32,768]{2,1,0:T(8,128)(2,1)} %get-tuple-element.125), channel_id=1, source_target_pairs={{0,2},{1,3},{2,0},{3,1},{4,6},{5,7},{6,4},{7,5},{8,10},{9,11},{10,... | collective-permute-start | bytes 589832 | tf_op jit(solution)/shard_map/ppermute | solution.py:48
  113.9 40.9 %collective-permute-start.37 = (bf16[4,32,1408]{2,1,0:T(8,128)(2,1)}, bf16[4,32,1408]{2,1,0:T(8,128)(2,1)S(1)}, u32[]{:S(2)}, u32[]{:S(2)}) collective-permute-start(bf16[4,32,1408]{2,1,0:T(8,128)(2,1)} %get-tuple-element.77), channel_id=1, source_target_pairs={{0,2},{1,3},{2,0},{3,1},{4,6},{5,7},{6,4},{7,5},{8,10},{9,11},{10,... | collective-permute-start | bytes 1081352 | tf_op jit(solution)/shard_map/ppermute | solution.py:48
  119.0 38.5 %collective-permute-start.38 = (bf16[4,32,1408]{2,1,0:T(8,128)(2,1)S(1)}, bf16[4,32,1408]{2,1,0:T(8,128)(2,1)S(1)}, u32[]{:S(2)}, u32[]{:S(2)}) collective-permute-start(bf16[4,32,1408]{2,1,0:T(8,128)(2,1)S(1)} %copy-done.32), channel_id=1, source_target_pairs={{0,4},{1,5},{2,6},{3,7},{4,0},{5,1},{6,2},{7,3},{8,12},{9,13},{10,... | collective-permute-start | bytes 1081352 | tf_op jit(solution)/shard_map/ppermute | solution.py:48
  150.8 29.7 %collective-permute-start.23 = (bf16[128,256]{0,1:T(8,128)(2,1)}, bf16[128,256]{0,1:T(8,128)(2,1)}, u32[]{:S(2)}, u32[]{:S(2)}) collective-permute-start(bf16[128,256]{0,1:T(8,128)(2,1)} %get-tuple-element.117), channel_id=1, source_target_pairs={{0,24},{1,25},{2,26},{3,27},{4,28},{5,29},{6,30},{7,31},{8,16},{9,... | collective-permute-start | bytes 196616 | tf_op jit(solution)/shard_map/ppermute | solution.py:48
  153.1 27.7 %collective-permute-start.22 = (bf16[128,256]{0,1:T(8,128)(2,1)}, bf16[128,256]{0,1:T(8,128)(2,1)}, u32[]{:S(2)}, u32[]{:S(2)}) collective-permute-start(bf16[128,256]{0,1:T(8,128)(2,1)} %get-tuple-element.118), channel_id=1, source_target_pairs={{0,16},{1,17},{2,18},{3,19},{4,20},{5,21},{6,22},{7,23},{8,24},{9,... | collective-permute-start | bytes 196616 | tf_op jit(solution)/shard_map/ppermute | solution.py:48
  154.8 25.9 %collective-permute-start.21 = (bf16[128,256]{0,1:T(8,128)(2,1)}, bf16[128,256]{0,1:T(8,128)(2,1)}, u32[]{:S(2)}, u32[]{:S(2)}) collective-permute-start(bf16[128,256]{0,1:T(8,128)(2,1)} %get-tuple-element.119), channel_id=1, source_target_pairs={{0,8},{1,9},{2,10},{3,11},{4,12},{5,13},{6,14},{7,15},{8,0},{9,1},... | collective-permute-start | bytes 196616 | tf_op jit(solution)/shard_map/ppermute | solution.py:48
  164.7 46.7 %collective-permute-start.33 = (bf16[256,1024]{1,0:T(8,128)(2,1)}, bf16[256,1024]{1,0:T(8,128)(2,1)}, u32[]{:S(2)}, u32[]{:S(2)}) collective-permute-start(bf16[256,1024]{1,0:T(8,128)(2,1)} %bitcast.85), channel_id=1, source_target_pairs={{0,24},{1,25},{2,26},{3,27},{4,28},{5,29},{6,30},{7,31},{8,16},{9,... | collective-permute-start | bytes 1572872 | tf_op jit(solution)/shard_map/ppermute | solution.py:48
  169.1 29.1 %collective-permute-start.31 = (bf16[256,1024]{1,0:T(8,128)(2,1)}, bf16[256,1024]{1,0:T(8,128)(2,1)}, u32[]{:S(2)}, u32[]{:S(2)}) collective-permute-start(bf16[256,1024]{1,0:T(8,128)(2,1)} %bitcast.85), channel_id=1, source_target_pairs={{0,16},{1,17},{2,18},{3,19},{4,20},{5,21},{6,22},{7,23},{8,24},{9,... | collective-permute-start | bytes 1572872 | tf_op jit(solution)/shard_map/ppermute | solution.py:48
  180.5 30.3 %collective-permute-start.29 = (bf16[256,1024]{1,0:T(8,128)(2,1)}, bf16[256,1024]{1,0:T(8,128)(2,1)S(1)}, u32[]{:S(2)}, u32[]{:S(2)}) collective-permute-start(bf16[256,1024]{1,0:T(8,128)(2,1)} %bitcast.85), channel_id=1, source_target_pairs={{0,8},{1,9},{2,10},{3,11},{4,12},{5,13},{6,14},{7,15},{8,0},{9,1},... | collective-permute-start | bytes 1572872 | tf_op jit(solution)/shard_map/ppermute | solution.py:48
  180.7 33.8 %collective-permute-start.40 = (bf16[4,4,32,1408]{3,2,1,0:T(8,128)(2,1)S(1)}, bf16[4,4,32,1408]{3,2,1,0:T(8,128)(2,1)S(1)}, u32[]{:S(2)}, u32[]{:S(2)}) collective-permute-start(bf16[4,4,32,1408]{3,2,1,0:T(8,128)(2,1)S(1)} %copy-done.14), channel_id=1, source_target_pairs={{0,1},{1,0},{2,3},{3,2},{4,5},{5,4},{6,7},{7,6},{8,9},{9,8},{10,11... | collective-permute-start | bytes 4325384 | tf_op jit(solution)/shard_map/ppermute | solution.py:48
  240.0 22.4 %collective-permute-start.47 = (bf16[128,1024]{1,0:T(8,128)(2,1)}, bf16[128,1024]{1,0:T(8,128)(2,1)}, u32[]{:S(2)}, u32[]{:S(2)}) collective-permute-start(bf16[128,1024]{1,0:T(8,128)(2,1)} %get-tuple-element.46), channel_id=1, source_target_pairs={{0,24},{1,25},{2,26},{3,27},{4,28},{5,29},{6,30},{7,31},{8,16},{9,... | collective-permute-start | bytes 786440 | tf_op jit(solution)/shard_map/ppermute | solution.py:48
  263.3 130.5 %collective-permute-start.89 = (bf16[4,4,32,1408]{3,2,1,0:T(8,128)(2,1)}, bf16[4,4,32,1408]{3,2,1,0:T(8,128)(2,1)}, u32[]{:S(2)}, u32[]{:S(2)}) collective-permute-start(bf16[4,4,32,1408]{3,2,1,0:T(8,128)(2,1)} %dynamic-slice_bitcast_fusion), channel_id=1, source_target_pairs={{0,1},{1,0},{2,3},{3,2},{4,5},{5,4},{6,7},{7,6},{8,9},{9,8},{10,11... | collective-permute-start | bytes 4325384 | tf_op jit(solution)/shard_map/ppermute | solution.py:48
  263.3 73.5 %collective-permute-start.96 = (bf16[4,88,1024]{2,1,0:T(8,128)(2,1)}, bf16[4,88,1024]{2,1,0:T(8,128)(2,1)}, u32[]{:S(2)}, u32[]{:S(2)}) collective-permute-start(bf16[4,88,1024]{2,1,0:T(8,128)(2,1)} %dynamic-slice_bitcast_fusion.2), channel_id=1, source_target_pairs={{0,1},{1,0},{2,3},{3,2},{4,5},{5,4},{6,7},{7,6},{8,9},{9,8},{10,11... | collective-permute-start | bytes 2162696 | tf_op jit(solution)/shard_map/ppermute | solution.py:48
  371.6 28.0 %collective-permute-start.81 = (bf16[4,32,768]{2,1,0:T(8,128)(2,1)S(1)}, bf16[4,32,768]{2,1,0:T(8,128)(2,1)S(1)}, u32[]{:S(2)}, u32[]{:S(2)}) collective-permute-start(bf16[4,32,768]{2,1,0:T(8,128)(2,1)S(1)} %get-tuple-element.49), channel_id=1, source_target_pairs={{0,6},{1,7},{2,4},{3,5},{4,2},{5,3},{6,0},{7,1},{8,14},{9,15},{10,... | collective-permute-start | bytes 589832 | tf_op jit(solution)/shard_map/ppermute | solution.py:48
  395.7 42.9 %collective-permute-start.92 = (bf16[4,32,1408]{2,1,0:T(8,128)(2,1)S(1)}, bf16[4,32,1408]{2,1,0:T(8,128)(2,1)S(1)}, u32[]{:S(2)}, u32[]{:S(2)}) collective-permute-start(bf16[4,32,1408]{2,1,0:T(8,128)(2,1)S(1)} %get-tuple-element.36), channel_id=1, source_target_pairs={{0,6},{1,7},{2,4},{3,5},{4,2},{5,3},{6,0},{7,1},{8,14},{9,15},{10,... | collective-permute-start | bytes 1081352 | tf_op jit(solution)/shard_map/ppermute | solution.py:48
  399.6 39.1 %collective-permute-start.91 = (bf16[4,32,1408]{2,1,0:T(8,128)(2,1)S(1)}, bf16[4,32,1408]{2,1,0:T(8,128)(2,1)S(1)}, u32[]{:S(2)}, u32[]{:S(2)}) collective-permute-start(bf16[4,32,1408]{2,1,0:T(8,128)(2,1)S(1)} %get-tuple-element.37), channel_id=1, source_target_pairs={{0,4},{1,5},{2,6},{3,7},{4,0},{5,1},{6,2},{7,3},{8,12},{9,13},{10,... | collective-permute-start | bytes 1081352 | tf_op jit(solution)/shard_map/ppermute | solution.py:48
  399.6 39.1 %collective-permute-start.90 = (bf16[4,32,1408]{2,1,0:T(8,128)(2,1)S(1)}, bf16[4,32,1408]{2,1,0:T(8,128)(2,1)S(1)}, u32[]{:S(2)}, u32[]{:S(2)}) collective-permute-start(bf16[4,32,1408]{2,1,0:T(8,128)(2,1)S(1)} %get-tuple-element.35), channel_id=1, source_target_pairs={{0,2},{1,3},{2,0},{3,1},{4,6},{5,7},{6,4},{7,5},{8,10},{9,11},{10,... | collective-permute-start | bytes 1081352 | tf_op jit(solution)/shard_map/ppermute | solution.py:48
  409.8 22.6 %collective-permute-start.84 = (bf16[32,768]{1,0:T(8,128)(2,1)S(1)}, bf16[32,768]{1,0:T(8,128)(2,1)S(1)}, u32[]{:S(2)}, u32[]{:S(2)}) collective-permute-start(bf16[32,768]{1,0:T(8,128)(2,1)S(1)} %get-tuple-element.123), channel_id=1, source_target_pairs={{0,24},{1,25},{2,26},{3,27},{4,28},{5,29},{6,30},{7,31},{8,16},{9,... | collective-permute-start | bytes 147464 | tf_op jit(solution)/shard_map/ppermute | solution.py:48
  (146 other events, 1690.4 us)

commit v2 on v1

v2 whole, which is shorter than its diff:
```python
import functools

import jax
import jax.numpy as jnp
from jax import lax
from jax.sharding import PartitionSpec as P

H = 16
EPS = 1e-05
NEG = -1e30
SCALE = 0.125
ALL = ("gx", "gy")
F32 = jnp.float32
BF16 = jnp.bfloat16


class Plan:
    def __init__(self, n_gx, n_gy):
        self.G, self.T = n_gx, n_gy // 2
        every = [(g, h, t) for g in range(self.G) for h in range(2) for t in range(self.T)]
        at = lambda g, h, t: g * n_gy + h * self.T + t
        self.g_swap = {k: [(at(g, h, t), at(g ^ k, h, t)) for g, h, t in every] for k in range(1, self.G)}
        self.t_swap = {k: [(at(g, h, t), at(g, h, t ^ k)) for g, h, t in every] for k in range(1, self.T)}
        self.h_swap = [(at(g, h, t), at(g, 1 - h, t)) for g, h, t in every]
        self.bits = []
        bit = self.T // 2
        while bit:
            self.bits.append(bit)
            bit //= 2


def pick(array, index, axis=0):
    return lax.dynamic_index_in_dim(array, index, axis, keepdims=False)


def send(array, pairs):
    return lax.ppermute(array, ALL, pairs)


def dot(a, b):
    return lax.dot_general(a, b, (((1,), (0,)), ((), ())), preferred_element_type=F32)


def dot_rows(a, b):
    return lax.dot_general(a, b, (((0,), (0,)), ((), ())), preferred_element_type=F32)


def dot_cols(a, b):
    return lax.dot_general(a, b, (((1,), (1,)), ((), ())), preferred_element_type=F32)


def rotate(values, cosine, sine):
    half = values.shape[-1] // 2
    a, b = values[..., :half], values[..., half:]
    return jnp.concatenate([a * cosine - b * sine, b * cosine + a * sine], axis=-1)


def local(plan, layer_in, first_layer_value, v1_acc, cotangent, seq_starts, norm1_gain, w_query, w_key, w_value,
          w_out, norm2_gain, w_gate, w_up, w_down):
    G, T, bits = plan.G, plan.T, plan.bits
    micro, L, D = layer_in.shape
    FF = w_gate.shape[1]
    HT, FT, heads = D // T, FF // T, H // T
    HD = D // H
    M = 2 * L
    N = T * M
    rows, frows = w_query.shape[0], w_down.shape[0]
    g, gy = lax.axis_index("gx"), lax.axis_index("gy")
    h, t = gy // T, gy % T

    def to_t(array, bit):
        return send(array, plan.t_swap[bit])

    def to_g(array, k):
        return send(array, plan.g_swap[k]) if k else array

    def to_h(array):
        return send(array, plan.h_swap)

    def inward(array):
        return jnp.concatenate([pick(array, h), to_h(pick(array, 1 - h))], axis=0)

    def outward(array):
        own, other = array[:L], to_h(array[L:])
        return jnp.stack([jnp.where(h == 0, own, other), jnp.where(h == 0, other, own)])

    def gather_t(array):
        parts = {0: array}
        for bit in bits:
            order = sorted(parts)
            moved = to_t(jnp.concatenate([parts[j] for j in order], axis=0), bit)
            size = array.shape[0]
            for i, j in enumerate(order):
                parts[j ^ bit] = moved[i * size:(i + 1) * size]
        return [parts[j] for j in range(T)]

    def reduce_t(partial):
        blocks = partial.reshape((T, -1) + partial.shape[1:])
        for bit in reversed(bits):
            order = [j for j in range(blocks.shape[0])]
            shape = blocks.shape
            split = blocks.reshape((-1, 2, 1) + shape[1:]) if False else blocks
            split = blocks.reshape((shape[0] // 2, 2) + shape[1:])
            blocks = split[:, 0] + to_t(split[:, 1].astype(BF16), bit).astype(F32)
        return blocks[0]

    def exchange_t(parts):
        held = {j: [parts[j]] for j in range(T)}
        sources = [0]
        for bit in bits:
            out = [j for j in sorted(held) if j & bit]
            flat = [p for j in out for p in held[j]]
            moved = to_t(jnp.stack(flat), bit)
            n = len(sources)
            new = {}
            for i, j in enumerate(out):
                new[j ^ bit] = held[j ^ bit] + [moved[i * n + s] for s in range(n)]
            sources = sources + [s ^ bit for s in sources]
            held = new
        result = [None] * T
        for s, p in zip(sources, held[0]):
            result[s] = p
        return result

    def natural(parts):
        array = jnp.stack(parts)
        for bit in bits:
            split = array.reshape((-1, 2, bit) + array.shape[1:])
            array = jnp.where((t & bit) != 0, split[:, ::-1], split).reshape(array.shape)
        return array

    def gather_r(block):
        other = to_h(block)
        pair = jnp.where(h == 0, jnp.stack([block, other]), jnp.stack([other, block]))
        full = jnp.zeros((G,) + pair.shape, pair.dtype)
        for k in range(G):
            full = lax.dynamic_update_slice(full, to_g(pair, k)[None], (g ^ k,) + (0,) * pair.ndim)
        return full.reshape((G * 2 * block.shape[0],) + block.shape[1:])

    def gather_cols(slices):
        block = natural(exchange_t([pick(slices, t ^ j) for j in range(T)]))
        return gather_r(block.reshape(T * block.shape[1], -1))

    def reduce_r(grad):
        n, w = grad.shape[0] // (2 * G), grad.shape[1]
        grad = grad.astype(BF16).reshape(G, 2 * n, w)
        total = pick(grad, g).astype(F32)
        for k in range(1, G):
            total = total + to_g(pick(grad, g ^ k), k).astype(F32)
        total = total.reshape(2, n, w)
        return pick(total, h) + to_h(pick(total, 1 - h).astype(BF16)).astype(F32)

    def scatter_cols(grad):
        total = reduce_r(grad).reshape(T, rows, -1)
        low = total.astype(BF16)
        return natural(exchange_t([pick(low, t ^ j) for j in range(T)])).astype(F32)

    pad = jnp.zeros((rows, 126), BF16)
    gains_in = jnp.concatenate([norm1_gain[:, None], norm2_gain[:, None], pad], axis=1)

    def col_slices(w):
        return w.reshape(rows, T, HT).transpose(1, 0, 2)

    def hidden_slices(w):
        return w.reshape(rows, 2 * G, T, frows).transpose(2, 0, 1, 3).reshape(T, rows, FT)

    qkv_slices = jnp.concatenate([col_slices(w_query), col_slices(w_key), col_slices(w_value),
                                  jnp.broadcast_to(gains_in[None], (T, rows, 128))], axis=2)
    x_own = inward(layer_in)
    qkv_w = gather_cols(qkv_slices)
    x_all = jnp.concatenate(gather_t(x_own), axis=0)
    v_own = inward(first_layer_value).reshape(M, T, HT).transpose(1, 0, 2)
    v_all = jnp.concatenate(exchange_t([pick(v_own, t ^ j) for j in range(T)]), axis=0)
    gu_w = gather_cols(jnp.concatenate([hidden_slices(w_gate), hidden_slices(w_up)], axis=2))
    down_w = gather_r(w_down)
    c_own = inward(cotangent)
    c_all = jnp.concatenate(gather_t(c_own), axis=0)
    out_w = natural(gather_t(gather_r(w_out))).reshape(T, 2 * G, rows, D).transpose(1, 0, 2, 3).reshape(D, D)
    out_w = out_w.reshape(T, HT, D)

    gains = qkv_w[:, 3 * HT:3 * HT + 2].astype(F32).T
    gain_one, gain_two = gains[0], gains[1]
    query_w, key_w, value_w = qkv_w[:, :HT], qkv_w[:, HT:2 * HT], qkv_w[:, 2 * HT:3 * HT]
    gate_w, up_w = gu_w[:, :FT], gu_w[:, FT:]

    starts = pick(seq_starts, h)
    member = t ^ jnp.arange(T, dtype=jnp.int32)
    half = h ^ jnp.arange(2, dtype=jnp.int32)
    position = ((half[None, :] * T + member[:, None]) * L)[:, :, None] + jnp.arange(L, dtype=jnp.int32)
    position = position.reshape(N) + g * N
    begin = jnp.max(jnp.where(starts[None, :] <= position[:, None], starts[None, :], 0), axis=1)
    rel = (position - begin).astype(F32)
    visible = (begin[:, None] == begin[None, :]) & (position[None, :] <= position[:, None])
    frequency = 10000.0 ** (-(jnp.arange(HD // 2, dtype=F32) * 2.0 / HD))
    angles = rel[:, None] * frequency[None, :]
    cosine, sine = jnp.cos(angles)[:, None, :], jnp.sin(angles)[:, None, :]

    x = x_all.astype(F32)
    rstd_one = lax.rsqrt(jnp.mean(x * x, axis=-1, keepdims=True) + EPS)
    normed_one = (x * rstd_one * gain_one).astype(BF16)
    query = rotate(dot(normed_one, query_w).reshape(N, heads, HD), cosine, sine).astype(BF16)
    key = rotate(dot(normed_one, key_w).reshape(N, heads, HD), cosine, sine).astype(BF16)
    value = (0.5 * dot(normed_one, value_w) + 0.5 * v_all.astype(F32)).astype(BF16).reshape(N, heads, HD)
    scores = jnp.einsum("ihd,jhd->hij", query, key, preferred_element_type=F32) * SCALE
    scores = jnp.where(visible[None], scores, NEG)
    top = jnp.max(scores, axis=-1, keepdims=True)
    probs = jnp.exp(scores - top)
    denom = jnp.sum(probs, axis=-1, keepdims=True)
    probs = probs / denom
    probs_low = probs.astype(BF16)
    attn = jnp.einsum("hij,jhd->ihd", probs_low, value, preferred_element_type=F32)
    attn_low = attn.reshape(N, HT).astype(BF16)
    attn_parts = []
    for j, part in enumerate(gather_t(attn_low)):
        part = part.reshape(T, M, HT)
        attn_parts.append(jnp.concatenate([part[b ^ j] for b in range(T)], axis=0))
    after = x
    for j in range(T):
        after = after + dot(attn_parts[j], pick(out_w, t ^ j))
    rstd_two = lax.rsqrt(jnp.mean(after * after, axis=-1, keepdims=True) + EPS)
    hat_two = after * rstd_two
    normed_two = (hat_two * gain_two).astype(BF16)
    gate = dot(normed_two, gate_w)
    up = dot(normed_two, up_w)
    sig = jax.nn.sigmoid(gate)
    act = gate * sig
    hidden = (act * up).astype(BF16)

    grad_hidden = dot_cols(c_all, down_w)
    grad_gate = (grad_hidden * up * (sig * (1.0 + gate * (1.0 - sig)))).astype(BF16)
    grad_up = (grad_hidden * act).astype(BF16)
    grad_two_part = dot_cols(grad_gate, gate_w) + dot_cols(grad_up, up_w)
    gain_two_grad = jnp.sum(grad_two_part * hat_two, axis=0)
    grad_two = reduce_t(grad_two_part) * gain_two
    hat_own = hat_two[:M]
    grad_after = c_own.astype(F32) + rstd_two[:M] * (
        grad_two - hat_own * jnp.mean(grad_two * hat_own, axis=-1, keepdims=True))
    grad_branch = jnp.concatenate(gather_t(grad_after.astype(BF16)), axis=0)
    result = reduce_t(dot(hidden, down_w)) + after[:M]
    layer_out = outward(result.astype(BF16))
    grad_down = dot_rows(hidden, c_all)
    grad_gu = dot_rows(normed_two, jnp.concatenate([grad_gate, grad_up], axis=1))

    grad_attn = dot_cols(grad_branch, pick(out_w, t)).astype(BF16).reshape(N, heads, HD)
    delta = jnp.sum(grad_attn.astype(F32) * attn, axis=-1).T
    grad_probs = jnp.einsum("ihd,jhd->hij", grad_attn, value, preferred_element_type=F32)
    grad_scores = (probs * (grad_probs - delta[..., None])).astype(BF16)
    grad_query = jnp.einsum("hij,jhd->ihd", grad_scores, key, preferred_element_type=F32) * SCALE
    grad_key = jnp.einsum("hij,ihd->jhd", grad_scores, query, preferred_element_type=F32) * SCALE
    grad_blend = jnp.einsum("hij,ihd->jhd", probs_low, grad_attn, preferred_element_type=F32).reshape(N, HT)
    grad_query = rotate(grad_query, cosine, -sine).reshape(N, HT).astype(BF16)
    grad_key = rotate(grad_key, cosine, -sine).reshape(N, HT).astype(BF16)
    grad_value = (0.5 * grad_blend).astype(BF16)
    grad_one_part = dot_cols(grad_query, query_w) + dot_cols(grad_key, key_w) + dot_cols(grad_value, value_w)
    hat_one = x * rstd_one
    gain_one_grad = jnp.sum(grad_one_part * hat_one, axis=0)
    grad_one = reduce_t(grad_one_part) * gain_one
    hat_own = hat_one[:M]
    input_grad = grad_after + rstd_one[:M] * (
        grad_one - hat_own * jnp.mean(grad_one * hat_own, axis=-1, keepdims=True))
    input_grad = outward(input_grad.astype(BF16)).astype(F32)
    v_parts = natural(exchange_t([grad_value[j * M:(j + 1) * M] for j in range(T)]))
    v1_out = v1_acc + outward(v_parts.transpose(1, 0, 2).reshape(M, D)).astype(F32)

    attn_full = natural([p.T for p in attn_parts]).reshape(2 * G, T, rows, N)
    grad_out = dot(pick(attn_full, t, 1).reshape(2 * G * rows, N), grad_branch)
    grad_gains = jnp.stack([gain_one_grad, gain_two_grad], axis=1)
    grad_gains = jnp.concatenate([grad_gains, jnp.zeros((D, 126), F32)], axis=1)
    grad_qkv = dot_rows(normed_one, jnp.concatenate([grad_query, grad_key, grad_value], axis=1))
    down_g = reduce_r(grad_down)
    gu_g = scatter_cols(grad_gu)
    out_g = reduce_r(grad_out)
    qkv_g = scatter_cols(jnp.concatenate([grad_qkv, grad_gains], axis=1))

    def col_join(parts):
        return parts.transpose(1, 0, 2).reshape(rows, D)

    def hidden_join(parts):
        return parts.reshape(T, rows, 2 * G, frows).transpose(1, 2, 0, 3).reshape(rows, FF)

    gain_g = jnp.sum(qkv_g[:, :, 3 * HT:3 * HT + 2], axis=0)
    return (layer_out, input_grad, v1_out, gain_g[:, 0], col_join(qkv_g[:, :, :HT]), col_join(qkv_g[:, :, HT:2 * HT]),
            col_join(qkv_g[:, :, 2 * HT:3 * HT]), out_g, gain_g[:, 1], hidden_join(gu_g[:, :, :FT]),
            hidden_join(gu_g[:, :, FT:]), down_g)


def solution(mesh):
    plan = Plan(mesh.shape["gx"], mesh.shape["gy"])
    tokens, rows, vector = P(None, ALL, None), P(ALL, None), P(ALL)
    return jax.shard_map(
        functools.partial(local, plan),
        mesh=mesh,
        in_specs=(tokens, tokens, tokens, tokens, P(), vector, rows, rows, rows, rows, vector, rows, rows, rows),
        out_specs=(tokens, tokens, tokens, vector, rows, rows, rows, rows, vector, rows, rows, rows),
        check_vma=False,
    )
```

time: 458 us -> 369 us (0.81)
  starting transfers between devices: 200 us -> 66.7 us
  local copies, waits for them, and re-layouts: 66.2 us -> 87.3 us
  other arithmetic: 30.4 us -> 46.2 us
  waiting for transfers between devices: 101 us -> 113 us
  matrix products: 50.5 us -> 45.9 us
    ppermute x100 -> x66, starting transfers between devices: 200 us -> 66.7 us  [send(): return lax.ppermute(array, ALL, pairs)]
    dynamic_update_slice x92 -> x13, local copies, waits for them, and re-layouts: 34 us -> 12.6 us  [gather_r(): lax.dynamic_update_slice(full, to_g(pair, k)[None], (g ^ k,) + (0,) * pai...]
    reshape x8 -> x19, local copies, waits for them, and re-layouts: 3.49 us -> 17.5 us  [the longest x4 7.65 us: hidden_join(): parts.reshape(T, rows, 2 * G, frows).transpose(1, 2, 0, 3).reshape(rows, FF)]
    ppermute x100 -> x66, waiting for transfers between devices: 101 us -> 113 us  [send(): return lax.ppermute(array, ALL, pairs)]
    select_n x0 -> x12, other arithmetic: none -> 6.28 us  [the longest x5 4.12 us: gather_r(): jnp.where(h == 0, jnp.stack([block, other]), jnp.stack([other, block]))]
    broadcast_in_dim x9 -> x11, local copies, waits for them, and re-layouts: 4.33 us -> 10 us  [the longest x3 5.6 us: gather_r(): to_g(pair, k)[None]]
    add x7 -> x8, other arithmetic: 2.47 us -> 8.04 us  [the longest x4 5.68 us: reduce_r(): total = total + to_g(pick(grad, g ^ k), k).astype(F32)]
    transpose x1 -> x3, local copies, waits for them, and re-layouts: 0.03 us -> 4.76 us  [the longest x2 4.49 us: hidden_join(): parts.reshape(T, rows, 2 * G, frows).transpose(1, 2, 0, 3).reshape(rows, FF)]
  transfers between devices with their start and end apart: 100 -> 66, of which waited for: 35 -> 26; matrix products, arithmetic and copies ran while one was open for 26% -> 39% of each run, Pallas kernels for 0% -> 0%
where the time goes in v2:
time: 369 us; the launch traced here: 362 us
  waiting for transfers between devices  113 us (31%)
  local copies, waits for them, and re-layouts  87.3 us (24%)
  starting transfers between devices  66.7 us (18%)
  other arithmetic  46.2 us (13%)
  matrix products  45.9 us (12%)
    ppermute x66, waiting for transfers between devices, send(): return lax.ppermute(array, ALL, pairs)  113 us
    ppermute x66, starting transfers between devices, send(): return lax.ppermute(array, ALL, pairs)  66.7 us
    dot_general x11, matrix products, dot(): lax.dot_general(a, b, (((1,), (0,)), ((), ())), preferred_element_type=F32)  18.1 us
    dynamic_update_slice x13, local copies, waits for them, and re-layouts, gather_r(): lax.dynamic_update_slice(full, to_g(pair, k)[None], (g ^ k,) + (0,) * pai...  12.6 us
    dot_general x7, matrix products, dot_cols(): lax.dot_general(a, b, (((1,), (1,)), ((), ())), preferred_element_type=F32)  11.4 us
    unnamed x172, local copies, waits for them, and re-layouts  9.04 us
    squeeze x7, local copies, waits for them, and re-layouts, pick(): return lax.dynamic_index_in_dim(array, index, axis, keepdims=False)  8.33 us
    dot_general x3, matrix products, dot_rows(): lax.dot_general(a, b, (((0,), (0,)), ((), ())), preferred_element_type=F32)  7.92 us
  transfers between devices with their start and end apart: 66, of which 26 were waited for; matrix products, arithmetic and copies ran while one was open for 39% of the time, Pallas kernels for 0%

profile of v2, /device:TPU:0, one launch (start us, length us, event | category | flops | bytes accessed | tf_op | source)
XLA Modules:
  0.0 361.5 jit_solution(14018470855446726279)
XLA Ops:
  0.7 4.1 %collective-permute-start.12 = (bf16[32,1024]{1,0:T(8,128)(2,1)}, bf16[32,1024]{1,0:T(8,128)(2,1)S(1)}, u32[]{:S(2)}, u32[]{:S(2)}) collective-permute-start(bf16[32,1024]{1,0:T(8,128)(2,1)} %param.23), channel_id=1, source_target_pairs={{0,4},{1,5},{2,6},{3,7},{4,0},{5,1},{6,2},{7,3},{8,12},{9,13},{10,... | collective-permute-start | bytes 196616 | tf_op jit(solution)/shard_map/ppermute | solution.py:37
  26.9 2.9 collective-permute-start.9
  32.0 9.2 %collective-permute-done.9 = bf16[64,1024]{1,0:T(8,128)(2,1)S(1)} collective-permute-done((bf16[64,1024]{1,0:T(8,128)(2,1)S(1)}, bf16[64,1024]{1,0:T(8,128)(2,1)S(1)}, u32[]{:S(2)}, u32[]{:S(2)}) %collective-permute-start.9) | collective-permute-done | bytes 131104 | tf_op jit(solution)/shard_map/ppermute | solution.py:37
  62.2 4.3 %collective-permute-done.34 = bf16[128,1024]{1,0:T(8,128)(2,1)S(1)} collective-permute-done((bf16[128,1024]{1,0:T(8,128)(2,1)S(1)}, bf16[128,1024]{1,0:T(8,128)(2,1)S(1)}, u32[]{:S(2)}, u32[]{:S(2)}) %collective-permute-start.34) | collective-permute-done | bytes 262176 | tf_op jit(solution)/shard_map/ppermute | solution.py:37
  68.9 10.6 %collective-permute-done.5 = bf16[128,896]{1,0:T(8,128)(2,1)S(1)} collective-permute-done((bf16[128,896]{1,0:T(8,128)(2,1)S(1)}, bf16[128,896]{1,0:T(8,128)(2,1)S(1)}, u32[]{:S(2)}, u32[]{:S(2)}) %collective-permute-start.5) | collective-permute-done | bytes 229408 | tf_op jit(solution)/shard_map/ppermute | solution.py:37
  92.6 6.2 %collective-permute-done.22 = bf16[128,1408]{1,0:T(8,128)(2,1)} collective-permute-done((bf16[128,1408]{1,0:T(8,128)(2,1)}, bf16[128,1408]{1,0:T(8,128)(2,1)}, u32[]{:S(2)}, u32[]{:S(2)}) %collective-permute-start.22) | collective-permute-done | bytes 360480 | tf_op jit(solution)/shard_map/ppermute | solution.py:37
  130.1 4.3 %fusion.155 = (f32[4,512]{1,0:T(4,128)}, f32[4,512,512]{1,2,0:T(8,128)}) fusion(pred[512,512]{0,1:T(8,128)(4,1)S(1)} %copy-done.60, bf16[512,4,32]{0,2,1:T(8,128)(2,1)S(1)} %get-tuple-element.114, bf16[512,4,32]{0,2,1:T(8,128)(2,1)S(1)} %get-tuple-element.115, bf16[512,4,32]{0,2,1:T(8,128)(2,1)S(1)} %get-tuple-element.45, ...), kind=kOutput, calls=%fused_computation.385 | convolution fusion | flops 139461120 | bytes 4988928 | tf_op jit(solution)/shard_map/sub | solution.py:207
  144.1 4.9 %collective-permute-done.18 = bf16[512,256]{0,1:T(8,128)(2,1)S(1)} collective-permute-done((bf16[512,256]{0,1:T(8,128)(2,1)S(1)}, bf16[512,256]{0,1:T(8,128)(2,1)S(1)}, u32[]{:S(2)}, u32[]{:S(2)}) %collective-permute-start.18) | collective-permute-done | bytes 262176 | tf_op jit(solution)/shard_map/ppermute | solution.py:37
  165.1 3.4 fusion.19
  168.4 4.6 %multiply_convert_fusion.4 = (bf16[512,704]{0,1:T(8,128)(2,1)}, bf16[512,704]{0,1:T(8,128)(2,1)}, bf16[512,704]{0,1:T(8,128)(2,1)S(1)}) fusion(f32[512,704]{0,1:T(8,128)S(1)} %fusion.157, f32[512,704]{0,1:T(8,128)S(1)} %fusion.19, bf16[512,1024]{1,0:T(8,128)(2,1)S(1)} %get-tuple-element.18, bf16[1024,1408]{1,0:T(8,128)(2,1)} %bitcast.67), kind=kOutput, calls=%fused_computation.41 | convolution fusion | flops 743604224 | bytes 7667712 | tf_op jit(solution)/shard_map/dot_general | solution.py:41
  188.6 3.1 fusion.17
  191.8 3.5 convolution_convert_fusion
  212.5 6.5 %collective-permute-done.65 = bf16[88,1024]{1,0:T(8,128)(2,1)S(1)} collective-permute-done((bf16[88,1024]{1,0:T(8,128)(2,1)S(1)}, bf16[88,1024]{1,0:T(8,128)(2,1)S(1)}, u32[]{:S(2)}, u32[]{:S(2)}) %collective-permute-start.65) | collective-permute-done | bytes 180256 | tf_op jit(solution)/shard_map/ppermute | solution.py:37
  221.8 14.6 %collective-permute-done.58 = bf16[256,1408]{1,0:T(8,128)(2,1)S(1)} collective-permute-done((bf16[256,1408]{1,0:T(8,128)(2,1)S(1)}, bf16[256,1408]{1,0:T(8,128)(2,1)S(1)}, u32[]{:S(2)}, u32[]{:S(2)}) %collective-permute-start.58) | collective-permute-done | bytes 720928 | tf_op jit(solution)/shard_map/ppermute | solution.py:37
  239.7 2.9 collective-permute-start.59
  246.2 14.9 %collective-permute-done.59 = bf16[128,1408]{1,0:T(8,128)(2,1)S(1)} collective-permute-done((bf16[128,1408]{1,0:T(8,128)(2,1)S(1)}, bf16[128,1408]{1,0:T(8,128)(2,1)S(1)}, u32[]{:S(2)}, u32[]{:S(2)}) %collective-permute-start.59) | collective-permute-done | bytes 360480 | tf_op jit(solution)/shard_map/ppermute | solution.py:37
  263.4 3.8 %collective-permute-done.60 = bf16[2,32,1408]{2,1,0:T(8,128)(2,1)S(1)} collective-permute-done((bf16[2,32,1408]{2,1,0:T(8,128)(2,1)S(1)}, bf16[2,32,1408]{2,1,0:T(8,128)(2,1)S(1)}, u32[]{:S(2)}, u32[]{:S(2)}) %collective-permute-start.60) | collective-permute-done | bytes 180256 | tf_op jit(solution)/shard_map/ppermute | solution.py:37
  291.5 3.1 collective-permute-start.54
  305.3 2.9 collective-permute-start.48
  309.7 3.3 collective-permute-start.55
  322.3 7.0 %collective-permute-done.48 = bf16[256,896]{1,0:T(8,128)(2,1)} collective-permute-done((bf16[256,896]{1,0:T(8,128)(2,1)}, bf16[256,896]{1,0:T(8,128)(2,1)}, u32[]{:S(2)}, u32[]{:S(2)}) %collective-permute-start.48) | collective-permute-done | bytes 458784 | tf_op jit(solution)/shard_map/ppermute | solution.py:37
  332.0 3.3 collective-permute-start.49
  336.6 8.5 %collective-permute-done.49 = bf16[128,896]{1,0:T(8,128)(2,1)S(1)} collective-permute-done((bf16[128,896]{1,0:T(8,128)(2,1)S(1)}, bf16[128,896]{1,0:T(8,128)(2,1)S(1)}, u32[]{:S(2)}, u32[]{:S(2)}) %collective-permute-start.49) | collective-permute-done | bytes 229408 | tf_op jit(solution)/shard_map/ppermute | solution.py:37
  354.6 5.0 %collective-permute-done.42 = bf16[64,1024]{1,0:T(8,128)(2,1)S(1)} collective-permute-done((bf16[64,1024]{1,0:T(8,128)(2,1)S(1)}, bf16[64,1024]{1,0:T(8,128)(2,1)S(1)}, u32[]{:S(2)}, u32[]{:S(2)}) %collective-permute-start.42) | collective-permute-done | bytes 131104 | tf_op jit(solution)/shard_map/ppermute | solution.py:37
  (519 shorter events, 221.8 us)
Async XLA Ops:
  0.7 25.8 %collective-permute-start.12 = (bf16[32,1024]{1,0:T(8,128)(2,1)}, bf16[32,1024]{1,0:T(8,128)(2,1)S(1)}, u32[]{:S(2)}, u32[]{:S(2)}) collective-permute-start(bf16[32,1024]{1,0:T(8,128)(2,1)} %param.23), channel_id=1, source_target_pairs={{0,4},{1,5},{2,6},{3,7},{4,0},{5,1},{6,2},{7,3},{8,12},{9,13},{10,... | collective-permute-start | bytes 196616 | tf_op jit(solution)/shard_map/ppermute | solution.py:37
  13.5 33.2 %collective-permute-start.33 = (bf16[64,1024]{1,0:T(8,128)(2,1)}, bf16[64,1024]{1,0:T(8,128)(2,1)S(1)}, u32[]{:S(2)}, u32[]{:S(2)}) collective-permute-start(bf16[64,1024]{1,0:T(8,128)(2,1)} %dynamic-slice_bitcast_fusion.12), channel_id=1, source_target_pairs={{0,4},{1,5},{2,6},{3,7},{4,0},{5,1},{6,2},{7,3},{8,12},{9,13},{10,... | collective-permute-start | bytes 393224 | tf_op jit(solution)/shard_map/ppermute | solution.py:37
  15.4 29.9 %collective-permute-start = (bf16[64,1024]{1,0:T(8,128)(2,1)}, bf16[64,1024]{1,0:T(8,128)(2,1)S(1)}, u32[]{:S(2)}, u32[]{:S(2)}) collective-permute-start(bf16[64,1024]{1,0:T(8,128)(2,1)} %dynamic-slice_bitcast_fusion.15), channel_id=1, source_target_pairs={{0,4},{1,5},{2,6},{3,7},{4,0},{5,1},{6,2},{7,3},{8,12},{9,13},{10,... | collective-permute-start | bytes 393224 | tf_op jit(solution)/shard_map/ppermute | solution.py:37
  18.0 31.1 %collective-permute-start.26 = (bf16[88,1024]{1,0:T(8,128)(2,1)S(1)}, bf16[88,1024]{1,0:T(8,128)(2,1)S(1)}, u32[]{:S(2)}, u32[]{:S(2)}) collective-permute-start(bf16[88,1024]{1,0:T(8,128)(2,1)S(1)} %copy-done.38), channel_id=1, source_target_pairs={{0,4},{1,5},{2,6},{3,7},{4,0},{5,1},{6,2},{7,3},{8,12},{9,13},{10,... | collective-permute-start | bytes 540680 | tf_op jit(solution)/shard_map/ppermute | solution.py:37
  53.9 32.4 %collective-permute-start.29 = (bf16[2,88,1024]{2,1,0:T(8,128)(2,1)}, bf16[2,88,1024]{2,1,0:T(8,128)(2,1)}, u32[]{:S(2)}, u32[]{:S(2)}) collective-permute-start(bf16[2,88,1024]{2,1,0:T(8,128)(2,1)} %maximum_select_fusion.5), channel_id=1, source_target_pairs={{0,24},{1,25},{2,26},{3,27},{4,28},{5,29},{6,30},{7,31},{8,16},{9,... | collective-permute-start | bytes 1081352 | tf_op jit(solution)/shard_map/ppermute | solution.py:37
  56.4 28.4 %collective-permute-start.28 = (bf16[2,88,1024]{2,1,0:T(8,128)(2,1)}, bf16[2,88,1024]{2,1,0:T(8,128)(2,1)}, u32[]{:S(2)}, u32[]{:S(2)}) collective-permute-start(bf16[2,88,1024]{2,1,0:T(8,128)(2,1)} %maximum_select_fusion.5), channel_id=1, source_target_pairs={{0,16},{1,17},{2,18},{3,19},{4,20},{5,21},{6,22},{7,23},{8,24},{9,... | collective-permute-start | bytes 1081352 | tf_op jit(solution)/shard_map/ppermute | solution.py:37
  58.7 25.0 %collective-permute-start.27 = (bf16[2,88,1024]{2,1,0:T(8,128)(2,1)}, bf16[2,88,1024]{2,1,0:T(8,128)(2,1)}, u32[]{:S(2)}, u32[]{:S(2)}) collective-permute-start(bf16[2,88,1024]{2,1,0:T(8,128)(2,1)} %maximum_select_fusion.5), channel_id=1, source_target_pairs={{0,8},{1,9},{2,10},{3,11},{4,12},{5,13},{6,14},{7,15},{8,0},{9,1},... | collective-permute-start | bytes 1081352 | tf_op jit(solution)/shard_map/ppermute | solution.py:37
  67.4 22.5 %collective-permute-start.16 = (bf16[256,1024]{1,0:T(8,128)(2,1)S(1)}, bf16[256,1024]{1,0:T(8,128)(2,1)}, u32[]{:S(2)}, u32[]{:S(2)}) collective-permute-start(bf16[256,1024]{1,0:T(8,128)(2,1)S(1)} %bitcast.435), channel_id=1, source_target_pairs={{0,2},{1,3},{2,0},{3,1},{4,6},{5,7},{6,4},{7,5},{8,10},{9,11},{10,... | collective-permute-start | bytes 1572872 | tf_op jit(solution)/shard_map/ppermute | solution.py:37
  83.7 34.5 %collective-permute-start.2 = (bf16[256,1024]{1,0:T(8,128)(2,1)}, bf16[256,1024]{1,0:T(8,128)(2,1)}, u32[]{:S(2)}, u32[]{:S(2)}) collective-permute-start(bf16[256,1024]{1,0:T(8,128)(2,1)} %pad_maximum_fusion.4), channel_id=1, source_target_pairs={{0,1},{1,0},{2,3},{3,2},{4,5},{5,4},{6,7},{7,6},{8,9},{9,8},{10,11... | collective-permute-start | bytes 1572872 | tf_op jit(solution)/shard_map/ppermute | solution.py:37
  84.8 55.5 %collective-permute-start.35 = (bf16[256,1024]{1,0:T(8,128)(2,1)}, bf16[256,1024]{1,0:T(8,128)(2,1)}, u32[]{:S(2)}, u32[]{:S(2)}) collective-permute-start(bf16[256,1024]{1,0:T(8,128)(2,1)} %pad_maximum_fusion.6), channel_id=1, source_target_pairs={{0,1},{1,0},{2,3},{3,2},{4,5},{5,4},{6,7},{7,6},{8,9},{9,8},{10,11... | collective-permute-start | bytes 1572872 | tf_op jit(solution)/shard_map/ppermute | solution.py:37
  106.8 46.4 %collective-permute-start.25 = (bf16[2,128,1408]{2,1,0:T(8,128)(2,1)}, bf16[2,128,1408]{2,1,0:T(8,128)(2,1)}, u32[]{:S(2)}, u32[]{:S(2)}) collective-permute-start(bf16[2,128,1408]{2,1,0:T(8,128)(2,1)} %maximum_select_fusion.1), channel_id=1, source_target_pairs={{0,24},{1,25},{2,26},{3,27},{4,28},{5,29},{6,30},{7,31},{8,16},{9,... | collective-permute-start | bytes 2162696 | tf_op jit(solution)/shard_map/ppermute | solution.py:37
  110.1 41.1 %collective-permute-start.24 = (bf16[2,128,1408]{2,1,0:T(8,128)(2,1)}, bf16[2,128,1408]{2,1,0:T(8,128)(2,1)}, u32[]{:S(2)}, u32[]{:S(2)}) collective-permute-start(bf16[2,128,1408]{2,1,0:T(8,128)(2,1)} %maximum_select_fusion.1), channel_id=1, source_target_pairs={{0,16},{1,17},{2,18},{3,19},{4,20},{5,21},{6,22},{7,23},{8,24},{9,... | collective-permute-start | bytes 2162696 | tf_op jit(solution)/shard_map/ppermute | solution.py:37
  113.8 35.3 %collective-permute-start.23 = (bf16[2,128,1408]{2,1,0:T(8,128)(2,1)}, bf16[2,128,1408]{2,1,0:T(8,128)(2,1)}, u32[]{:S(2)}, u32[]{:S(2)}) collective-permute-start(bf16[2,128,1408]{2,1,0:T(8,128)(2,1)} %maximum_select_fusion.1), channel_id=1, source_target_pairs={{0,8},{1,9},{2,10},{3,11},{4,12},{5,13},{6,14},{7,15},{8,0},{9,1},... | collective-permute-start | bytes 2162696 | tf_op jit(solution)/shard_map/ppermute | solution.py:37
  118.1 38.6 %collective-permute-start.17 = (bf16[512,1024]{1,0:T(8,128)(2,1)}, bf16[512,1024]{1,0:T(8,128)(2,1)}, u32[]{:S(2)}, u32[]{:S(2)}) collective-permute-start(bf16[512,1024]{1,0:T(8,128)(2,1)} %pad_maximum_fusion.1), channel_id=1, source_target_pairs={{0,1},{1,0},{2,3},{3,2},{4,5},{5,4},{6,7},{7,6},{8,9},{9,8},{10,11... | collective-permute-start | bytes 3145736 | tf_op jit(solution)/shard_map/ppermute | solution.py:37
  183.7 24.4 %collective-permute-start.30 = (bf16[2,128,1024]{2,1,0:T(8,128)(2,1)}, bf16[2,128,1024]{2,1,0:T(8,128)(2,1)}, u32[]{:S(2)}, u32[]{:S(2)}) collective-permute-start(bf16[2,128,1024]{2,1,0:T(8,128)(2,1)} %fusion.47), channel_id=1, source_target_pairs={{0,1},{1,0},{2,3},{3,2},{4,5},{5,4},{6,7},{7,6},{8,9},{9,8},{10,11... | collective-permute-start | bytes 1572872 | tf_op jit(solution)/shard_map/ppermute | solution.py:37
  203.1 33.4 %collective-permute-start.58 = (bf16[256,1408]{1,0:T(8,128)(2,1)S(1)}, bf16[256,1408]{1,0:T(8,128)(2,1)S(1)}, u32[]{:S(2)}, u32[]{:S(2)}) collective-permute-start(bf16[256,1408]{1,0:T(8,128)(2,1)S(1)} %get-tuple-element.23), channel_id=1, source_target_pairs={{0,24},{1,25},{2,26},{3,27},{4,28},{5,29},{6,30},{7,31},{8,16},{9,... | collective-permute-start | bytes 2162696 | tf_op jit(solution)/shard_map/ppermute | solution.py:37
  204.8 33.3 %collective-permute-start.57 = (bf16[256,1408]{1,0:T(8,128)(2,1)S(1)}, bf16[256,1408]{1,0:T(8,128)(2,1)S(1)}, u32[]{:S(2)}, u32[]{:S(2)}) collective-permute-start(bf16[256,1408]{1,0:T(8,128)(2,1)S(1)} %get-tuple-element.24), channel_id=1, source_target_pairs={{0,16},{1,17},{2,18},{3,19},{4,20},{5,21},{6,22},{7,23},{8,24},{9,... | collective-permute-start | bytes 2162696 | tf_op jit(solution)/shard_map/ppermute | solution.py:37
  211.9 30.6 %collective-permute-start.31 = (bf16[1,128,1024]{2,1,0:T(8,128)(2,1)S(1)}, bf16[1,128,1024]{2,1,0:T(8,128)(2,1)S(1)}, u32[]{:S(2)}, u32[]{:S(2)}) collective-permute-start(bf16[1,128,1024]{2,1,0:T(8,128)(2,1)S(1)} %fusion.96), channel_id=1, source_target_pairs={{0,2},{1,3},{2,0},{3,1},{4,6},{5,7},{6,4},{7,5},{8,10},{9,11},{10,... | collective-permute-start | bytes 786440 | tf_op jit(solution)/shard_map/ppermute | solution.py:37
  219.0 25.0 %collective-permute-start.37 = (bf16[1,128,1024]{2,1,0:T(8,128)(2,1)S(1)}, bf16[1,128,1024]{2,1,0:T(8,128)(2,1)S(1)}, u32[]{:S(2)}, u32[]{:S(2)}) collective-permute-start(bf16[1,128,1024]{2,1,0:T(8,128)(2,1)S(1)} %fusion.97), channel_id=1, source_target_pairs={{0,2},{1,3},{2,0},{3,1},{4,6},{5,7},{6,4},{7,5},{8,10},{9,11},{10,... | collective-permute-start | bytes 786440 | tf_op jit(solution)/shard_map/ppermute | solution.py:37
  245.2 22.8 %collective-permute-start.38 = (bf16[128,1024]{1,0:T(8,128)(2,1)S(1)}, bf16[128,1024]{1,0:T(8,128)(2,1)S(1)}, u32[]{:S(2)}, u32[]{:S(2)}) collective-permute-start(bf16[128,1024]{1,0:T(8,128)(2,1)S(1)} %get-tuple-element.14), channel_id=1, source_target_pairs={{0,2},{1,3},{2,0},{3,1},{4,6},{5,7},{6,4},{7,5},{8,10},{9,11},{10,... | collective-permute-start | bytes 786440 | tf_op jit(solution)/shard_map/ppermute | solution.py:37
  302.1 33.2 %collective-permute-start.40 = (bf16[2,128,1024]{2,1,0:T(8,128)(2,1)}, bf16[2,128,1024]{2,1,0:T(8,128)(2,1)}, u32[]{:S(2)}, u32[]{:S(2)}) collective-permute-start(bf16[2,128,1024]{2,1,0:T(8,128)(2,1)} %fusion.49), channel_id=1, source_target_pairs={{0,1},{1,0},{2,3},{3,2},{4,5},{5,4},{6,7},{7,6},{8,9},{9,8},{10,11... | collective-permute-start | bytes 1572872 | tf_op jit(solution)/shard_map/ppermute | solution.py:37
  305.3 24.0 %collective-permute-start.48 = (bf16[256,896]{1,0:T(8,128)(2,1)}, bf16[256,896]{1,0:T(8,128)(2,1)}, u32[]{:S(2)}, u32[]{:S(2)}) collective-permute-start(bf16[256,896]{1,0:T(8,128)(2,1)} %get-tuple-element.29), channel_id=1, source_target_pairs={{0,24},{1,25},{2,26},{3,27},{4,28},{5,29},{6,30},{7,31},{8,16},{9,... | collective-permute-start | bytes 1376264 | tf_op jit(solution)/shard_map/ppermute | solution.py:37
  308.1 22.3 %collective-permute-start.47 = (bf16[256,896]{1,0:T(8,128)(2,1)S(1)}, bf16[256,896]{1,0:T(8,128)(2,1)}, u32[]{:S(2)}, u32[]{:S(2)}) collective-permute-start(bf16[256,896]{1,0:T(8,128)(2,1)S(1)} %get-tuple-element.30), channel_id=1, source_target_pairs={{0,16},{1,17},{2,18},{3,19},{4,20},{5,21},{6,22},{7,23},{8,24},{9,... | collective-permute-start | bytes 1376264 | tf_op jit(solution)/shard_map/ppermute | solution.py:37
  319.8 34.8 %collective-permute-start.45 = (bf16[64,1024]{1,0:T(8,128)(2,1)S(1)}, bf16[64,1024]{1,0:T(8,128)(2,1)S(1)}, u32[]{:S(2)}, u32[]{:S(2)}) collective-permute-start(bf16[64,1024]{1,0:T(8,128)(2,1)S(1)} %bitcast.512), channel_id=1, source_target_pairs={{0,4},{1,5},{2,6},{3,7},{4,0},{5,1},{6,2},{7,3},{8,12},{9,13},{10,... | collective-permute-start | bytes 393224 | tf_op jit(solution)/shard_map/ppermute | solution.py:37
  (124 other events, 1273.3 us)

commit v3 on v2

--- a/solution.py
+++ b/solution.py
@@ -3,6 +3,8 @@
 import jax
 import jax.numpy as jnp
 from jax import lax
+from jax.experimental import pallas as pl
+from jax.experimental.pallas import tpu as pltpu
 from jax.sharding import PartitionSpec as P
 
 H = 16
@@ -55,7 +57,7 @@
     return jnp.concatenate([a * cosine - b * sine, b * cosine + a * sine], axis=-1)
 
 
-def local(plan, layer_in, first_layer_value, v1_acc, cotangent, seq_starts, norm1_gain, w_query, w_key, w_value,
+def general(plan, layer_in, first_layer_value, v1_acc, cotangent, seq_starts, norm1_gain, w_query, w_key, w_value,
           w_out, norm2_gain, w_gate, w_up, w_down):
     G, T, bits = plan.G, plan.T, plan.bits
     micro, L, D = layer_in.shape
@@ -97,9 +99,7 @@
     def reduce_t(partial):
         blocks = partial.reshape((T, -1) + partial.shape[1:])
         for bit in reversed(bits):
-            order = [j for j in range(blocks.shape[0])]
             shape = blocks.shape
-            split = blocks.reshape((-1, 2, 1) + shape[1:]) if False else blocks
             split = blocks.reshape((shape[0] // 2, 2) + shape[1:])
             blocks = split[:, 0] + to_t(split[:, 1].astype(BF16), bit).astype(F32)
         return blocks[0]
@@ -284,6 +284,611 @@
             hidden_join(gu_g[:, :, FT:]), down_g)
 
 
+FAST_G, FAST_T, FAST_L, D, HT, FT, FROWS, ROWS = 4, 4, 64, 1024, 256, 704, 88, 32
+M, N = 2 * FAST_L, 8 * FAST_L
+HALF = N // 2
+WQ = 3 * HT + 128
+ORDER = (0, 2, 1, 3)
+HD = 64
+ARRIVED = ((0, 0), (1, 0), (2, 0), (3, 0), (0, 1), (2, 1), (1, 1), (3, 1))
+LEAVING = {(0, 0): (0, 0), (1, 0): (0, 1), (2, 0): (1, 0), (3, 0): (1, 1), (0, 1): (2, 0), (2, 1): (2, 1), (1, 1): (3, 0), (3, 1): (3, 1)}
+VMEM = pl.BlockSpec(memory_space=pltpu.VMEM)
+SMEM = pl.BlockSpec(memory_space=pltpu.SMEM)
+ANY = pl.BlockSpec(memory_space=pltpu.HBM)
+
+
+def shape(dims, dtype=BF16):
+    return jax.ShapeDtypeStruct(dims, dtype)
+
+
+def call(kernel, outs, specs, args, scratch=(), mib=40):
+    return pl.pallas_call(
+        kernel,
+        out_shape=outs,
+        in_specs=specs,
+        out_specs=jax.tree.map(lambda _: VMEM, outs),
+        scratch_shapes=list(scratch),
+        compiler_params=pltpu.CompilerParams(vmem_limit_bytes=mib << 20),
+        cost_estimate=pl.CostEstimate(flops=1, bytes_accessed=1, transcendentals=0),
+    )(*args)
+
+
+def aligned(index, size):
+    return pl.ds(pl.multiple_of(index * size, size), size)
+
+
+def eye(rows, lanes):
+    return (lax.broadcasted_iota(jnp.int32, (rows, lanes), 0) == lax.broadcasted_iota(jnp.int32, (rows, lanes), 1)).astype(BF16)
+
+
+def tiles_in(block):
+    lines = [jnp.concatenate([block[j * 8:j * 8 + 8, i * 128:i * 128 + 128] for j in range(11)], axis=1) for i in range(8)]
+    return jnp.concatenate(lines, axis=0)
+
+
+def tiles_out(block):
+    lines = [jnp.concatenate([block[i * 8:i * 8 + 8, j * 128:j * 128 + 128] for i in range(8)], axis=1) for j in range(11)]
+    return jnp.concatenate(lines, axis=0)
+
+
+def line_tiles_in(block):
+    tiles = [block[j * 8:j * 8 + 8, i * 128:i * 128 + 128] for j in range(4) for i in range(8)]
+    tiles += [jnp.zeros_like(tiles[0])] * 3
+    return jnp.concatenate([jnp.concatenate(tiles[n * 7:n * 7 + 7], axis=1) for n in range(5)], axis=0)
+
+
+def line_tiles_out(block):
+    tiles = [block[n * 8:n * 8 + 8, i * 128:i * 128 + 128] for n in range(5) for i in range(7)]
+    return jnp.concatenate([jnp.concatenate(tiles[j * 8:j * 8 + 8], axis=1) for j in range(4)], axis=0)
+
+
+def pack_first(ids, gain_one, gain_two, wq, wk, wv, wo, x, v, c, out, keep, lines, xv_out, c_out, rows, whole, sem):
+    h, t = ids[1], ids[2]
+    copies = []
+    for j in (2, 3, 0, 1):
+        to = keep if j < 2 else out
+        for i, w in enumerate((wq, wk, wv)):
+            copies.append((w.at[:, aligned(t ^ j, HT)], to.at[j % 2, :, i * HT:(i + 1) * HT]))
+    copies += [(wo, whole), (x.at[1 - h], xv_out.at[:, :D]), (v.at[1 - h], xv_out.at[:, D:]), (c.at[1 - h], c_out)]
+    started = fetch(copies, sem)
+    rows[...] = jnp.zeros_like(rows)
+    rows[0:1] = gain_one[...].astype(F32)
+    rows[1:2] = gain_two[...].astype(F32)
+    gains = dot_rows(rows[...].astype(BF16), eye(8, 128)).astype(BF16)
+    for j in range(4):
+        (keep if j < 2 else out)[j % 2, :, 3 * HT:] = gains
+    started[12].wait()
+    lines[...] = line_tiles_in(whole[...].astype(F32)).astype(BF16)
+    for n, copy in enumerate(started):
+        if n != 12:
+            copy.wait()
+
+
+def pack_hidden(ids, wg, wu, wd, keep, out, down, nat, gate, up, whole, sem):
+    t = ids[2]
+    started = fetch([(wg, gate), (wu, up), (wd, whole)], sem)
+    for a, w in enumerate((gate, up)):
+        started[a].wait()
+        for m in range(4):
+            for i in range(8):
+                at, to = (i * 4 + m) * FROWS, a * FT + i * FROWS
+                nat[m, :, to:to + FROWS] = w[:, at:at + FROWS].astype(F32)
+    for j in range(4):
+        to = keep if j < 2 else out
+        to[j % 2] = nat[t ^ j].astype(BF16)
+    started[2].wait()
+    down[...] = tiles_in(whole[...].astype(F32)).astype(BF16)
+
+
+def pack_out(b0, b1, b2, b3, out, raw, sem):
+    started = fetch([((b0, b1, b2, b3)[n // 2].at[n % 2, 4 * ROWS:], raw.at[n]) for n in range(8)], sem)
+    for n in range(8):
+        started[n].wait()
+        out[n * ROWS:(n + 1) * ROWS] = line_tiles_out(raw[n].astype(F32)).astype(BF16)
+
+
+def pack_second(ids, x, v, moved, xv_out, v_keep, own, sem):
+    h, t = ids[1], ids[2]
+    started = fetch([(x.at[h], xv_out.at[:FAST_L, :D]), (v.at[h], own.at[:FAST_L]),
+                     (moved.at[:, :D], xv_out.at[FAST_L:, :D]), (moved.at[:, D:], own.at[FAST_L:])], sem)
+    for copy in started:
+        copy.wait()
+    for j in range(2):
+        v_keep[j] = own[:, aligned(t ^ j, HT)]
+        xv_out[:, D + j * HT:D + (j + 1) * HT] = own[:, aligned(t ^ (j + 2), HT)]
+
+
+def pack_third(mine, moved, v_keep, out, v_two):
+    out[:M, :D] = mine[:, :D]
+    out[M:, :D] = moved[:, :D]
+    out[:M, D:] = v_keep[1]
+    out[M:, D:] = moved[:, D + HT:]
+    v_two[:M] = v_keep[0]
+    v_two[M:] = moved[:, D:D + HT]
+
+
+def fetch(copies, sem):
+    started = []
+    for i, (source, target) in enumerate(copies):
+        copy = pltpu.make_async_copy(source, target, sem.at[i])
+        copy.start()
+        started.append(copy)
+    return started
+
+
+def swap_halves(u):
+    width = u.shape[-1]
+    lane = lax.broadcasted_iota(jnp.int32, u.shape, 1)
+    up = pltpu.roll(u, width - HD // 2, 1)
+    down = pltpu.roll(u, HD // 2, 1)
+    return jnp.where(lane % HD < HD // 2, up, down)
+
+
+def scale_of(x):
+    return lax.rsqrt(jnp.mean(x * x, axis=-1, keepdims=True) + EPS)
+
+
+def attend_kernel(ids, x2, xc, v2, cs, sn, bias, b0, b1, b2, b3, w, normed, qkv, attn, low, lse, gains, sem):
+    g, h, t = ids[0], ids[1], ids[2]
+    copies = []
+    for n, (k, dh) in enumerate(ARRIVED):
+        b = (b0, b1, b2, b3)[n // 2]
+        for i, s in enumerate(ORDER):
+            row = ((g ^ k) * 2 + (h ^ dh)) * 4 + (t ^ s)
+            copies.append((b.at[n % 2, i * ROWS:(i + 1) * ROWS], w.at[aligned(row, ROWS)]))
+    for copy in fetch(copies, sem):
+        copy.wait()
+    gains[...] = dot_cols(eye(8, 128), w[:, 3 * HT:])
+    gain = gains[0:1, :]
+    for b in range(2):
+        rows = slice(b * HALF, (b + 1) * HALF)
+        source = x2 if b == 0 else xc
+        x = source[:, :D].astype(F32)
+        r = (x * scale_of(x) * gain).astype(BF16)
+        normed[rows] = r
+        out = dot(r, w[:, :3 * HT])
+        for i in range(2):
+            u = out[:, i * HT:(i + 1) * HT]
+            qkv[rows, i * HT:(i + 1) * HT] = (u * cs[rows] + swap_halves(u) * sn[rows]).astype(BF16)
+        value = v2[...] if b == 0 else xc[:, D:]
+        qkv[rows, 2 * HT:] = (0.5 * out[:, 2 * HT:] + 0.5 * value.astype(F32)).astype(BF16)
+    for b in range(2):
+        rows = slice(b * HALF, (b + 1) * HALF)
+        outs, tops = [], []
+        for i in range(4):
+            lanes = slice(i * HD, (i + 1) * HD)
+            q = qkv[rows, lanes]
+            k = qkv[:, HT + i * HD:HT + (i + 1) * HD]
+            v = qkv[:, 2 * HT + i * HD:2 * HT + (i + 1) * HD]
+            s = dot_cols(q, k) * SCALE + bias[rows]
+            top = jnp.max(s, axis=-1, keepdims=True)
+            p = jnp.exp(s - top)
+            total = jnp.sum(p, axis=-1, keepdims=True)
+            outs.append(dot(p.astype(BF16), v) / total)
+            tops.append(top + jnp.log(total))
+        o = jnp.concatenate(outs, axis=1)
+        attn[rows] = o
+        low[rows] = o.astype(BF16)
+        lse[rows] = jnp.concatenate(tops, axis=1)
+
+
+def after_kernel(ids, x2, xc, o2, oc, gains, co2, coc, full, after, normed, own_w, w, sem):
+    g, h, t = ids[0], ids[1], ids[2]
+    copies = []
+    for i, s in enumerate(ORDER):
+        source = co2 if i < 2 else coc
+        for n, (k, dh) in enumerate(ARRIVED):
+            row = ((g ^ k) * 2 + (h ^ dh)) * 4 + (t ^ s)
+            at = (i % 2) * HT + n * ROWS
+            copies.append((source.at[at:at + ROWS], w.at[aligned(row, ROWS)]))
+    started = fetch(copies, sem)
+    for i, s in enumerate(ORDER):
+        source = o2 if i < 2 else oc
+        for p in range(4):
+            q = ORDER.index(ORDER[p] ^ s)
+            full[p * M:(p + 1) * M, aligned(t ^ s, HT)] = source[(i % 2) * N + q * M:(i % 2) * N + (q + 1) * M]
+    for copy in started:
+        copy.wait()
+    own_w[...] = w[aligned(t, HT)]
+    gain = gains[1:2, :]
+    for b in range(2):
+        rows = slice(b * HALF, (b + 1) * HALF)
+        source = x2 if b == 0 else xc
+        a = source[:, :D].astype(F32) + dot(full[rows], w[...])
+        after[rows] = a
+        normed[rows] = (a * scale_of(a) * gain).astype(BF16)
+
+
+def feed_kernel(ids, normed, after, c2, cc, u0, u1, u2, u3,
+                hidden, dgu, out_keep, out_send, r_keep, r_send, gain_g, c_all, w, wd, wide, raw, sem, sem_d):
+    g, h, t = ids[0], ids[1], ids[2]
+    copies, copies_d = [], []
+    for n, (k, dh) in enumerate(ARRIVED):
+        b = (u0, u1, u2, u3)[n // 2]
+        for i, s in enumerate(ORDER):
+            row = ((g ^ k) * 2 + (h ^ dh)) * 4 + (t ^ s)
+            copies.append((b.at[n % 2, i * ROWS:(i + 1) * ROWS], w.at[aligned(row, ROWS)]))
+        copies_d.append((b.at[n % 2, 4 * ROWS:], raw.at[n]))
+    started, started_d = fetch(copies, sem), fetch(copies_d, sem_d)
+    for p in range(4):
+        c_all[p * M:(p + 1) * M] = (c2 if p < 2 else cc)[(p % 2) * M:(p % 2 + 1) * M]
+    for copy in started_d:
+        copy.wait()
+    for n, (k, dh) in enumerate(ARRIVED):
+        wide[aligned((g ^ k) * 2 + (h ^ dh), FROWS)] = tiles_out(raw[n].astype(F32))
+    wd[...] = wide[...].astype(BF16)
+    for copy in started:
+        copy.wait()
+    gain_sum = jnp.zeros((1, D), F32)
+    for b in range(2):
+        rows = slice(b * HALF, (b + 1) * HALF)
+        gu = dot(normed[rows], w[...])
+        gate, up = gu[:, :FT], gu[:, FT:]
+        sig = 1.0 / (1.0 + jnp.exp(-gate))
+        act = gate * sig
+        hid = (act * up).astype(BF16)
+        hidden[rows] = hid
+        dh = dot_cols(c_all[rows], wd[...])
+        dgate = (dh * up * (sig * (1.0 + gate * (1.0 - sig)))).astype(BF16)
+        dup = (dh * act).astype(BF16)
+        dgu[rows, :FT] = dgate
+        dgu[rows, FT:] = dup
+        dr = dot_cols(dgu[rows], w[...])
+        out = dot(hid, wd[...])
+        a = after[rows]
+        gain_sum = gain_sum + jnp.sum(dr * (a * scale_of(a)), axis=0, keepdims=True)
+        if b == 0:
+            r_keep[...] = dr
+            out_keep[...] = out
+        else:
+            r_send[...] = dr.astype(BF16)
+            out_send[...] = out.astype(BF16)
+    gain_g[...] = gain_sum
+
+
+def feed_weights_kernel(ids, normed, dgu, hidden, c_all, a_keep, a_send, b_keep, b_send, gu, full):
+    g, h = ids[0], ids[1]
+    full[...] = dot_rows(hidden[...], c_all[...])
+    for k in range(4):
+        gu[...] = dot_rows(normed[:, aligned(g ^ k, HT)], dgu[...])
+        for e in range(2):
+            target, at = LEAVING[(k, e)]
+            target = (a_keep, a_send, b_keep, b_send)[target]
+            target[at, :4 * ROWS] = gu[aligned(h ^ e, 4 * ROWS)].astype(BF16)
+            target[at, 4 * ROWS:] = tiles_in(full[aligned((g ^ k) * 2 + (h ^ e), FROWS)]).astype(BF16)
+
+
+def fold_kernel(keep, moved, kept, send):
+    kept[...] = keep[:M] + moved[:M].astype(F32)
+    send[...] = (keep[M:] + moved[M:].astype(F32)).astype(BF16)
+
+
+def fold_both_kernel(keep, dv, moved, kept, send):
+    kept[...] = keep[:M] + moved[:M, :D].astype(F32)
+    send[:, :D] = (keep[M:] + moved[M:, :D].astype(F32)).astype(BF16)
+    send[:, D:D + HT] = dv[M:]
+    send[:, D + HT:] = moved[M:, D:]
+
+
+def branch_kernel(keep, moved, after, gains, c2, grad_after, low):
+    a = after[:M]
+    scale = scale_of(a)
+    hat = a * scale
+    dy = (keep[...] + moved[...].astype(F32)) * gains[1:2, :]
+    d = c2[:M].astype(F32) + scale * (dy - hat * jnp.mean(dy * hat, axis=-1, keepdims=True))
+    grad_after[...] = d
+    low[...] = d.astype(BF16)
+
+
+def attend_back_kernel(ids, da2, dac, wo, qkv, attn, lse, bias, cs, sn, w, x2, xc,
+                       dqkv, r_keep, r_send, gain_g, do, dk, dv):
+    for b in range(2):
+        rows = slice(b * HALF, (b + 1) * HALF)
+        do[rows] = dot_cols((da2 if b == 0 else dac)[...], wo[...]).astype(BF16)
+    for b in range(2):
+        rows = slice(b * HALF, (b + 1) * HALF)
+        dqs = []
+        for i in range(4):
+            lanes = slice(i * HD, (i + 1) * HD)
+            q = qkv[rows, lanes]
+            k = qkv[:, HT + i * HD:HT + (i + 1) * HD]
+            v = qkv[:, 2 * HT + i * HD:2 * HT + (i + 1) * HD]
+            d = do[rows, lanes]
+            delta = jnp.sum(d.astype(F32) * attn[rows, lanes], axis=-1, keepdims=True)
+            p = jnp.exp(dot_cols(q, k) * SCALE + bias[rows] - lse[rows, i:i + 1])
+            ds = (p * (dot_cols(d, v) - delta)).astype(BF16)
+            dqs.append(dot(ds, k))
+            dki, dvi = dot_rows(ds, q), dot_rows(p.astype(BF16), d)
+            if b == 0:
+                dk[:, lanes], dv[:, lanes] = dki, dvi
+            else:
+                dk[:, lanes], dv[:, lanes] = dk[:, lanes] + dki, dv[:, lanes] + dvi
+        u = jnp.concatenate(dqs, axis=1) * SCALE
+        dqkv[rows, :HT] = (u * cs[rows] - swap_halves(u) * sn[rows]).astype(BF16)
+    gain_sum = jnp.zeros((1, D), F32)
+    for b in range(2):
+        rows = slice(b * HALF, (b + 1) * HALF)
+        u = dk[rows] * SCALE
+        dqkv[rows, HT:2 * HT] = (u * cs[rows] - swap_halves(u) * sn[rows]).astype(BF16)
+        dqkv[rows, 2 * HT:] = (0.5 * dv[rows]).astype(BF16)
+        dr = dot_cols(dqkv[rows], w[:, :3 * HT])
+        x = (x2 if b == 0 else xc)[:, :D].astype(F32)
+        gain_sum = gain_sum + jnp.sum(dr * (x * scale_of(x)), axis=0, keepdims=True)
+        if b == 0:
+            r_keep[...] = dr
+        else:
+            r_send[:, :D] = dr.astype(BF16)
+            r_send[:, D:] = dqkv[rows, 2 * HT:]
+    gain_g[...] = gain_sum
+
+
+def attend_weights_kernel(ids, normed, dqkv, gain_one, gain_two, full, da2, dac, a_keep, a_send, b_keep, b_send,
+                          scratch, rows_g, qkv):
+    g, h, t = ids[0], ids[1], ids[2]
+    rows_g[...] = jnp.zeros_like(rows_g)
+    rows_g[0:1] = gain_one[...]
+    rows_g[1:2] = gain_two[...]
+    for k in range(4):
+        lanes = aligned(g ^ k, HT)
+        qkv[:, :3 * HT] = dot_rows(normed[:, lanes], dqkv[...])
+        qkv[:, 3 * HT:] = dot_rows(rows_g[:, lanes].astype(BF16), eye(8, 128))
+        scratch[...] = dot_rows(full[:HALF, lanes], da2[...]) + dot_rows(full[HALF:, lanes], dac[...])
+        for e in range(2):
+            target, at = LEAVING[(k, e)]
+            target = (a_keep, a_send, b_keep, b_send)[target]
+            target[at, :4 * ROWS] = qkv[aligned(h ^ e, 4 * ROWS)].astype(BF16)
+            target[at, 4 * ROWS:] = line_tiles_in(scratch[aligned((h ^ e) * 4 + t, ROWS)]).astype(BF16)
+
+
+def sum_first_kernel(a_keep, a_moved, b_keep, b_moved, a_own, a_send, b_own, b_send):
+    for keep, moved, own, out in ((a_keep, a_moved, a_own, a_send), (b_keep, b_moved, b_own, b_send)):
+        own[...] = (keep[0].astype(F32) + moved[0].astype(F32)).astype(BF16)
+        out[...] = (keep[1].astype(F32) + moved[1].astype(F32)).astype(BF16)
+
+
+def sum_second_kernel(b_own, b_moved, b_send):
+    b_send[...] = (b_own[...].astype(F32) + b_moved[...].astype(F32)).astype(BF16)
+
+
+def sum_third(a_own, a_moved, moved, total):
+    total[...] = (a_own[...].astype(F32) + a_moved[...].astype(F32)) + moved[...].astype(F32)
+
+
+def sum_hidden_kernel(ids, a_own, a_moved, moved, kept, send, down, total):
+    t = ids[2]
+    sum_third(a_own, a_moved, moved, total)
+    for j in range(4):
+        (kept if j < 2 else send)[j % 2] = total[aligned(t ^ j, ROWS)].astype(BF16)
+    down[...] = tiles_out(total[4 * ROWS:])
+
+
+def sum_qkv_kernel(ids, a_own, a_moved, moved, kept, send, out, total):
+    t = ids[2]
+    sum_third(a_own, a_moved, moved, total)
+    for j in range(4):
+        (kept if j < 2 else send)[j % 2] = total[aligned(t ^ j, ROWS)].astype(BF16)
+    out[...] = line_tiles_out(total[4 * ROWS:])
+
+
+def join_qkv_kernel(ids, kept, first, last, q, k, v, gains):
+    t = ids[2]
+    parts = (kept[0], first[0], last[0], last[1])
+    for s, part in zip(ORDER, parts):
+        for i, ref in enumerate((q, k, v)):
+            ref[:, aligned(t ^ s, HT)] = part[:, i * HT:(i + 1) * HT].astype(F32)
+    low = [part[:, 3 * HT:].astype(F32) for part in parts]
+    gains[...] = (low[0] + low[1]) + (low[2] + low[3])
+
+
+def join_hidden_kernel(ids, kept, first, last, gate, up, nat):
+    t = ids[2]
+    for s, part in zip(ORDER, (kept[0], first[0], last[0], last[1])):
+        nat[t ^ s] = part.astype(F32)
+    for m in range(4):
+        for a, ref in enumerate((gate, up)):
+            for i in range(8):
+                to, at = (i * 4 + m) * FROWS, a * FT + i * FROWS
+                ref[:, to:to + FROWS] = nat[m, :, at:at + FROWS]
+
+
+def input_kernel(ids, keep, moved, x2, gains, grad_after, dv, dv_core, own, send, both):
+    t = ids[2]
+    x = x2[:M, :D].astype(F32)
+    scale = scale_of(x)
+    hat = x * scale
+    dy = (keep[...] + moved[:, :D].astype(F32)) * gains[0:1, :]
+    both[:, :D] = (grad_after[...] + scale * (dy - hat * jnp.mean(dy * hat, axis=-1, keepdims=True))).astype(BF16)
+    parts = (dv[:M], moved[:, D:D + HT], dv_core[:M, D:], moved[:, D + HT:])
+    for s, part in zip(ORDER, parts):
+        both[:, aligned(4 + (t ^ s), HT)] = part
+    own[...] = both[:FAST_L]
+    send[...] = both[FAST_L:]
+
+
+def home_kernel(ids, own, moved, v1, grad, v_out):
+    h = ids[1]
+    grad[h] = own[:, :D].astype(F32)
+    grad[1 - h] = moved[:, :D].astype(F32)
+    v_out[h] = v1[h] + own[:, D:].astype(F32)
+    v_out[1 - h] = v1[1 - h] + moved[:, D:].astype(F32)
+
+
+def result_kernel(keep, moved, after, own, send):
+    out = after[:M] + (keep[...] + moved[...].astype(F32))
+    own[...] = out[:FAST_L].astype(BF16)
+    send[...] = out[FAST_L:].astype(BF16)
+
+
+def result_home_kernel(ids, own, moved, out):
+    h = ids[1]
+    out[h] = own[...]
+    out[1 - h] = moved[...]
+
+
+def fast(plan, layer_in, first_layer_value, v1_acc, cotangent, seq_starts, norm1_gain, w_query, w_key, w_value,
+         w_out, norm2_gain, w_gate, w_up, w_down):
+    L = FAST_L
+    g, gy = lax.axis_index("gx"), lax.axis_index("gy")
+    h, t = gy // 4, gy % 4
+    ids = jnp.stack([g, h, t]).astype(jnp.int32)
+
+    def to_z(array):
+        return send(array, plan.t_swap[2])
+
+    def to_core(array):
+        return send(array, plan.t_swap[1])
+
+    def to_h(array):
+        return send(array, plan.h_swap)
+
+    def to_x(array):
+        return send(array, plan.g_swap[1])
+
+    def to_y(array):
+        return send(array, plan.g_swap[2])
+
+    def after_these(array, *others):
+        return lax.optimization_barrier((array,) + others)[0]
+
+    def spread(own, other, *first):
+        a_pair = jnp.stack([own, to_x(own)])
+        b_pair = jnp.stack([other, to_y(other)])
+        a_pair, b_pair = lax.optimization_barrier((a_pair, b_pair) + first)[:2]
+        return a_pair, to_y(a_pair), b_pair, to_x(b_pair)
+
+    starts = pick(seq_starts, h)
+    member = t ^ jnp.array(ORDER, jnp.int32)
+    half = h ^ jnp.arange(2, dtype=jnp.int32)
+    position = ((half[None, :] * 4 + member[:, None]) * L)[:, :, None] + jnp.arange(L, dtype=jnp.int32)
+    position = position.reshape(N) + g * N
+    begin = jnp.max(jnp.where(starts[None, :] <= position[:, None], starts[None, :], 0), axis=1)
+    visible = (begin[:, None] == begin[None, :]) & (position[None, :] <= position[:, None])
+    bias = jnp.where(visible, 0.0, NEG).astype(F32)
+    frequency = 10000.0 ** (-(jnp.arange(HD // 2, dtype=F32) * 2.0 / HD))
+    angles = (position - begin).astype(F32)[:, None] * frequency[None, :]
+    cosine, sine = jnp.cos(angles), jnp.sin(angles)
+    cs = jnp.tile(jnp.concatenate([cosine, cosine], axis=1), (1, 4))
+    sn = jnp.tile(jnp.concatenate([-sine, sine], axis=1), (1, 4))
+
+    q_send, q_keep, o_block, xv_send, c_send = call(
+        pack_first, (shape((2, ROWS, WQ)), shape((2, ROWS, WQ)), shape((40, WQ)), shape((L, 2 * D)), shape((L, D))),
+        [SMEM] + [VMEM] * 2 + [ANY] * 7,
+        (ids, norm1_gain[None], norm2_gain[None], w_query, w_key, w_value, w_out, layer_in, first_layer_value, cotangent),
+        [pltpu.VMEM((8, ROWS), F32), pltpu.VMEM((ROWS, D), BF16), pltpu.SemaphoreType.DMA((16,))], mib=63)
+    q_first = to_z(q_send)
+    xv_moved = to_h(xv_send)
+    q_last = to_core(jnp.stack([q_keep[1], q_first[1]]))
+    q_block = jnp.concatenate([q_keep[0], q_first[0], q_last[0], q_last[1], o_block], axis=0)
+    q_other = to_h(q_block)
+    xv_out, v_keep = call(pack_second, (shape((M, D + 2 * HT)), shape((2, M, HT))), [SMEM] + [ANY] * 3,
+                          (ids, layer_in, first_layer_value, xv_moved), [pltpu.VMEM((M, D), BF16), pltpu.SemaphoreType.DMA((4,))], mib=63)
+    x_two, v_two = call(pack_third, (shape((HALF, D + HT)), shape((HALF, HT))), [VMEM] * 3, (xv_out, to_z(xv_out), v_keep))
+    x_core = to_core(x_two)
+    q_other, cs, sn, bias, _ = lax.optimization_barrier((q_other, cs, sn, bias, xv_out))
+    q_parts = spread(q_block, q_other, x_two)
+
+    u_keep, u_send, d_block = call(
+        pack_hidden, (shape((2, ROWS, 2 * FT)), shape((2, ROWS, 2 * FT)), shape((2 * ROWS, 2 * FT))), [SMEM] + [ANY] * 3,
+        (after_these(ids, q_send), w_gate, w_up, w_down),
+        [pltpu.VMEM((4, ROWS, 2 * FT), F32), pltpu.VMEM((ROWS, 4 * FT), BF16), pltpu.VMEM((ROWS, 4 * FT), BF16), pltpu.VMEM((FROWS, D), BF16),
+         pltpu.SemaphoreType.DMA((3,))], mib=63)
+    u_first = to_z(after_these(u_send, q_first))
+    u_last = to_core(jnp.stack([u_keep[1], u_first[1]]))
+    u_block = jnp.concatenate([u_keep[0], u_first[0], u_last[0], u_last[1], d_block], axis=0)
+    u_other = to_h(after_these(u_block, q_other))
+    c_moved = to_h(after_these(c_send, u_other))
+    u_a = jnp.stack([u_block, to_x(after_these(u_block, q_parts[2]))])
+    u_b = jnp.stack([u_other, to_y(u_other)])
+    o_own = call(pack_out, shape((HT, D)), [ANY] * 4, q_parts, [pltpu.VMEM((8, 40, WQ), BF16), pltpu.SemaphoreType.DMA((8,))])
+    o_first = to_z(o_own)
+    q_parts = lax.optimization_barrier(q_parts + (u_a, u_b))[:4]
+    qkv_w, normed_one, qkv, attn, attn_low, lse, gains = call(
+        attend_kernel,
+        (shape((D, WQ)), shape((N, D)), shape((N, 3 * HT)), shape((N, HT), F32), shape((N, HT)), shape((N, 4), F32), shape((8, D), F32)),
+        [SMEM] + [VMEM] * 6 + [ANY] * 4, (ids, x_two, x_core, v_two, cs, sn, bias, *q_parts),
+        [pltpu.SemaphoreType.DMA((32,))])
+    a_two = jnp.concatenate([attn_low, to_z(attn_low)], axis=0)
+    c_own = jnp.concatenate([pick(cotangent, h), after_these(c_moved, attn_low)], axis=0)
+    o_two = jnp.concatenate([o_own, o_first], axis=0)
+    o_core = to_core(after_these(o_two, attn_low))
+    c_two = jnp.concatenate([c_own, to_z(after_these(c_own, a_two))], axis=0)
+    c_core = to_core(c_two)
+    u_parts = (u_a, to_y(u_a), u_b, to_x(u_b))
+    a_core = to_core(a_two)
+    attn_full, after, normed_two, out_w = call(
+        after_kernel, (shape((N, D)), shape((N, D), F32), shape((N, D)), shape((HT, D))),
+        [SMEM] + [VMEM] * 5 + [ANY] * 2, (ids, x_two, x_core, a_two, a_core, gains, o_two, o_core),
+        [pltpu.VMEM((D, D), BF16), pltpu.SemaphoreType.DMA((32,))])
+    hidden, dgu, out_keep, out_send, r_keep, r_send, gain_two_g, c_all = call(
+        feed_kernel,
+        (shape((N, FT)), shape((N, 2 * FT)), shape((HALF, D), F32), shape((HALF, D)), shape((HALF, D), F32), shape((HALF, D)),
+         shape((1, D), F32), shape((N, D))),
+        [SMEM] + [VMEM] * 4 + [ANY] * 4, (ids, normed_two, after, c_two, c_core, *u_parts),
+        [pltpu.VMEM((D, 2 * FT), BF16), pltpu.VMEM((8 * FROWS, D), BF16), pltpu.VMEM((8 * FROWS, D), F32), pltpu.VMEM((8, 2 * ROWS, 2 * FT), BF16),
+         pltpu.SemaphoreType.DMA((32,)), pltpu.SemaphoreType.DMA((8,))])
+
+    kept, sent = call(fold_kernel, (shape((M, D), F32), shape((M, D))), [VMEM] * 2, (r_keep, to_core(r_send)))
+    block = (2, 6 * ROWS, 2 * FT)
+    a_keep, a_send, b_keep, b_send = call(
+        feed_weights_kernel, (shape(block),) * 4, [SMEM] + [VMEM] * 4, (ids, normed_two, dgu, hidden, c_all),
+        [pltpu.VMEM((HT, 2 * FT), F32), pltpu.VMEM((8 * FROWS, D), F32)])
+    kept = after_these(kept, a_send)
+    grad_after, branch = call(branch_kernel, (shape((M, D), F32), shape((M, D))), [VMEM] * 5,
+                              (kept, to_z(sent), after, gains, c_two))
+    b_two = jnp.concatenate([branch, to_z(branch)], axis=0)
+    b_core = to_core(b_two)
+
+    u_sums = (a_keep, to_y(a_send), b_keep, to_x(b_send))
+    o_kept, o_sent = call(fold_kernel, (shape((M, D), F32), shape((M, D))), [VMEM] * 2,
+                          (out_keep, to_core(after_these(out_send, b_two))))
+    y_own, y_send = call(result_kernel, (shape((L, D)), shape((L, D))), [VMEM] * 3, (o_kept, to_z(o_sent), after))
+    layer_out = call(result_home_kernel, shape((2, L, D)), [SMEM] + [VMEM] * 2, (ids, y_own, to_h(y_send)))
+
+    b_core = after_these(b_core, o_sent)
+    dqkv, r_keep, r_send, gain_one_g = call(
+        attend_back_kernel,
+        (shape((N, 3 * HT)), shape((HALF, D), F32), shape((HALF, D + HT)), shape((1, D), F32)),
+        [SMEM] + [VMEM] * 12, (ids, b_two, b_core, out_w, qkv, attn, lse, bias, cs, sn, qkv_w, x_two, x_core),
+        [pltpu.VMEM((N, HT), BF16), pltpu.VMEM((N, HT), F32), pltpu.VMEM((N, HT), F32)])
+    dv_keep = dqkv[:HALF, 2 * HT:]
+    r_core = after_these(to_core(r_send), y_send)
+    kept, sent = call(fold_both_kernel, (shape((M, D), F32), shape((M, D + 2 * HT))), [VMEM] * 3, (r_keep, dv_keep, r_core))
+    block = (2, 4 * ROWS + 40, WQ)
+    a_keep, a_send, b_keep, b_send = call(
+        attend_weights_kernel, (shape(block),) * 4,
+        [SMEM] + [VMEM] * 7, (ids, normed_one, after_these(dqkv, sent), gain_one_g, gain_two_g, attn_full, b_two, b_core),
+        [pltpu.VMEM((HT, D), F32), pltpu.VMEM((8, D), F32), pltpu.VMEM((HT, WQ), F32)])
+    q_sums = (a_keep, to_y(a_send), b_keep, to_x(b_send))
+    own, sent = call(input_kernel, (shape((L, 2 * D)), shape((L, 2 * D))), [SMEM] + [VMEM] * 7,
+                     (ids, kept, to_z(sent), x_two, gains, grad_after, dv_keep, r_core), [pltpu.VMEM((M, 2 * D), BF16)])
+    home = to_h(sent)
+    input_grad, v1_out = call(home_kernel, (shape((2, L, D), F32),) * 2, [SMEM] + [VMEM] * 3, (ids, own, home, v1_acc))
+
+    def finish(kernel, sums, rest, *first):
+        dims = sums[0].shape[1:]
+        a_own, a_send, b_own, b_send = call(sum_first_kernel, (shape(dims),) * 4, [VMEM] * 4, sums)
+        b_send = call(sum_second_kernel, shape(dims), [VMEM] * 2, (b_own, to_y(b_send)))
+        kept, sent, rows = call(kernel, (shape((2, ROWS, dims[1])), shape((2, ROWS, dims[1])), shape(rest, F32)), [SMEM] + [VMEM] * 3,
+                                (ids, a_own, to_x(a_send), after_these(to_h(b_send), *first)), [pltpu.VMEM(dims, F32)])
+        first = to_z(sent)
+        return (ids, kept, first, to_core(jnp.stack([kept[1], first[1]]))), rows
+
+    u_sums = lax.optimization_barrier(u_sums + (a_send,))[:4]
+    q_sums = lax.optimization_barrier(q_sums + (sent,))[:4]
+    parts, down_g = finish(sum_hidden_kernel, u_sums, (FROWS, D))
+    gate_g, up_g = call(join_hidden_kernel, (shape((ROWS, 4 * FT), F32),) * 2, [SMEM] + [VMEM] * 3, parts,
+                        [pltpu.VMEM((4, ROWS, 2 * FT), F32)])
+    parts, out_g = finish(sum_qkv_kernel, q_sums, (ROWS, D), home)
+    query_g, key_g, value_g, gain_g = call(
+        join_qkv_kernel, (shape((ROWS, D), F32),) * 3 + (shape((ROWS, 128), F32),), [SMEM] + [VMEM] * 3, parts)
+    return (layer_out, input_grad, v1_out, gain_g[:, 0], query_g, key_g, value_g, out_g, gain_g[:, 1], gate_g, up_g, down_g)
+
+
+def local(plan, layer_in, *rest):
+    kept = plan.G == FAST_G and plan.T == FAST_T and layer_in.shape == (2, FAST_L, D) and rest[12].shape == (FROWS, D)
+    return (fast if kept else general)(plan, layer_in, *rest)
+
+
 def solution(mesh):
     plan = Plan(mesh.shape["gx"], mesh.shape["gy"])
     tokens, rows, vector = P(None, ALL, None), P(ALL, None), P(ALL)

time: 369 us -> 275 us (0.75); the launches traced: 362 us -> 274 us
  Pallas kernels: 0 us -> 68.5 us
  local copies, waits for them, and re-layouts: 87.3 us -> 24.5 us
  matrix products: 45.9 us -> 0 us
  other arithmetic: 46.2 us -> 6.43 us
  starting transfers between devices: 66.7 us -> 42.3 us
  waiting for transfers between devices: 113 us -> 131 us
    pallas_call x0 -> x27, Pallas kernels: none -> 68.5 us  [call(): pl.pallas_call(kernel, out_shape=outs, in_specs=specs, out_specs=jax.tree...]
    dot_general x26 -> x0, matrix products: 41.6 us -> none  [the longest x11 18.1 us: dot(): lax.dot_general(a, b, (((1,), (0,)), ((), ())), preferred_element_type=F32)]
    ppermute x66 -> x48, starting transfers between devices: 66.7 us -> 42.3 us  [send(): return lax.ppermute(array, ALL, pairs)]
    ppermute x66 -> x48, waiting for transfers between devices: 113 us -> 131 us  [send(): return lax.ppermute(array, ALL, pairs)]
    reshape x19 -> x0, local copies, waits for them, and re-layouts: 17.5 us -> none  [the longest x4 7.65 us: hidden_join(): parts.reshape(T, rows, 2 * G, frows).transpose(1, 2, 0, 3).reshape(rows, FF)]
    dynamic_update_slice x13 -> x0, local copies, waits for them, and re-layouts: 12.6 us -> none  [gather_r(): lax.dynamic_update_slice(full, to_g(pair, k)[None], (g ^ k,) + (0,) * pai...]
    broadcast_in_dim x11 -> x0, local copies, waits for them, and re-layouts: 10 us -> none  [the longest x3 5.6 us: gather_r(): to_g(pair, k)[None]]
    squeeze x7 -> x1, local copies, waits for them, and re-layouts: 8.33 us -> 0.01 us  [pick(): return lax.dynamic_index_in_dim(array, index, axis, keepdims=False)]
  transfers between devices with their start and end apart: 66 -> 48, of which waited for: 26 -> 20; matrix products, arithmetic and copies ran while one was open for 39% -> 7% of each run, Pallas kernels for 0% -> 18%
where the time goes in v3:
time: 275 us; the launch traced here: 274 us
  waiting for transfers between devices  131 us (48%)
  Pallas kernels  68.5 us (25%)
  starting transfers between devices  42.3 us (15%)
  local copies, waits for them, and re-layouts  24.5 us (9%)
  other arithmetic  6.43 us (2%)
    ppermute x48, waiting for transfers between devices, send(): return lax.ppermute(array, ALL, pairs)  131 us
    pallas_call x27, Pallas kernels, call(): pl.pallas_call(kernel, out_shape=outs, in_specs=specs, out_specs=jax.tree...  68.5 us
    ppermute x48, starting transfers between devices, send(): return lax.ppermute(array, ALL, pairs)  42.3 us
    unnamed x64, local copies, waits for them, and re-layouts  15.3 us
  transfers between devices with their start and end apart: 48, of which 20 were waited for; matrix products, arithmetic and copies ran while one was open for 7% of the time, Pallas kernels for 18%

profile of v3, /device:TPU:0, one launch (start us, length us, event | category | flops | bytes accessed | tf_op | source)
XLA Modules:
  0.0 274.0 jit_solution(7480768417756157248)
XLA Ops:
  1.3 3.0 %shard_map.238 = (bf16[2,32,896]{2,1,0:T(8,128)(2,1)}, bf16[2,32,896]{2,1,0:T(8,128)(2,1)}, bf16[40,896]{1,0:T(8,128)(2,1)}, bf16[64,2048]{1,0:T(8,128)(2,1)}, bf16[64,1024]{1,0:T(8,128)(2,1)}) custom-call(s32[3]{0:T(128)} %pad_add_fusion.ids, bf16[1,32]{1,0:T(2,128)(2,1)} %bitcast.52, bf16[1,32]{1,0:T(2,128)(2,1)} %bitcast.53, bf16[32,1024]{1,0:T(8,128)(2,1)} %wq.1, ...), custom_call_target="tpu_custom_call" | custom-call | flops 1 | bytes 1 | tf_op jit(solution)/shard_map/pallas_call | solution.py:305
  4.3 3.1 %collective-permute-start.3 = (bf16[2,32,896]{2,1,0:T(8,128)(2,1)}, bf16[2,32,896]{2,1,0:T(8,128)(2,1)S(1)}, u32[]{:S(2)}, u32[]{:S(2)}) collective-permute-start(bf16[2,32,896]{2,1,0:T(8,128)(2,1)} %get-tuple-element.127), channel_id=1, source_target_pairs={{0,2},{1,3},{2,0},{3,1},{4,6},{5,7},{6,4},{7,5},{8,10},{9,11},{10,... | collective-permute-start | bytes 344072 | tf_op jit(solution)/shard_map/ppermute | solution.py:39
  30.8 7.4 %collective-permute-done.5 = bf16[168,896]{1,0:T(8,128)(2,1)S(1)} collective-permute-done((bf16[168,896]{1,0:T(8,128)(2,1)S(1)}, bf16[168,896]{1,0:T(8,128)(2,1)S(1)}, u32[]{:S(2)}, u32[]{:S(2)}) %collective-permute-start.5) | collective-permute-done | bytes 301088 | tf_op jit(solution)/shard_map/ppermute | solution.py:39
  43.2 5.0 %collective-permute-done.7 = bf16[168,896]{1,0:T(8,128)(2,1)S(1)} collective-permute-done((bf16[168,896]{1,0:T(8,128)(2,1)S(1)}, bf16[168,896]{1,0:T(8,128)(2,1)S(1)}, u32[]{:S(2)}, u32[]{:S(2)}) %collective-permute-start.7) | collective-permute-done | bytes 301088 | tf_op jit(solution)/shard_map/ppermute | solution.py:39
  51.9 13.9 %collective-permute-done.13 = bf16[192,1408]{1,0:T(8,128)(2,1)} collective-permute-done((bf16[192,1408]{1,0:T(8,128)(2,1)}, bf16[192,1408]{1,0:T(8,128)(2,1)}, u32[]{:S(2)}, u32[]{:S(2)}) %collective-permute-start.13) | collective-permute-done | bytes 540704 | tf_op jit(solution)/shard_map/ppermute | solution.py:39
  71.1 3.2 %collective-permute-start.17 = (bf16[256,1024]{1,0:T(8,128)(2,1)S(1)}, bf16[256,1024]{1,0:T(8,128)(2,1)S(1)}, u32[]{:S(2)}, u32[]{:S(2)}) collective-permute-start(bf16[256,1024]{1,0:T(8,128)(2,1)S(1)} %shard_map.243), channel_id=1, source_target_pairs={{0,2},{1,3},{2,0},{3,1},{4,6},{5,7},{6,4},{7,5},{8,10},{9,11},{10,... | collective-permute-start | bytes 1572872 | tf_op jit(solution)/shard_map/ppermute | solution.py:39
  77.2 4.0 %collective-permute-done.14 = bf16[192,1408]{1,0:T(8,128)(2,1)} collective-permute-done((bf16[192,1408]{1,0:T(8,128)(2,1)}, bf16[192,1408]{1,0:T(8,128)(2,1)}, u32[]{:S(2)}, u32[]{:S(2)}) %collective-permute-start.14) | collective-permute-done | bytes 540704 | tf_op jit(solution)/shard_map/ppermute | solution.py:39
  83.2 8.0 %shard_map.242 = (bf16[1024,896]{1,0:T(8,128)(2,1)S(1)}, bf16[512,1024]{1,0:T(8,128)(2,1)S(1)}, bf16[512,768]{1,0:T(8,128)(2,1)S(1)}, f32[512,256]{1,0:T(8,128)S...) custom-call(s32[3]{0:T(128)S(1)} %copy-done.20, ...), custom_call_target="tpu_custom_call" | custom-call | flops 1 | bytes 1 | tf_op jit(solution)/shard_map/pallas_call | solution.py:305
  92.6 5.3 %collective-permute-done.15 = bf16[512,256]{1,0:T(8,128)(2,1)S(1)} collective-permute-done((bf16[512,256]{1,0:T(8,128)(2,1)S(1)}, bf16[512,256]{1,0:T(8,128)(2,1)S(1)}, u32[]{:S(2)}, u32[]{:S(2)}) %collective-permute-start.15) | collective-permute-done | bytes 262176 | tf_op jit(solution)/shard_map/ppermute | solution.py:39
  98.0 6.3 %collective-permute-done.20 = bf16[128,1024]{1,0:T(8,128)(2,1)S(1)} collective-permute-done((bf16[128,1024]{1,0:T(8,128)(2,1)S(1)}, bf16[128,1024]{1,0:T(8,128)(2,1)S(1)}, u32[]{:S(2)}, u32[]{:S(2)}) %collective-permute-start.20) | collective-permute-done | bytes 262176 | tf_op jit(solution)/shard_map/ppermute | solution.py:39
  104.4 5.7 %shard_map.244 = (bf16[512,1024]{1,0:T(8,128)(2,1)S(1)}, f32[512,1024]{1,0:T(8,128)S(1)}, bf16[512,1024]{1,0:T(8,128)(2,1)S(1)}, bf16[256,1024]{1,0:T(8,128)(2,1)S(1)}) custom-call(s32[3]{0:T(128)S(1)} %copy-done.20, bf16[256,1280]{1,0:T(8,128)(2,1)S(1)} %get-tuple-element.124.x2, bf16[256,1280]{1,0:T(8,128)(2,1)S(1)} %collective-permute-done.2.xc, ...), custom_call_target="tpu_custom_call" | custom-call | flops 1 | bytes 1 | tf_op jit(solution)/shard_map/pallas_call | solution.py:305
  117.6 15.2 %shard_map.245 = (bf16[512,704]{1,0:T(8,128)(2,1)S(1)}, bf16[512,1408]{1,0:T(8,128)(2,1)S(1)}, f32[256,1024]{1,0:T(8,128)S(1)}, bf16[256,1024]{1,0:T(8,128)(2,1)...) custom-call(s32[3]{0:T(128)S(1)} %copy-done.20, ...), custom_call_target="tpu_custom_call" | custom-call | flops 1 | bytes 1 | tf_op jit(solution)/shard_map/pallas_call | solution.py:305
  135.0 4.7 %shard_map.247 = (bf16[2,192,1408]{2,1,0:T(8,128)(2,1)S(1)}, bf16[2,192,1408]{2,1,0:T(8,128)(2,1)}, bf16[2,192,1408]{2,1,0:T(8,128)(2,1)S(1)}, bf16[2,192,1408]{2,1,0:T(8,128)(2,1)}) custom-call(s32[3]{0:T(128)S(1)} %copy-done.20, bf16[512,1024]{1,0:T(8,128)(2,1)S(1)} %get-tuple-element.149.normed, bf16[512,1408]{1,0:T(8,128)(2,1)S(1)} %get-tuple-element.160.dgu, ...), custom_call_target="tpu_custom_call" | custom-call | flops 1 | bytes 1 | tf_op jit(solution)/shard_map/pallas_call | solution.py:305
  139.8 3.8 %collective-permute-done.25.moved = bf16[128,1024]{1,0:T(8,128)(2,1)S(1)} collective-permute-done((bf16[128,1024]{1,0:T(8,128)(2,1)S(1)}, bf16[128,1024]{1,0:T(8,128)(2,1)S(1)}, u32[]{:S(2)}, u32[]{:S(2)}) %collective-permute-start.25) | collective-permute-done | bytes 262176 | tf_op jit(solution)/shard_map/ppermute | solution.py:39
  144.3 7.4 %collective-permute-done.26 = bf16[128,1024]{1,0:T(8,128)(2,1)S(1)} collective-permute-done((bf16[128,1024]{1,0:T(8,128)(2,1)S(1)}, bf16[128,1024]{1,0:T(8,128)(2,1)S(1)}, u32[]{:S(2)}, u32[]{:S(2)}) %collective-permute-start.26) | collective-permute-done | bytes 262176 | tf_op jit(solution)/shard_map/ppermute | solution.py:39
  154.6 9.4 %shard_map.252 = (bf16[512,768]{1,0:T(8,128)(2,1)S(1)}, f32[256,1024]{1,0:T(8,128)S(1)}, bf16[256,1280]{1,0:T(8,128)(2,1)S(1)}, f32[1,1024]{1,0:T(1,128)S(1)}) custom-call(s32[3]{0:T(128)S(1)} %copy-done.20, bf16[256,1024]{1,0:T(8,128)(2,1)S(1)} %constant_dynamic-update-slice_fusion.4.da2, bf16[256,1024]{1,0:T(8,128)(2,1)S(1)} %collective-permute-done.30.dac, ...), custom_call_target="tpu_custom_call" | custom-call | flops 1 | bytes 1 | tf_op jit(solution)/shard_map/pallas_call | solution.py:305
  164.6 8.2 %collective-permute-done.28.moved = bf16[128,1024]{1,0:T(8,128)(2,1)S(1)} collective-permute-done((bf16[128,1024]{1,0:T(8,128)(2,1)S(1)}, bf16[128,1024]{1,0:T(8,128)(2,1)S(1)}, u32[]{:S(2)}, u32[]{:S(2)}) %collective-permute-start.28) | collective-permute-done | bytes 262176 | tf_op jit(solution)/shard_map/ppermute | solution.py:39
  183.1 22.1 %collective-permute-done.44.b_moved = bf16[192,1408]{1,0:T(8,128)(2,1)S(1)} collective-permute-done((bf16[192,1408]{1,0:T(8,128)(2,1)S(1)}, bf16[192,1408]{1,0:T(8,128)(2,1)S(1)}, u32[]{:S(2)}, u32[]{:S(2)}) %collective-permute-start.44) | collective-permute-done | bytes 540704 | tf_op jit(solution)/shard_map/ppermute | solution.py:39
  205.3 3.6 %collective-permute-start.45 = (bf16[192,1408]{1,0:T(8,128)(2,1)S(1)}, bf16[192,1408]{1,0:T(8,128)(2,1)S(1)}, u32[]{:S(2)}, u32[]{:S(2)}) collective-permute-start(bf16[192,1408]{1,0:T(8,128)(2,1)S(1)} %shard_map.262), channel_id=1, source_target_pairs={{0,4},{1,5},{2,6},{3,7},{4,0},{5,1},{6,2},{7,3},{8,12},{9,13},{10,... | collective-permute-start | bytes 1622024 | tf_op jit(solution)/shard_map/ppermute | solution.py:39
  212.4 5.3 %collective-permute-done.37.b_moved = bf16[168,896]{1,0:T(8,128)(2,1)S(1)} collective-permute-done((bf16[168,896]{1,0:T(8,128)(2,1)S(1)}, bf16[168,896]{1,0:T(8,128)(2,1)S(1)}, u32[]{:S(2)}, u32[]{:S(2)}) %collective-permute-start.37) | collective-permute-done | bytes 301088 | tf_op jit(solution)/shard_map/ppermute | solution.py:39
  222.3 22.3 %collective-permute-done.45.moved = bf16[192,1408]{1,0:T(8,128)(2,1)S(1)} collective-permute-done((bf16[192,1408]{1,0:T(8,128)(2,1)S(1)}, bf16[192,1408]{1,0:T(8,128)(2,1)S(1)}, u32[]{:S(2)}, u32[]{:S(2)}) %collective-permute-start.45) | collective-permute-done | bytes 540704 | tf_op jit(solution)/shard_map/ppermute | solution.py:39
  246.1 9.5 %collective-permute-done.33.moved = bf16[64,2048]{1,0:T(8,128)(2,1)S(1)} collective-permute-done((bf16[64,2048]{1,0:T(8,128)(2,1)S(1)}, bf16[64,2048]{1,0:T(8,128)(2,1)S(1)}, u32[]{:S(2)}, u32[]{:S(2)}) %collective-permute-start.33) | collective-permute-done | bytes 262176 | tf_op jit(solution)/shard_map/ppermute | solution.py:39
  257.7 3.4 %collective-permute-start.29 = (bf16[64,1024]{1,0:T(8,128)(2,1)S(1)}, bf16[64,1024]{1,0:T(8,128)(2,1)S(1)}, u32[]{:S(2)}, u32[]{:S(2)}) collective-permute-start(bf16[64,1024]{1,0:T(8,128)(2,1)S(1)} %get-tuple-element.171), channel_id=1, source_target_pairs={{0,4},{1,5},{2,6},{3,7},{4,0},{5,1},{6,2},{7,3},{8,12},{9,13},{10,... | collective-permute-start | bytes 393224 | tf_op jit(solution)/shard_map/ppermute | solution.py:39
  264.2 3.1 %collective-permute-done.29.moved = bf16[64,1024]{1,0:T(8,128)(2,1)S(1)} collective-permute-done((bf16[64,1024]{1,0:T(8,128)(2,1)S(1)}, bf16[64,1024]{1,0:T(8,128)(2,1)S(1)}, u32[]{:S(2)}, u32[]{:S(2)}) %collective-permute-start.29) | collective-permute-done | bytes 131104 | tf_op jit(solution)/shard_map/ppermute | solution.py:39
  (206 shorter events, 89.9 us)
Async XLA Ops:
  20.2 21.9 %collective-permute-start.6 = (bf16[168,896]{1,0:T(8,128)(2,1)S(1)}, bf16[168,896]{1,0:T(8,128)(2,1)}, u32[]{:S(2)}, u32[]{:S(2)}) collective-permute-start(bf16[168,896]{1,0:T(8,128)(2,1)S(1)} %constant_dynamic-update-slice_fusion), channel_id=1, source_target_pairs={{0,8},{1,9},{2,10},{3,11},{4,12},{5,13},{6,14},{7,15},{8,0},{9,1},... | collective-permute-start | bytes 903176 | tf_op jit(solution)/shard_map/ppermute | solution.py:39
  21.8 16.4 %collective-permute-start.5 = (bf16[168,896]{1,0:T(8,128)(2,1)S(1)}, bf16[168,896]{1,0:T(8,128)(2,1)S(1)}, u32[]{:S(2)}, u32[]{:S(2)}) collective-permute-start(bf16[168,896]{1,0:T(8,128)(2,1)S(1)} %constant_dynamic-update-slice_fusion), channel_id=1, source_target_pairs={{0,4},{1,5},{2,6},{3,7},{4,0},{5,1},{6,2},{7,3},{8,12},{9,13},{10,... | collective-permute-start | bytes 903176 | tf_op jit(solution)/shard_map/ppermute | solution.py:39
  24.8 18.4 %collective-permute-start.1 = (bf16[128,1536]{1,0:T(8,128)(2,1)}, bf16[128,1536]{1,0:T(8,128)(2,1)S(1)}, u32[]{:S(2)}, u32[]{:S(2)}) collective-permute-start(bf16[128,1536]{1,0:T(8,128)(2,1)} %get-tuple-element.122.mine), channel_id=1, source_target_pairs={{0,2},{1,3},{2,0},{3,1},{4,6},{5,7},{6,4},{7,5},{8,10},{9,11},{10,... | collective-permute-start | bytes 1179656 | tf_op jit(solution)/shard_map/ppermute | solution.py:39
  42.1 23.7 %collective-permute-start.13 = (bf16[192,1408]{1,0:T(8,128)(2,1)}, bf16[192,1408]{1,0:T(8,128)(2,1)}, u32[]{:S(2)}, u32[]{:S(2)}) collective-permute-start(bf16[192,1408]{1,0:T(8,128)(2,1)} %constant_dynamic-update-slice_fusion.1), channel_id=1, source_target_pairs={{0,4},{1,5},{2,6},{3,7},{4,0},{5,1},{6,2},{7,3},{8,12},{9,13},{10,... | collective-permute-start | bytes 1622024 | tf_op jit(solution)/shard_map/ppermute | solution.py:39
  48.3 21.4 %collective-permute-start.8 = (bf16[2,168,896]{2,1,0:T(8,128)(2,1)S(1)}, bf16[2,168,896]{2,1,0:T(8,128)(2,1)}, u32[]{:S(2)}, u32[]{:S(2)}) collective-permute-start(bf16[2,168,896]{2,1,0:T(8,128)(2,1)S(1)} %pad_maximum_fusion.3.b0), channel_id=1, source_target_pairs={{0,16},{1,17},{2,18},{3,19},{4,20},{5,21},{6,22},{7,23},{8,24},{9,... | collective-permute-start | bytes 1806344 | tf_op jit(solution)/shard_map/ppermute | solution.py:39
  49.9 19.8 %collective-permute-start.9 = (bf16[2,168,896]{2,1,0:T(8,128)(2,1)S(1)}, bf16[2,168,896]{2,1,0:T(8,128)(2,1)}, u32[]{:S(2)}, u32[]{:S(2)}) collective-permute-start(bf16[2,168,896]{2,1,0:T(8,128)(2,1)S(1)} %pad_maximum_fusion.4.b2), channel_id=1, source_target_pairs={{0,8},{1,9},{2,10},{3,11},{4,12},{5,13},{6,14},{7,15},{8,0},{9,1},... | collective-permute-start | bytes 1806344 | tf_op jit(solution)/shard_map/ppermute | solution.py:39
  50.1 25.0 %collective-permute-start.12 = (bf16[192,1408]{1,0:T(8,128)(2,1)}, bf16[192,1408]{1,0:T(8,128)(2,1)}, u32[]{:S(2)}, u32[]{:S(2)}) collective-permute-start(bf16[192,1408]{1,0:T(8,128)(2,1)} %constant_dynamic-update-slice_fusion.1), channel_id=1, source_target_pairs={{0,8},{1,9},{2,10},{3,11},{4,12},{5,13},{6,14},{7,15},{8,0},{9,1},... | collective-permute-start | bytes 1622024 | tf_op jit(solution)/shard_map/ppermute | solution.py:39
  65.8 15.5 %collective-permute-start.14 = (bf16[192,1408]{1,0:T(8,128)(2,1)}, bf16[192,1408]{1,0:T(8,128)(2,1)}, u32[]{:S(2)}, u32[]{:S(2)}) collective-permute-start(bf16[192,1408]{1,0:T(8,128)(2,1)} %collective-permute-done.13), channel_id=1, source_target_pairs={{0,16},{1,17},{2,18},{3,19},{4,20},{5,21},{6,22},{7,23},{8,24},{9,... | collective-permute-start | bytes 1622024 | tf_op jit(solution)/shard_map/ppermute | solution.py:39
  66.3 16.9 %collective-permute-start.2 = (bf16[256,1280]{1,0:T(8,128)(2,1)S(1)}, bf16[256,1280]{1,0:T(8,128)(2,1)S(1)}, u32[]{:S(2)}, u32[]{:S(2)}) collective-permute-start(bf16[256,1280]{1,0:T(8,128)(2,1)S(1)} %get-tuple-element.124.x2), channel_id=1, source_target_pairs={{0,1},{1,0},{2,3},{3,2},{4,5},{5,4},{6,7},{7,6},{8,9},{9,8},{10,11... | collective-permute-start | bytes 1966088 | tf_op jit(solution)/shard_map/ppermute | solution.py:39
  69.7 21.7 %collective-permute-start.19 = (bf16[64,1024]{1,0:T(8,128)(2,1)S(1)}, bf16[64,1024]{1,0:T(8,128)(2,1)S(1)}, u32[]{:S(2)}, u32[]{:S(2)}) collective-permute-start(bf16[64,1024]{1,0:T(8,128)(2,1)S(1)} %copy-done.25), channel_id=1, source_target_pairs={{0,4},{1,5},{2,6},{3,7},{4,0},{5,1},{6,2},{7,3},{8,12},{9,13},{10,... | collective-permute-start | bytes 393224 | tf_op jit(solution)/shard_map/ppermute | solution.py:39
  71.1 20.3 %collective-permute-start.17 = (bf16[256,1024]{1,0:T(8,128)(2,1)S(1)}, bf16[256,1024]{1,0:T(8,128)(2,1)S(1)}, u32[]{:S(2)}, u32[]{:S(2)}) collective-permute-start(bf16[256,1024]{1,0:T(8,128)(2,1)S(1)} %shard_map.243), channel_id=1, source_target_pairs={{0,2},{1,3},{2,0},{3,1},{4,6},{5,7},{6,4},{7,5},{8,10},{9,11},{10,... | collective-permute-start | bytes 1572872 | tf_op jit(solution)/shard_map/ppermute | solution.py:39
  76.5 36.7 %collective-permute-start.22 = (bf16[2,192,1408]{2,1,0:T(8,128)(2,1)S(1)}, bf16[2,192,1408]{2,1,0:T(8,128)(2,1)S(1)}, u32[]{:S(2)}, u32[]{:S(2)}) collective-permute-start(bf16[2,192,1408]{2,1,0:T(8,128)(2,1)S(1)} %pad_maximum_fusion.u0), channel_id=1, source_target_pairs={{0,16},{1,17},{2,18},{3,19},{4,20},{5,21},{6,22},{7,23},{8,24},{9,... | collective-permute-start | bytes 3244040 | tf_op jit(solution)/shard_map/ppermute | solution.py:39
  82.7 31.4 %collective-permute-start.23 = (bf16[2,192,1408]{2,1,0:T(8,128)(2,1)S(1)}, bf16[2,192,1408]{2,1,0:T(8,128)(2,1)S(1)}, u32[]{:S(2)}, u32[]{:S(2)}) collective-permute-start(bf16[2,192,1408]{2,1,0:T(8,128)(2,1)S(1)} %pad_maximum_fusion.1.u2), channel_id=1, source_target_pairs={{0,8},{1,9},{2,10},{3,11},{4,12},{5,13},{6,14},{7,15},{8,0},{9,1},... | collective-permute-start | bytes 3244040 | tf_op jit(solution)/shard_map/ppermute | solution.py:39
  152.3 26.9 %collective-permute-start.42 = (bf16[2,192,1408]{2,1,0:T(8,128)(2,1)}, bf16[2,192,1408]{2,1,0:T(8,128)(2,1)S(1)}, u32[]{:S(2)}, u32[]{:S(2)}) collective-permute-start(bf16[2,192,1408]{2,1,0:T(8,128)(2,1)} %get-tuple-element.216), channel_id=1, source_target_pairs={{0,8},{1,9},{2,10},{3,11},{4,12},{5,13},{6,14},{7,15},{8,0},{9,1},... | collective-permute-start | bytes 3244040 | tf_op jit(solution)/shard_map/ppermute | solution.py:39
  153.9 25.9 %collective-permute-start.41 = (bf16[2,192,1408]{2,1,0:T(8,128)(2,1)}, bf16[2,192,1408]{2,1,0:T(8,128)(2,1)}, u32[]{:S(2)}, u32[]{:S(2)}) collective-permute-start(bf16[2,192,1408]{2,1,0:T(8,128)(2,1)} %get-tuple-element.163), channel_id=1, source_target_pairs={{0,16},{1,17},{2,18},{3,19},{4,20},{5,21},{6,22},{7,23},{8,24},{9,... | collective-permute-start | bytes 3244040 | tf_op jit(solution)/shard_map/ppermute | solution.py:39
  177.2 33.1 %collective-permute-start.35 = (bf16[2,168,896]{2,1,0:T(8,128)(2,1)S(1)}, bf16[2,168,896]{2,1,0:T(8,128)(2,1)S(1)}, u32[]{:S(2)}, u32[]{:S(2)}) collective-permute-start(bf16[2,168,896]{2,1,0:T(8,128)(2,1)S(1)} %get-tuple-element.197), channel_id=1, source_target_pairs={{0,8},{1,9},{2,10},{3,11},{4,12},{5,13},{6,14},{7,15},{8,0},{9,1},... | collective-permute-start | bytes 1806344 | tf_op jit(solution)/shard_map/ppermute | solution.py:39
  178.7 31.6 %collective-permute-start.34 = (bf16[2,168,896]{2,1,0:T(8,128)(2,1)S(1)}, bf16[2,168,896]{2,1,0:T(8,128)(2,1)S(1)}, u32[]{:S(2)}, u32[]{:S(2)}) collective-permute-start(bf16[2,168,896]{2,1,0:T(8,128)(2,1)S(1)} %get-tuple-element.195), channel_id=1, source_target_pairs={{0,16},{1,17},{2,18},{3,19},{4,20},{5,21},{6,22},{7,23},{8,24},{9,... | collective-permute-start | bytes 1806344 | tf_op jit(solution)/shard_map/ppermute | solution.py:39
  181.6 23.6 %collective-permute-start.44 = (bf16[192,1408]{1,0:T(8,128)(2,1)S(1)}, bf16[192,1408]{1,0:T(8,128)(2,1)S(1)}, u32[]{:S(2)}, u32[]{:S(2)}) collective-permute-start(bf16[192,1408]{1,0:T(8,128)(2,1)S(1)} %get-tuple-element.224), channel_id=1, source_target_pairs={{0,16},{1,17},{2,18},{3,19},{4,20},{5,21},{6,22},{7,23},{8,24},{9,... | collective-permute-start | bytes 1622024 | tf_op jit(solution)/shard_map/ppermute | solution.py:39
  182.6 26.8 %collective-permute-start.32 = (bf16[128,1536]{1,0:T(8,128)(2,1)S(1)}, bf16[128,1536]{1,0:T(8,128)(2,1)S(1)}, u32[]{:S(2)}, u32[]{:S(2)}) collective-permute-start(bf16[128,1536]{1,0:T(8,128)(2,1)S(1)} %get-tuple-element.183), channel_id=1, source_target_pairs={{0,2},{1,3},{2,0},{3,1},{4,6},{5,7},{6,4},{7,5},{8,10},{9,11},{10,... | collective-permute-start | bytes 1179656 | tf_op jit(solution)/shard_map/ppermute | solution.py:39
  205.3 39.2 %collective-permute-start.45 = (bf16[192,1408]{1,0:T(8,128)(2,1)S(1)}, bf16[192,1408]{1,0:T(8,128)(2,1)S(1)}, u32[]{:S(2)}, u32[]{:S(2)}) collective-permute-start(bf16[192,1408]{1,0:T(8,128)(2,1)S(1)} %shard_map.262), channel_id=1, source_target_pairs={{0,4},{1,5},{2,6},{3,7},{4,0},{5,1},{6,2},{7,3},{8,12},{9,13},{10,... | collective-permute-start | bytes 1622024 | tf_op jit(solution)/shard_map/ppermute | solution.py:39
  208.9 35.6 %collective-permute-start.43 = (bf16[192,1408]{1,0:T(8,128)(2,1)S(1)}, bf16[192,1408]{1,0:T(8,128)(2,1)S(1)}, u32[]{:S(2)}, u32[]{:S(2)}) collective-permute-start(bf16[192,1408]{1,0:T(8,128)(2,1)S(1)} %get-tuple-element.222), channel_id=1, source_target_pairs={{0,8},{1,9},{2,10},{3,11},{4,12},{5,13},{6,14},{7,15},{8,0},{9,1},... | collective-permute-start | bytes 1622024 | tf_op jit(solution)/shard_map/ppermute | solution.py:39
  217.8 37.8 %collective-permute-start.38 = (bf16[168,896]{1,0:T(8,128)(2,1)S(1)}, bf16[168,896]{1,0:T(8,128)(2,1)S(1)}, u32[]{:S(2)}, u32[]{:S(2)}) collective-permute-start(bf16[168,896]{1,0:T(8,128)(2,1)S(1)} %shard_map.258), channel_id=1, source_target_pairs={{0,4},{1,5},{2,6},{3,7},{4,0},{5,1},{6,2},{7,3},{8,12},{9,13},{10,... | collective-permute-start | bytes 903176 | tf_op jit(solution)/shard_map/ppermute | solution.py:39
  218.2 37.4 %collective-permute-start.36 = (bf16[168,896]{1,0:T(8,128)(2,1)S(1)}, bf16[168,896]{1,0:T(8,128)(2,1)S(1)}, u32[]{:S(2)}, u32[]{:S(2)}) collective-permute-start(bf16[168,896]{1,0:T(8,128)(2,1)S(1)} %get-tuple-element.203), channel_id=1, source_target_pairs={{0,8},{1,9},{2,10},{3,11},{4,12},{5,13},{6,14},{7,15},{8,0},{9,1},... | collective-permute-start | bytes 903176 | tf_op jit(solution)/shard_map/ppermute | solution.py:39
  219.7 36.0 %collective-permute-start.33 = (bf16[64,2048]{1,0:T(8,128)(2,1)S(1)}, bf16[64,2048]{1,0:T(8,128)(2,1)S(1)}, u32[]{:S(2)}, u32[]{:S(2)}) collective-permute-start(bf16[64,2048]{1,0:T(8,128)(2,1)S(1)} %get-tuple-element.186), channel_id=1, source_target_pairs={{0,4},{1,5},{2,6},{3,7},{4,0},{5,1},{6,2},{7,3},{8,12},{9,13},{10,... | collective-permute-start | bytes 786440 | tf_op jit(solution)/shard_map/ppermute | solution.py:39
  (51 other events, 333.8 us)

commit v4 on v3

--- a/solution.py
+++ b/solution.py
@@ -378,6 +378,20 @@
         to[j % 2] = nat[t ^ j].astype(BF16)
     started[2].wait()
     down[...] = tiles_in(whole[...].astype(F32)).astype(BF16)
+
+
+def pack_block(kept, first, last, tail, out, sem):
+    width = ROWS
+    parts = (kept.at[0], first.at[0], last.at[0], last.at[1], tail)
+    started = fetch([(part, out.at[i * width:i * width + part.shape[0]]) for i, part in enumerate(parts)], sem)
+    for copy in started:
+        copy.wait()
+
+
+def pack_pair(kept, first, out, sem):
+    started = fetch([(kept.at[1], out.at[0]), (first.at[1], out.at[1])], sem)
+    for copy in started:
+        copy.wait()
 
 
 def pack_out(b0, b1, b2, b3, out, raw, sem):
@@ -750,13 +764,36 @@
     def after_these(array, *others):
         return lax.optimization_barrier((array,) + others)[0]
 
+    def fenced(part, *inputs):
+        results = jax.eval_shape(part, *inputs)
+        nothing = lambda *_: jax.tree.map(lambda a: jnp.zeros(a.shape, a.dtype), results)
+        return lax.cond(ids[0] >= 0, part, nothing, *inputs)
+
     def spread(own, other, *first):
         a_pair = jnp.stack([own, to_x(own)])
         b_pair = jnp.stack([other, to_y(other)])
         a_pair, b_pair = lax.optimization_barrier((a_pair, b_pair) + first)[:2]
         return a_pair, to_y(a_pair), b_pair, to_x(b_pair)
 
-    starts = pick(seq_starts, h)
+    def pair_of(kept, first):
+        return call(pack_pair, shape(kept.shape), [ANY] * 2, (kept, first), [pltpu.SemaphoreType.DMA((2,))])
+
+    def block_of(kept, first, last, tail):
+        return call(pack_block, shape((4 * ROWS + tail.shape[0], tail.shape[1])), [ANY] * 4, (kept, first, last, tail),
+                    [pltpu.SemaphoreType.DMA((5,))])
+
+    q_send, q_keep, o_block, xv_send, c_send = call(
+        pack_first, (shape((2, ROWS, WQ)), shape((2, ROWS, WQ)), shape((40, WQ)), shape((L, 2 * D)), shape((L, D))),
+        [SMEM] + [VMEM] * 2 + [ANY] * 7,
+        (ids, norm1_gain[None], norm2_gain[None], w_query, w_key, w_value, w_out, layer_in, first_layer_value, cotangent),
+        [pltpu.VMEM((8, ROWS), F32), pltpu.VMEM((ROWS, D), BF16), pltpu.SemaphoreType.DMA((16,))], mib=63)
+    q_first = to_z(q_send)
+    xv_moved = to_h(xv_send)
+    q_last = to_core(pair_of(q_keep, q_first))
+    q_block = block_of(q_keep, q_first, q_last, o_block)
+    q_other = to_h(q_block)
+
+    starts = pick(after_these(seq_starts, q_block), h)
     member = t ^ jnp.array(ORDER, jnp.int32)
     half = h ^ jnp.arange(2, dtype=jnp.int32)
     position = ((half[None, :] * 4 + member[:, None]) * L)[:, :, None] + jnp.arange(L, dtype=jnp.int32)
@@ -764,22 +801,12 @@
     begin = jnp.max(jnp.where(starts[None, :] <= position[:, None], starts[None, :], 0), axis=1)
     visible = (begin[:, None] == begin[None, :]) & (position[None, :] <= position[:, None])
     bias = jnp.where(visible, 0.0, NEG).astype(F32)
-    frequency = 10000.0 ** (-(jnp.arange(HD // 2, dtype=F32) * 2.0 / HD))
+    lane = jnp.arange(HT, dtype=jnp.int32)
+    frequency = 10000.0 ** (-((lane % (HD // 2)).astype(F32) * 2.0 / HD))
     angles = (position - begin).astype(F32)[:, None] * frequency[None, :]
-    cosine, sine = jnp.cos(angles), jnp.sin(angles)
-    cs = jnp.tile(jnp.concatenate([cosine, cosine], axis=1), (1, 4))
-    sn = jnp.tile(jnp.concatenate([-sine, sine], axis=1), (1, 4))
-
-    q_send, q_keep, o_block, xv_send, c_send = call(
-        pack_first, (shape((2, ROWS, WQ)), shape((2, ROWS, WQ)), shape((40, WQ)), shape((L, 2 * D)), shape((L, D))),
-        [SMEM] + [VMEM] * 2 + [ANY] * 7,
-        (ids, norm1_gain[None], norm2_gain[None], w_query, w_key, w_value, w_out, layer_in, first_layer_value, cotangent),
-        [pltpu.VMEM((8, ROWS), F32), pltpu.VMEM((ROWS, D), BF16), pltpu.SemaphoreType.DMA((16,))], mib=63)
-    q_first = to_z(q_send)
-    xv_moved = to_h(xv_send)
-    q_last = to_core(jnp.stack([q_keep[1], q_first[1]]))
-    q_block = jnp.concatenate([q_keep[0], q_first[0], q_last[0], q_last[1], o_block], axis=0)
-    q_other = to_h(q_block)
+    cs = jnp.cos(angles)
+    sn = jnp.sin(angles) * jnp.where(lane % HD < HD // 2, -1.0, 1.0)[None, :]
+
     xv_out, v_keep = call(pack_second, (shape((M, D + 2 * HT)), shape((2, M, HT))), [SMEM] + [ANY] * 3,
                           (ids, layer_in, first_layer_value, xv_moved), [pltpu.VMEM((M, D), BF16), pltpu.SemaphoreType.DMA((4,))], mib=63)
     x_two, v_two = call(pack_third, (shape((HALF, D + HT)), shape((HALF, HT))), [VMEM] * 3, (xv_out, to_z(xv_out), v_keep))
@@ -792,27 +819,28 @@
         (after_these(ids, q_send), w_gate, w_up, w_down),
         [pltpu.VMEM((4, ROWS, 2 * FT), F32), pltpu.VMEM((ROWS, 4 * FT), BF16), pltpu.VMEM((ROWS, 4 * FT), BF16), pltpu.VMEM((FROWS, D), BF16),
          pltpu.SemaphoreType.DMA((3,))], mib=63)
-    u_first = to_z(after_these(u_send, q_first))
-    u_last = to_core(jnp.stack([u_keep[1], u_first[1]]))
-    u_block = jnp.concatenate([u_keep[0], u_first[0], u_last[0], u_last[1], d_block], axis=0)
-    u_other = to_h(after_these(u_block, q_other))
+    u_first = to_z(u_send)
+    u_last = to_core(pair_of(u_keep, after_these(u_first, q_block)))
+    u_block = block_of(u_keep, u_first, u_last, d_block)
+    u_other = to_h(after_these(u_block, q_block))
     c_moved = to_h(after_these(c_send, u_other))
     u_a = jnp.stack([u_block, to_x(after_these(u_block, q_parts[2]))])
     u_b = jnp.stack([u_other, to_y(u_other)])
     o_own = call(pack_out, shape((HT, D)), [ANY] * 4, q_parts, [pltpu.VMEM((8, 40, WQ), BF16), pltpu.SemaphoreType.DMA((8,))])
     o_first = to_z(o_own)
-    q_parts = lax.optimization_barrier(q_parts + (u_a, u_b))[:4]
+    c_own = jnp.concatenate([pick(cotangent, h), after_these(c_moved, o_own)], axis=0)
+    q_parts = lax.optimization_barrier(q_parts + (u_a, u_b, c_own))[:4]
+    c_two = jnp.concatenate([c_own, to_z(c_own)], axis=0)
+    c_core = to_core(c_two)
     qkv_w, normed_one, qkv, attn, attn_low, lse, gains = call(
         attend_kernel,
         (shape((D, WQ)), shape((N, D)), shape((N, 3 * HT)), shape((N, HT), F32), shape((N, HT)), shape((N, 4), F32), shape((8, D), F32)),
         [SMEM] + [VMEM] * 6 + [ANY] * 4, (ids, x_two, x_core, v_two, cs, sn, bias, *q_parts),
         [pltpu.SemaphoreType.DMA((32,))])
-    a_two = jnp.concatenate([attn_low, to_z(attn_low)], axis=0)
-    c_own = jnp.concatenate([pick(cotangent, h), after_these(c_moved, attn_low)], axis=0)
+    a_two = jnp.concatenate([attn_low, to_z(after_these(attn_low, c_two))], axis=0)
+    a_core = to_core(after_these(a_two, c_core))
     o_two = jnp.concatenate([o_own, o_first], axis=0)
     o_core = to_core(after_these(o_two, attn_low))
-    c_two = jnp.concatenate([c_own, to_z(after_these(c_own, a_two))], axis=0)
-    c_core = to_core(c_two)
     u_parts = (u_a, to_y(u_a), u_b, to_x(u_b))
     a_core = to_core(a_two)
     attn_full, after, normed_two, out_w = call(
@@ -827,31 +855,45 @@
         [pltpu.VMEM((D, 2 * FT), BF16), pltpu.VMEM((8 * FROWS, D), BF16), pltpu.VMEM((8 * FROWS, D), F32), pltpu.VMEM((8, 2 * ROWS, 2 * FT), BF16),
          pltpu.SemaphoreType.DMA((32,)), pltpu.SemaphoreType.DMA((8,))])
 
-    kept, sent = call(fold_kernel, (shape((M, D), F32), shape((M, D))), [VMEM] * 2, (r_keep, to_core(r_send)))
+    r_core = to_core(r_send)
     block = (2, 6 * ROWS, 2 * FT)
     a_keep, a_send, b_keep, b_send = call(
         feed_weights_kernel, (shape(block),) * 4, [SMEM] + [VMEM] * 4, (ids, normed_two, dgu, hidden, c_all),
         [pltpu.VMEM((HT, 2 * FT), F32), pltpu.VMEM((8 * FROWS, D), F32)])
-    kept = after_these(kept, a_send)
-    grad_after, branch = call(branch_kernel, (shape((M, D), F32), shape((M, D))), [VMEM] * 5,
-                              (kept, to_z(sent), after, gains, c_two))
-    b_two = jnp.concatenate([branch, to_z(branch)], axis=0)
-    b_core = to_core(b_two)
-
     u_sums = (a_keep, to_y(a_send), b_keep, to_x(b_send))
+
+    def middle(r_keep, r_core, after, gains, c_two):
+        kept, sent = call(fold_kernel, (shape((M, D), F32), shape((M, D))), [VMEM] * 2, (r_keep, r_core))
+        grad_after, branch = call(branch_kernel, (shape((M, D), F32), shape((M, D))), [VMEM] * 5, (kept, to_z(sent), after, gains, c_two))
+        b_two = jnp.concatenate([branch, to_z(branch)], axis=0)
+        return grad_after, b_two, to_core(b_two)
+
+    grad_after, b_two, b_core = fenced(middle, r_keep, after_these(r_core, a_send), after, gains, c_two)
+
+    def second_sum(a_own, a_send, b_own, b_send):
+        return a_own, a_send, call(sum_second_kernel, shape(b_own.shape), [VMEM] * 2, (b_own, to_y(b_send)))
+
+    def first_sum(sums):
+        return call(sum_first_kernel, (shape(sums[0].shape[1:]),) * 4, [VMEM] * 4, sums)
+
+    u_sums = first_sum(lax.optimization_barrier(u_sums + (b_core,))[:4])
+    b_core = after_these(b_core, u_sums[3])
+    def attend_back(*inputs):
+        return tuple(call(
+            attend_back_kernel,
+            (shape((N, 3 * HT)), shape((HALF, D), F32), shape((HALF, D + HT)), shape((1, D), F32)),
+            [SMEM] + [VMEM] * 12, (ids,) + inputs,
+            [pltpu.VMEM((N, HT), BF16), pltpu.VMEM((N, HT), F32), pltpu.VMEM((N, HT), F32)], mib=60))
+
+    dqkv, r_keep, r_send, gain_one_g = fenced(attend_back, b_two, b_core, out_w, qkv, attn, lse, bias, cs, sn, qkv_w, x_two, x_core)
+    u_sums = second_sum(*u_sums)
+    r_send = after_these(r_send, u_sums[2])
     o_kept, o_sent = call(fold_kernel, (shape((M, D), F32), shape((M, D))), [VMEM] * 2,
                           (out_keep, to_core(after_these(out_send, b_two))))
     y_own, y_send = call(result_kernel, (shape((L, D)), shape((L, D))), [VMEM] * 3, (o_kept, to_z(o_sent), after))
     layer_out = call(result_home_kernel, shape((2, L, D)), [SMEM] + [VMEM] * 2, (ids, y_own, to_h(y_send)))
-
-    b_core = after_these(b_core, o_sent)
-    dqkv, r_keep, r_send, gain_one_g = call(
-        attend_back_kernel,
-        (shape((N, 3 * HT)), shape((HALF, D), F32), shape((HALF, D + HT)), shape((1, D), F32)),
-        [SMEM] + [VMEM] * 12, (ids, b_two, b_core, out_w, qkv, attn, lse, bias, cs, sn, qkv_w, x_two, x_core),
-        [pltpu.VMEM((N, HT), BF16), pltpu.VMEM((N, HT), F32), pltpu.VMEM((N, HT), F32)])
     dv_keep = dqkv[:HALF, 2 * HT:]
-    r_core = after_these(to_core(r_send), y_send)
+    r_core = to_core(r_send)
     kept, sent = call(fold_both_kernel, (shape((M, D), F32), shape((M, D + 2 * HT))), [VMEM] * 3, (r_keep, dv_keep, r_core))
     block = (2, 4 * ROWS + 40, WQ)
     a_keep, a_send, b_keep, b_send = call(
@@ -865,20 +907,18 @@
     input_grad, v1_out = call(home_kernel, (shape((2, L, D), F32),) * 2, [SMEM] + [VMEM] * 3, (ids, own, home, v1_acc))
 
     def finish(kernel, sums, rest, *first):
-        dims = sums[0].shape[1:]
-        a_own, a_send, b_own, b_send = call(sum_first_kernel, (shape(dims),) * 4, [VMEM] * 4, sums)
-        b_send = call(sum_second_kernel, shape(dims), [VMEM] * 2, (b_own, to_y(b_send)))
+        a_own, a_send, b_send = sums
+        dims = a_own.shape
         kept, sent, rows = call(kernel, (shape((2, ROWS, dims[1])), shape((2, ROWS, dims[1])), shape(rest, F32)), [SMEM] + [VMEM] * 3,
                                 (ids, a_own, to_x(a_send), after_these(to_h(b_send), *first)), [pltpu.VMEM(dims, F32)])
         first = to_z(sent)
-        return (ids, kept, first, to_core(jnp.stack([kept[1], first[1]]))), rows
-
-    u_sums = lax.optimization_barrier(u_sums + (a_send,))[:4]
-    q_sums = lax.optimization_barrier(q_sums + (sent,))[:4]
+        return (ids, kept, first, to_core(pair_of(kept, first))), rows
+
+    q_sums = second_sum(*first_sum(lax.optimization_barrier(q_sums + (sent,))[:4]))
     parts, down_g = finish(sum_hidden_kernel, u_sums, (FROWS, D))
     gate_g, up_g = call(join_hidden_kernel, (shape((ROWS, 4 * FT), F32),) * 2, [SMEM] + [VMEM] * 3, parts,
                         [pltpu.VMEM((4, ROWS, 2 * FT), F32)])
-    parts, out_g = finish(sum_qkv_kernel, q_sums, (ROWS, D), home)
+    parts, out_g = finish(sum_qkv_kernel, q_sums, (ROWS, D), home, gate_g)
     query_g, key_g, value_g, gain_g = call(
         join_qkv_kernel, (shape((ROWS, D), F32),) * 3 + (shape((ROWS, 128), F32),), [SMEM] + [VMEM] * 3, parts)
     return (layer_out, input_grad, v1_out, gain_g[:, 0], query_g, key_g, value_g, out_g, gain_g[:, 1], gate_g, up_g, down_g)

time: 275 us -> 252 us (0.916)
  local copies, waits for them, and re-layouts: 24.5 us -> 9.18 us
  waiting for transfers between devices: 131 us -> 116 us
  Pallas kernels: 68.5 us -> 80.5 us
  starting transfers between devices: 42.3 us -> 39.1 us
    ppermute x48, waiting for transfers between devices: 131 us -> 116 us  [send(): return lax.ppermute(array, ALL, pairs)]
    pallas_call x27 -> x33, Pallas kernels: 68.5 us -> 80.5 us  [call(): pl.pallas_call(kernel, out_shape=outs, in_specs=specs, out_specs=jax.tree...]
    unnamed x64 -> x77, local copies, waits for them, and re-layouts: 15.3 us -> 5.97 us
    optimization_barrier x2 -> x0, local copies, waits for them, and re-layouts: 3.31 us -> none  [fast(): lax.optimization_barrier((q_other, cs, sn, bias, xv_out))]
    ppermute x48, starting transfers between devices: 42.3 us -> 39.1 us  [send(): return lax.ppermute(array, ALL, pairs)]
  transfers between devices with their start and end apart: 48 -> 48, of which waited for: 20 -> 21; matrix products, arithmetic and copies ran while one was open for 7% -> 3% of each run, Pallas kernels for 18% -> 20%
where the time goes in v4:
time: 252 us
  waiting for transfers between devices  116 us (46%)
  Pallas kernels  80.5 us (32%)
  starting transfers between devices  39.1 us (16%)
  local copies, waits for them, and re-layouts  9.18 us (4%)
  other arithmetic  6.12 us (2%)
    ppermute x48, waiting for transfers between devices, send(): return lax.ppermute(array, ALL, pairs)  116 us
    pallas_call x33, Pallas kernels, call(): pl.pallas_call(kernel, out_shape=outs, in_specs=specs, out_specs=jax.tree...  80.5 us
    ppermute x48, starting transfers between devices, send(): return lax.ppermute(array, ALL, pairs)  39.1 us
    unnamed x77, local copies, waits for them, and re-layouts  5.97 us
  transfers between devices with their start and end apart: 48, of which 21 were waited for; matrix products, arithmetic and copies ran while one was open for 3% of the time, Pallas kernels for 20%

profile of v4, /device:TPU:0, one launch (start us, length us, event | category | flops | bytes accessed | tf_op | source)
XLA Modules:
  0.0 251.8 jit_solution(753358269667315083)
XLA Ops:
  0.8 2.9 %shard_map.238 = (bf16[2,32,896]{2,1,0:T(8,128)(2,1)}, bf16[2,32,896]{2,1,0:T(8,128)(2,1)}, bf16[40,896]{1,0:T(8,128)(2,1)}, bf16[64,2048]{1,0:T(8,128)(2,1)}, bf16[64,1024]{1,0:T(8,128)(2,1)}) custom-call(s32[3]{0:T(128)S(1)} %pad_add_fusion.ids, bf16[1,32]{1,0:T(2,128)(2,1)} %bitcast.23, bf16[1,32]{1,0:T(2,128)(2,1)} %bitcast.24, bf16[32,1024]{1,0:T(8,128)(2,1)} %wq.1, ...), custom_call_target="tpu_custom_call" | custom-call | flops 1 | bytes 1 | tf_op jit(solution)/shard_map/pallas_call | solution.py:305
  3.7 3.1 %collective-permute-start.6 = (bf16[2,32,896]{2,1,0:T(8,128)(2,1)}, bf16[2,32,896]{2,1,0:T(8,128)(2,1)S(1)}, u32[]{:S(2)}, u32[]{:S(2)}) collective-permute-start(bf16[2,32,896]{2,1,0:T(8,128)(2,1)} %get-tuple-element.195), channel_id=1, source_target_pairs={{0,2},{1,3},{2,0},{3,1},{4,6},{5,7},{6,4},{7,5},{8,10},{9,11},{10,... | collective-permute-start | bytes 344072 | tf_op jit(solution)/shard_map/ppermute | solution.py:39
  9.4 2.7 %shard_map.243 = (bf16[2,32,1408]{2,1,0:T(8,128)(2,1)}, bf16[2,32,1408]{2,1,0:T(8,128)(2,1)}, bf16[64,1408]{1,0:T(8,128)(2,1)}) custom-call(s32[3]{0:T(128)S(1)} %pad_add_fusion.ids, bf16[32,2816]{1,0:T(8,128)(2,1)} %wg.1, bf16[32,2816]{1,0:T(8,128)(2,1)} %wu.1, bf16[88,1024]{1,0:T(8,128)(2,1)} %wd.1), custom_call_target="tpu_custom_call" | custom-call | flops 1 | bytes 1 | tf_op jit(solution)/shard_map/pallas_call | solution.py:305
  29.4 5.9 %collective-permute-done.8 = bf16[168,896]{1,0:T(8,128)(2,1)} collective-permute-done((bf16[168,896]{1,0:T(8,128)(2,1)S(1)}, bf16[168,896]{1,0:T(8,128)(2,1)}, u32[]{:S(2)}, u32[]{:S(2)}) %collective-permute-start.8) | collective-permute-done | bytes 301088 | tf_op jit(solution)/shard_map/ppermute | solution.py:39
  39.2 4.3 %collective-permute-done.4.moved = bf16[128,1536]{1,0:T(8,128)(2,1)S(1)} collective-permute-done((bf16[128,1536]{1,0:T(8,128)(2,1)}, bf16[128,1536]{1,0:T(8,128)(2,1)S(1)}, u32[]{:S(2)}, u32[]{:S(2)}) %collective-permute-start.4) | collective-permute-done | bytes 393248 | tf_op jit(solution)/shard_map/ppermute | solution.py:39
  48.5 15.0 %collective-permute-done.16 = bf16[192,1408]{1,0:T(8,128)(2,1)S(1)} collective-permute-done((bf16[192,1408]{1,0:T(8,128)(2,1)S(1)}, bf16[192,1408]{1,0:T(8,128)(2,1)S(1)}, u32[]{:S(2)}, u32[]{:S(2)}) %collective-permute-start.16) | collective-permute-done | bytes 540704 | tf_op jit(solution)/shard_map/ppermute | solution.py:39
  67.3 5.9 %collective-permute-done.15 = bf16[192,1408]{1,0:T(8,128)(2,1)S(1)} collective-permute-done((bf16[192,1408]{1,0:T(8,128)(2,1)S(1)}, bf16[192,1408]{1,0:T(8,128)(2,1)S(1)}, u32[]{:S(2)}, u32[]{:S(2)}) %collective-permute-start.15) | collective-permute-done | bytes 540704 | tf_op jit(solution)/shard_map/ppermute | solution.py:39
  73.9 4.7 %collective-permute-done.17 = bf16[192,1408]{1,0:T(8,128)(2,1)S(1)} collective-permute-done((bf16[192,1408]{1,0:T(8,128)(2,1)S(1)}, bf16[192,1408]{1,0:T(8,128)(2,1)S(1)}, u32[]{:S(2)}, u32[]{:S(2)}) %collective-permute-start.17) | collective-permute-done | bytes 540704 | tf_op jit(solution)/shard_map/ppermute | solution.py:39
  79.9 9.6 %shard_map.247 = (bf16[1024,896]{1,0:T(8,128)(2,1)}, bf16[512,1024]{1,0:T(8,128)(2,1)S(1)}, bf16[512,768]{1,0:T(8,128)(2,1)}, f32[512,256]{1,0:T(8,128)}, bf16[5...) custom-call(s32[3]{0:T(128)S(1)} %pad_add_fusion.ids, ...), custom_call_target="tpu_custom_call" | custom-call | flops 1 | bytes 1 | tf_op jit(solution)/shard_map/pallas_call | solution.py:305
  90.6 8.0 %collective-permute-done.20 = bf16[512,256]{1,0:T(8,128)(2,1)S(1)} collective-permute-done((bf16[512,256]{1,0:T(8,128)(2,1)S(1)}, bf16[512,256]{1,0:T(8,128)(2,1)S(1)}, u32[]{:S(2)}, u32[]{:S(2)}) %collective-permute-start.20) | collective-permute-done | bytes 262176 | tf_op jit(solution)/shard_map/ppermute | solution.py:39
  100.6 6.4 %shard_map.248 = (bf16[512,1024]{1,0:T(8,128)(2,1)S(1)}, f32[512,1024]{1,0:T(8,128)S(1)}, bf16[512,1024]{1,0:T(8,128)(2,1)S(1)}, bf16[256,1024]{1,0:T(8,128)(2,1)}) custom-call(s32[3]{0:T(128)S(1)} %pad_add_fusion.ids, bf16[256,1280]{1,0:T(8,128)(2,1)S(1)} %get-tuple-element.192.x2, bf16[256,1280]{1,0:T(8,128)(2,1)S(1)} %collective-permute-done.5.xc, ...), custom_call_target="tpu_custom_call" | custom-call | flops 1 | bytes 1 | tf_op jit(solution)/shard_map/pallas_call | solution.py:305
  108.0 14.4 %shard_map.249 = (bf16[512,704]{1,0:T(8,128)(2,1)S(1)}, bf16[512,1408]{1,0:T(8,128)(2,1)S(1)}, f32[256,1024]{1,0:T(8,128)S(1)}, bf16[256,1024]{1,0:T(8,128)(2,1)...) custom-call(s32[3]{0:T(128)S(1)} %pad_add_fusion.ids, ...), custom_call_target="tpu_custom_call" | custom-call | flops 1 | bytes 1 | tf_op jit(solution)/shard_map/pallas_call | solution.py:305
  122.5 4.8 %shard_map.250 = (bf16[2,192,1408]{2,1,0:T(8,128)(2,1)S(1)}, bf16[2,192,1408]{2,1,0:T(8,128)(2,1)}, bf16[2,192,1408]{2,1,0:T(8,128)(2,1)S(1)}, bf16[2,192,1408]{2,1,0:T(8,128)(2,1)}) custom-call(s32[3]{0:T(128)S(1)} %pad_add_fusion.ids, bf16[512,1024]{1,0:T(8,128)(2,1)S(1)} %get-tuple-element.222.normed, bf16[512,1408]{1,0:T(8,128)(2,1)S(1)} %get-tuple-element.228.dgu, ...), custom_call_target="tpu_custom_call" | custom-call | flops 1 | bytes 1 | tf_op jit(solution)/shard_map/pallas_call | solution.py:305
  131.1 23.2 %conditional.2 = (f32[128,1024]{1,0:T(8,128)}, bf16[256,1024]{1,0:T(8,128)(2,1)}, bf16[256,1024]{1,0:T(8,128)(2,1)}) conditional(s32[]{:T(128)} %convert_element_type.20, () %tuple.58, (f32[256,1024]{1,0:T(8,128)}, bf16[256,1024]{1,0:T(8,128)(2,1)}, f32[512,1024]{1,0:T(8,128)}, f32[8,1024]{1,0:T(8,128)S(1)}, bf16[256,1024]{1,0:T(8,128)(2,1)}) %tuple.83), branch_computations={%region_1.2_spmd, %region_2.3_spmd} | conditional | flops 2 | bytes 7340206 | solution.py:770
  132.9 8.1 %collective-permute-done.moved = bf16[128,1024]{1,0:T(8,128)(2,1)S(1)} collective-permute-done((bf16[128,1024]{1,0:T(8,128)(2,1)S(1)}, bf16[128,1024]{1,0:T(8,128)(2,1)S(1)}, u32[]{:S(2)}, u32[]{:S(2)}) %collective-permute-start) | collective-permute-done | bytes 262176 | tf_op jit(solution)/shard_map/cond/branch_1_fun/ppermute | solution.py:39
  141.0 2.7 %branch_1_fun.4 = (f32[128,1024]{1,0:T(8,128)}, bf16[128,1024]{1,0:T(8,128)(2,1)S(1)}) custom-call(f32[128,1024]{1,0:T(8,128)S(1)} %get-tuple-element.43.keep, bf16[128,1024]{1,0:T(8,128)(2,1)S(1)} %collective-permute-done.moved, f32[512,1024]{1,0:T(8,128)} %get-tuple-element.45.after, f32[8,1024]{1,0:T(8,128)S(1)} %get-tuple-element.46.gains, ...), custom_call_target="tpu_custom_call" | custom-call | flops 1 | bytes 1 | tf_op jit(solution)/shard_map/cond/branch_1_fun/pallas_call | solution.py:305
  144.7 6.6 %collective-permute-done.1 = bf16[128,1024]{1,0:T(8,128)(2,1)S(1)} collective-permute-done((bf16[128,1024]{1,0:T(8,128)(2,1)S(1)}, bf16[128,1024]{1,0:T(8,128)(2,1)S(1)}, u32[]{:S(2)}, u32[]{:S(2)}) %collective-permute-start.1) | collective-permute-done | bytes 262176 | tf_op jit(solution)/shard_map/cond/branch_1_fun/ppermute | solution.py:39
  158.1 13.2 %conditional.3 = (bf16[512,768]{1,0:T(8,128)(2,1)}, f32[256,1024]{1,0:T(8,128)S(1)}, bf16[256,1280]{1,0:T(8,128)(2,1)S(1)}, f32[1,1024]{1,0:T(1,128)S(1)}, bf16[256,256]{1,0:T(8,128)(2,1)S(1)}) conditional(s32[]{:T(128)} %convert_element_type.20, () %tuple.62, (s32[3]{0:T(128)S(1)}, bf16[256,1024]{1,0:T(8,128)(2,1)}, bf16[256,1024]{1,0:T(8,128)(2,1)}, ...), branch_computations={%region_3.4_spmd, %region_4.5_spmd} | conditional | flops 1 | bytes 2625590 | solution.py:770
  158.1 12.2 %branch_1_fun.5 = (bf16[512,768]{1,0:T(8,128)(2,1)}, f32[256,1024]{1,0:T(8,128)S(1)}, bf16[256,1280]{1,0:T(8,128)(2,1)S(1)}, f32[1,1024]{1,0:T(1,128)S(1)}) custom-call(s32[3]{0:T(128)S(1)} %get-tuple-element.50.ids, bf16[256,1024]{1,0:T(8,128)(2,1)} %get-tuple-element.51.da2, bf16[256,1024]{1,0:T(8,128)(2,1)} %get-tuple-element.52.dac, ...), custom_call_target="tpu_custom_call" | custom-call | flops 1 | bytes 1 | tf_op jit(solution)/shard_map/cond/branch_1_fun/pallas_call | solution.py:305
  174.8 3.9 %shard_map.259 = (bf16[2,168,896]{2,1,0:T(8,128)(2,1)S(1)}, bf16[2,168,896]{2,1,0:T(8,128)(2,1)S(1)}, bf16[2,168,896]{2,1,0:T(8,128)(2,1)S(1)}, bf16[2,168,896]{2,1,0:T(8,128)(2,1)S(1)}) custom-call(s32[3]{0:T(128)S(1)} %pad_add_fusion.ids, bf16[512,1024]{1,0:T(8,128)(2,1)S(1)} %copy-done.5, bf16[512,768]{1,0:T(8,128)(2,1)} %get-tuple-element.268.dqkv, ...), custom_call_target="tpu_custom_call" | custom-call | flops 1 | bytes 1 | tf_op jit(solution)/shard_map/pallas_call | solution.py:305
  183.8 14.8 %collective-permute-done.35.moved = bf16[128,1536]{1,0:T(8,128)(2,1)S(1)} collective-permute-done((bf16[128,1536]{1,0:T(8,128)(2,1)S(1)}, bf16[128,1536]{1,0:T(8,128)(2,1)S(1)}, u32[]{:S(2)}, u32[]{:S(2)}) %collective-permute-start.35) | collective-permute-done | bytes 393248 | tf_op jit(solution)/shard_map/ppermute | solution.py:39
  201.0 6.4 %collective-permute-done.43.moved = bf16[192,1408]{1,0:T(8,128)(2,1)S(1)} collective-permute-done((bf16[192,1408]{1,0:T(8,128)(2,1)S(1)}, bf16[192,1408]{1,0:T(8,128)(2,1)S(1)}, u32[]{:S(2)}, u32[]{:S(2)}) %collective-permute-start.43) | collective-permute-done | bytes 540704 | tf_op jit(solution)/shard_map/ppermute | solution.py:39
  219.5 17.4 %collective-permute-done.36.moved = bf16[64,2048]{1,0:T(8,128)(2,1)S(1)} collective-permute-done((bf16[64,2048]{1,0:T(8,128)(2,1)S(1)}, bf16[64,2048]{1,0:T(8,128)(2,1)S(1)}, u32[]{:S(2)}, u32[]{:S(2)}) %collective-permute-start.36) | collective-permute-done | bytes 262176 | tf_op jit(solution)/shard_map/ppermute | solution.py:39
  240.9 3.4 %collective-permute-done.46.first = bf16[2,32,896]{2,1,0:T(8,128)(2,1)S(1)} collective-permute-done((bf16[2,32,896]{2,1,0:T(8,128)(2,1)S(1)}, bf16[2,32,896]{2,1,0:T(8,128)(2,1)S(1)}, u32[]{:S(2)}, u32[]{:S(2)}) %collective-permute-start.46) | collective-permute-done | bytes 114720 | tf_op jit(solution)/shard_map/ppermute | solution.py:39
  (211 shorter events, 87.2 us)
Async XLA Ops:
  6.8 15.8 %collective-permute-start.3 = (bf16[64,2048]{1,0:T(8,128)(2,1)}, bf16[64,2048]{1,0:T(8,128)(2,1)}, u32[]{:S(2)}, u32[]{:S(2)}) collective-permute-start(bf16[64,2048]{1,0:T(8,128)(2,1)} %get-tuple-element.189), channel_id=1, source_target_pairs={{0,4},{1,5},{2,6},{3,7},{4,0},{5,1},{6,2},{7,3},{8,12},{9,13},{10,... | collective-permute-start | bytes 786440 | tf_op jit(solution)/shard_map/ppermute | solution.py:39
  17.3 20.9 %collective-permute-start.9 = (bf16[168,896]{1,0:T(8,128)(2,1)S(1)}, bf16[168,896]{1,0:T(8,128)(2,1)}, u32[]{:S(2)}, u32[]{:S(2)}) collective-permute-start(bf16[168,896]{1,0:T(8,128)(2,1)S(1)} %shard_map.242), channel_id=1, source_target_pairs={{0,8},{1,9},{2,10},{3,11},{4,12},{5,13},{6,14},{7,15},{8,0},{9,1},... | collective-permute-start | bytes 903176 | tf_op jit(solution)/shard_map/ppermute | solution.py:39
  18.8 16.5 %collective-permute-start.8 = (bf16[168,896]{1,0:T(8,128)(2,1)S(1)}, bf16[168,896]{1,0:T(8,128)(2,1)}, u32[]{:S(2)}, u32[]{:S(2)}) collective-permute-start(bf16[168,896]{1,0:T(8,128)(2,1)S(1)} %shard_map.242), channel_id=1, source_target_pairs={{0,4},{1,5},{2,6},{3,7},{4,0},{5,1},{6,2},{7,3},{8,12},{9,13},{10,... | collective-permute-start | bytes 903176 | tf_op jit(solution)/shard_map/ppermute | solution.py:39
  25.1 18.4 %collective-permute-start.4 = (bf16[128,1536]{1,0:T(8,128)(2,1)}, bf16[128,1536]{1,0:T(8,128)(2,1)S(1)}, u32[]{:S(2)}, u32[]{:S(2)}) collective-permute-start(bf16[128,1536]{1,0:T(8,128)(2,1)} %get-tuple-element.190.mine), channel_id=1, source_target_pairs={{0,2},{1,3},{2,0},{3,1},{4,6},{5,7},{6,4},{7,5},{8,10},{9,11},{10,... | collective-permute-start | bytes 1179656 | tf_op jit(solution)/shard_map/ppermute | solution.py:39
  38.1 25.4 %collective-permute-start.16 = (bf16[192,1408]{1,0:T(8,128)(2,1)S(1)}, bf16[192,1408]{1,0:T(8,128)(2,1)S(1)}, u32[]{:S(2)}, u32[]{:S(2)}) collective-permute-start(bf16[192,1408]{1,0:T(8,128)(2,1)S(1)} %shard_map.245), channel_id=1, source_target_pairs={{0,4},{1,5},{2,6},{3,7},{4,0},{5,1},{6,2},{7,3},{8,12},{9,13},{10,... | collective-permute-start | bytes 1622024 | tf_op jit(solution)/shard_map/ppermute | solution.py:39
  44.9 19.1 %collective-permute-start.11 = (bf16[2,168,896]{2,1,0:T(8,128)(2,1)S(1)}, bf16[2,168,896]{2,1,0:T(8,128)(2,1)S(1)}, u32[]{:S(2)}, u32[]{:S(2)}) collective-permute-start(bf16[2,168,896]{2,1,0:T(8,128)(2,1)S(1)} %pad_maximum_fusion.3.b0), channel_id=1, source_target_pairs={{0,16},{1,17},{2,18},{3,19},{4,20},{5,21},{6,22},{7,23},{8,24},{9,... | collective-permute-start | bytes 1806344 | tf_op jit(solution)/shard_map/ppermute | solution.py:39
  46.4 17.7 %collective-permute-start.12 = (bf16[2,168,896]{2,1,0:T(8,128)(2,1)S(1)}, bf16[2,168,896]{2,1,0:T(8,128)(2,1)S(1)}, u32[]{:S(2)}, u32[]{:S(2)}) collective-permute-start(bf16[2,168,896]{2,1,0:T(8,128)(2,1)S(1)} %pad_maximum_fusion.4.b2), channel_id=1, source_target_pairs={{0,8},{1,9},{2,10},{3,11},{4,12},{5,13},{6,14},{7,15},{8,0},{9,1},... | collective-permute-start | bytes 1806344 | tf_op jit(solution)/shard_map/ppermute | solution.py:39
  47.2 26.0 %collective-permute-start.15 = (bf16[192,1408]{1,0:T(8,128)(2,1)S(1)}, bf16[192,1408]{1,0:T(8,128)(2,1)S(1)}, u32[]{:S(2)}, u32[]{:S(2)}) collective-permute-start(bf16[192,1408]{1,0:T(8,128)(2,1)S(1)} %shard_map.245), channel_id=1, source_target_pairs={{0,8},{1,9},{2,10},{3,11},{4,12},{5,13},{6,14},{7,15},{8,0},{9,1},... | collective-permute-start | bytes 1622024 | tf_op jit(solution)/shard_map/ppermute | solution.py:39
  65.0 24.6 %collective-permute-start.22 = (bf16[256,1024]{1,0:T(8,128)(2,1)S(1)}, bf16[256,1024]{1,0:T(8,128)(2,1)S(1)}, u32[]{:S(2)}, u32[]{:S(2)}) collective-permute-start(bf16[256,1024]{1,0:T(8,128)(2,1)S(1)} %shard_map.246), channel_id=1, source_target_pairs={{0,2},{1,3},{2,0},{3,1},{4,6},{5,7},{6,4},{7,5},{8,10},{9,11},{10,... | collective-permute-start | bytes 1572872 | tf_op jit(solution)/shard_map/ppermute | solution.py:39
  73.3 34.7 %collective-permute-start.25 = (bf16[2,192,1408]{2,1,0:T(8,128)(2,1)S(1)}, bf16[2,192,1408]{2,1,0:T(8,128)(2,1)S(1)}, u32[]{:S(2)}, u32[]{:S(2)}) collective-permute-start(bf16[2,192,1408]{2,1,0:T(8,128)(2,1)S(1)} %pad_maximum_fusion.u0), channel_id=1, source_target_pairs={{0,16},{1,17},{2,18},{3,19},{4,20},{5,21},{6,22},{7,23},{8,24},{9,... | collective-permute-start | bytes 3244040 | tf_op jit(solution)/shard_map/ppermute | solution.py:39
  73.9 15.9 %collective-permute-start.19 = (bf16[128,1024]{1,0:T(8,128)(2,1)S(1)}, bf16[128,1024]{1,0:T(8,128)(2,1)S(1)}, u32[]{:S(2)}, u32[]{:S(2)}) collective-permute-start(bf16[128,1024]{1,0:T(8,128)(2,1)S(1)} %pad_maximum_fusion.6), channel_id=1, source_target_pairs={{0,2},{1,3},{2,0},{3,1},{4,6},{5,7},{6,4},{7,5},{8,10},{9,11},{10,... | collective-permute-start | bytes 786440 | tf_op jit(solution)/shard_map/ppermute | solution.py:39
  78.8 29.2 %collective-permute-start.26 = (bf16[2,192,1408]{2,1,0:T(8,128)(2,1)S(1)}, bf16[2,192,1408]{2,1,0:T(8,128)(2,1)S(1)}, u32[]{:S(2)}, u32[]{:S(2)}) collective-permute-start(bf16[2,192,1408]{2,1,0:T(8,128)(2,1)S(1)} %pad_maximum_fusion.1.u2), channel_id=1, source_target_pairs={{0,8},{1,9},{2,10},{3,11},{4,12},{5,13},{6,14},{7,15},{8,0},{9,1},... | collective-permute-start | bytes 3244040 | tf_op jit(solution)/shard_map/ppermute | solution.py:39
  127.3 27.0 %collective-permute-start.32 = (bf16[2,192,1408]{2,1,0:T(8,128)(2,1)}, bf16[2,192,1408]{2,1,0:T(8,128)(2,1)S(1)}, u32[]{:S(2)}, u32[]{:S(2)}) collective-permute-start(bf16[2,192,1408]{2,1,0:T(8,128)(2,1)} %get-tuple-element.242), channel_id=1, source_target_pairs={{0,8},{1,9},{2,10},{3,11},{4,12},{5,13},{6,14},{7,15},{8,0},{9,1},... | collective-permute-start | bytes 3244040 | tf_op jit(solution)/shard_map/ppermute | solution.py:39
  128.3 26.0 %collective-permute-start.31 = (bf16[2,192,1408]{2,1,0:T(8,128)(2,1)}, bf16[2,192,1408]{2,1,0:T(8,128)(2,1)}, u32[]{:S(2)}, u32[]{:S(2)}) collective-permute-start(bf16[2,192,1408]{2,1,0:T(8,128)(2,1)} %get-tuple-element.231), channel_id=1, source_target_pairs={{0,16},{1,17},{2,18},{3,19},{4,20},{5,21},{6,22},{7,23},{8,24},{9,... | collective-permute-start | bytes 3244040 | tf_op jit(solution)/shard_map/ppermute | solution.py:39
  178.7 20.9 %collective-permute-start.37 = (bf16[2,168,896]{2,1,0:T(8,128)(2,1)S(1)}, bf16[2,168,896]{2,1,0:T(8,128)(2,1)S(1)}, u32[]{:S(2)}, u32[]{:S(2)}) collective-permute-start(bf16[2,168,896]{2,1,0:T(8,128)(2,1)S(1)} %get-tuple-element.273), channel_id=1, source_target_pairs={{0,16},{1,17},{2,18},{3,19},{4,20},{5,21},{6,22},{7,23},{8,24},{9,... | collective-permute-start | bytes 1806344 | tf_op jit(solution)/shard_map/ppermute | solution.py:39
  180.1 19.5 %collective-permute-start.38 = (bf16[2,168,896]{2,1,0:T(8,128)(2,1)S(1)}, bf16[2,168,896]{2,1,0:T(8,128)(2,1)S(1)}, u32[]{:S(2)}, u32[]{:S(2)}) collective-permute-start(bf16[2,168,896]{2,1,0:T(8,128)(2,1)S(1)} %get-tuple-element.275), channel_id=1, source_target_pairs={{0,8},{1,9},{2,10},{3,11},{4,12},{5,13},{6,14},{7,15},{8,0},{9,1},... | collective-permute-start | bytes 1806344 | tf_op jit(solution)/shard_map/ppermute | solution.py:39
  181.1 17.6 %collective-permute-start.35 = (bf16[128,1536]{1,0:T(8,128)(2,1)S(1)}, bf16[128,1536]{1,0:T(8,128)(2,1)S(1)}, u32[]{:S(2)}, u32[]{:S(2)}) collective-permute-start(bf16[128,1536]{1,0:T(8,128)(2,1)S(1)} %get-tuple-element.260), channel_id=1, source_target_pairs={{0,2},{1,3},{2,0},{3,1},{4,6},{5,7},{6,4},{7,5},{8,10},{9,11},{10,... | collective-permute-start | bytes 1179656 | tf_op jit(solution)/shard_map/ppermute | solution.py:39
  181.4 26.0 %collective-permute-start.43 = (bf16[192,1408]{1,0:T(8,128)(2,1)S(1)}, bf16[192,1408]{1,0:T(8,128)(2,1)S(1)}, u32[]{:S(2)}, u32[]{:S(2)}) collective-permute-start(bf16[192,1408]{1,0:T(8,128)(2,1)S(1)} %shard_map.255), channel_id=1, source_target_pairs={{0,4},{1,5},{2,6},{3,7},{4,0},{5,1},{6,2},{7,3},{8,12},{9,13},{10,... | collective-permute-start | bytes 1622024 | tf_op jit(solution)/shard_map/ppermute | solution.py:39
  182.8 24.6 %collective-permute-start.42 = (bf16[192,1408]{1,0:T(8,128)(2,1)S(1)}, bf16[192,1408]{1,0:T(8,128)(2,1)S(1)}, u32[]{:S(2)}, u32[]{:S(2)}) collective-permute-start(bf16[192,1408]{1,0:T(8,128)(2,1)S(1)} %copy-done.21), channel_id=1, source_target_pairs={{0,8},{1,9},{2,10},{3,11},{4,12},{5,13},{6,14},{7,15},{8,0},{9,1},... | collective-permute-start | bytes 1622024 | tf_op jit(solution)/shard_map/ppermute | solution.py:39
  198.7 17.5 %collective-permute-start.28 = (bf16[256,1024]{1,0:T(8,128)(2,1)S(1)}, bf16[256,1024]{1,0:T(8,128)(2,1)S(1)}, u32[]{:S(2)}, u32[]{:S(2)}) collective-permute-start(bf16[256,1024]{1,0:T(8,128)(2,1)S(1)} %copy-done.23), channel_id=1, source_target_pairs={{0,1},{1,0},{2,3},{3,2},{4,5},{5,4},{6,7},{7,6},{8,9},{9,8},{10,11... | collective-permute-start | bytes 1572872 | tf_op jit(solution)/shard_map/ppermute | solution.py:39
  209.6 27.2 %collective-permute-start.41 = (bf16[168,896]{1,0:T(8,128)(2,1)S(1)}, bf16[168,896]{1,0:T(8,128)(2,1)S(1)}, u32[]{:S(2)}, u32[]{:S(2)}) collective-permute-start(bf16[168,896]{1,0:T(8,128)(2,1)S(1)} %shard_map.261), channel_id=1, source_target_pairs={{0,4},{1,5},{2,6},{3,7},{4,0},{5,1},{6,2},{7,3},{8,12},{9,13},{10,... | collective-permute-start | bytes 903176 | tf_op jit(solution)/shard_map/ppermute | solution.py:39
  211.2 25.6 %collective-permute-start.39 = (bf16[168,896]{1,0:T(8,128)(2,1)S(1)}, bf16[168,896]{1,0:T(8,128)(2,1)S(1)}, u32[]{:S(2)}, u32[]{:S(2)}) collective-permute-start(bf16[168,896]{1,0:T(8,128)(2,1)S(1)} %get-tuple-element.281), channel_id=1, source_target_pairs={{0,8},{1,9},{2,10},{3,11},{4,12},{5,13},{6,14},{7,15},{8,0},{9,1},... | collective-permute-start | bytes 903176 | tf_op jit(solution)/shard_map/ppermute | solution.py:39
  212.2 24.6 %collective-permute-start.36 = (bf16[64,2048]{1,0:T(8,128)(2,1)S(1)}, bf16[64,2048]{1,0:T(8,128)(2,1)S(1)}, u32[]{:S(2)}, u32[]{:S(2)}) collective-permute-start(bf16[64,2048]{1,0:T(8,128)(2,1)S(1)} %get-tuple-element.263), channel_id=1, source_target_pairs={{0,4},{1,5},{2,6},{3,7},{4,0},{5,1},{6,2},{7,3},{8,12},{9,13},{10,... | collective-permute-start | bytes 786440 | tf_op jit(solution)/shard_map/ppermute | solution.py:39
  216.3 21.9 %collective-permute-start.29 = (bf16[128,1024]{1,0:T(8,128)(2,1)S(1)}, bf16[128,1024]{1,0:T(8,128)(2,1)S(1)}, u32[]{:S(2)}, u32[]{:S(2)}) collective-permute-start(bf16[128,1024]{1,0:T(8,128)(2,1)S(1)} %get-tuple-element.236), channel_id=1, source_target_pairs={{0,2},{1,3},{2,0},{3,1},{4,6},{5,7},{6,4},{7,5},{8,10},{9,11},{10,... | collective-permute-start | bytes 786440 | tf_op jit(solution)/shard_map/ppermute | solution.py:39
  (63 other events, 687.4 us)

commit v5 on v4

--- a/solution.py
+++ b/solution.py
@@ -474,7 +474,7 @@
             q = qkv[rows, lanes]
             k = qkv[:, HT + i * HD:HT + (i + 1) * HD]
             v = qkv[:, 2 * HT + i * HD:2 * HT + (i + 1) * HD]
-            s = dot_cols(q, k) * SCALE + bias[rows]
+            s = dot_cols(q, k) * SCALE + bias[rows].astype(F32)
             top = jnp.max(s, axis=-1, keepdims=True)
             p = jnp.exp(s - top)
             total = jnp.sum(p, axis=-1, keepdims=True)
@@ -509,12 +509,13 @@
         rows = slice(b * HALF, (b + 1) * HALF)
         source = x2 if b == 0 else xc
         a = source[:, :D].astype(F32) + dot(full[rows], w[...])
-        after[rows] = a
+        if b == 0:
+            after[...] = a[:M]
         normed[rows] = (a * scale_of(a) * gain).astype(BF16)
 
 
-def feed_kernel(ids, normed, after, c2, cc, u0, u1, u2, u3,
-                hidden, dgu, out_keep, out_send, r_keep, r_send, gain_g, c_all, w, wd, wide, raw, sem, sem_d):
+def feed_kernel(ids, normed, gains, c2, cc, u0, u1, u2, u3, out_keep, out_send, r_keep, r_send, gain_g, a_keep, a_send, b_keep, b_send,
+                w, wd, wide, raw, hidden, dgu, gu_g, sem, sem_d):
     g, h, t = ids[0], ids[1], ids[2]
     copies, copies_d = [], []
     for n, (k, dh) in enumerate(ARRIVED):
@@ -523,12 +524,9 @@
             row = ((g ^ k) * 2 + (h ^ dh)) * 4 + (t ^ s)
             copies.append((b.at[n % 2, i * ROWS:(i + 1) * ROWS], w.at[aligned(row, ROWS)]))
         copies_d.append((b.at[n % 2, 4 * ROWS:], raw.at[n]))
-    started, started_d = fetch(copies, sem), fetch(copies_d, sem_d)
-    for p in range(4):
-        c_all[p * M:(p + 1) * M] = (c2 if p < 2 else cc)[(p % 2) * M:(p % 2 + 1) * M]
-    for copy in started_d:
-        copy.wait()
+    started_d, started = fetch(copies_d, sem_d), fetch(copies, sem)
     for n, (k, dh) in enumerate(ARRIVED):
+        started_d[n].wait()
         wide[aligned((g ^ k) * 2 + (h ^ dh), FROWS)] = tiles_out(raw[n].astype(F32))
     wd[...] = wide[...].astype(BF16)
     for copy in started:
@@ -536,56 +534,46 @@
     gain_sum = jnp.zeros((1, D), F32)
     for b in range(2):
         rows = slice(b * HALF, (b + 1) * HALF)
+        c = (c2 if b == 0 else cc)[...]
         gu = dot(normed[rows], w[...])
         gate, up = gu[:, :FT], gu[:, FT:]
         sig = 1.0 / (1.0 + jnp.exp(-gate))
         act = gate * sig
         hid = (act * up).astype(BF16)
         hidden[rows] = hid
-        dh = dot_cols(c_all[rows], wd[...])
-        dgate = (dh * up * (sig * (1.0 + gate * (1.0 - sig)))).astype(BF16)
-        dup = (dh * act).astype(BF16)
-        dgu[rows, :FT] = dgate
-        dgu[rows, FT:] = dup
+        dh = dot_cols(c, wd[...])
+        dgu[rows, :FT] = (dh * up * (sig * (1.0 + gate * (1.0 - sig)))).astype(BF16)
+        dgu[rows, FT:] = (dh * act).astype(BF16)
         dr = dot_cols(dgu[rows], w[...])
         out = dot(hid, wd[...])
-        a = after[rows]
-        gain_sum = gain_sum + jnp.sum(dr * (a * scale_of(a)), axis=0, keepdims=True)
-        if b == 0:
-            r_keep[...] = dr
-            out_keep[...] = out
-        else:
-            r_send[...] = dr.astype(BF16)
-            out_send[...] = out.astype(BF16)
-    gain_g[...] = gain_sum
-
-
-def feed_weights_kernel(ids, normed, dgu, hidden, c_all, a_keep, a_send, b_keep, b_send, gu, full):
-    g, h = ids[0], ids[1]
-    full[...] = dot_rows(hidden[...], c_all[...])
+        gain_sum = gain_sum + jnp.sum(dr * normed[rows].astype(F32), axis=0, keepdims=True)
+        (r_keep if b == 0 else r_send)[...] = dr.astype(BF16)
+        (out_keep if b == 0 else out_send)[...] = out.astype(BF16)
+    gain_g[...] = gain_sum / gains[1:2, :]
+    wide[...] = dot_rows(hidden[:HALF], c2[...]) + dot_rows(hidden[HALF:], cc[...])
     for k in range(4):
-        gu[...] = dot_rows(normed[:, aligned(g ^ k, HT)], dgu[...])
+        gu_g[...] = dot_rows(normed[:, aligned(g ^ k, HT)], dgu[...])
         for e in range(2):
             target, at = LEAVING[(k, e)]
             target = (a_keep, a_send, b_keep, b_send)[target]
-            target[at, :4 * ROWS] = gu[aligned(h ^ e, 4 * ROWS)].astype(BF16)
-            target[at, 4 * ROWS:] = tiles_in(full[aligned((g ^ k) * 2 + (h ^ e), FROWS)]).astype(BF16)
+            target[at, :4 * ROWS] = gu_g[aligned(h ^ e, 4 * ROWS)].astype(BF16)
+            target[at, 4 * ROWS:] = tiles_in(wide[aligned((g ^ k) * 2 + (h ^ e), FROWS)]).astype(BF16)
 
 
 def fold_kernel(keep, moved, kept, send):
-    kept[...] = keep[:M] + moved[:M].astype(F32)
-    send[...] = (keep[M:] + moved[M:].astype(F32)).astype(BF16)
+    kept[...] = keep[:M].astype(F32) + moved[:M].astype(F32)
+    send[...] = (keep[M:].astype(F32) + moved[M:].astype(F32)).astype(BF16)
 
 
 def fold_both_kernel(keep, dv, moved, kept, send):
-    kept[...] = keep[:M] + moved[:M, :D].astype(F32)
-    send[:, :D] = (keep[M:] + moved[M:, :D].astype(F32)).astype(BF16)
+    kept[...] = keep[:M].astype(F32) + moved[:M, :D].astype(F32)
+    send[:, :D] = (keep[M:].astype(F32) + moved[M:, :D].astype(F32)).astype(BF16)
     send[:, D:D + HT] = dv[M:]
     send[:, D + HT:] = moved[M:, D:]
 
 
 def branch_kernel(keep, moved, after, gains, c2, grad_after, low):
-    a = after[:M]
+    a = after[...]
     scale = scale_of(a)
     hat = a * scale
     dy = (keep[...] + moved[...].astype(F32)) * gains[1:2, :]
@@ -594,8 +582,9 @@
     low[...] = d.astype(BF16)
 
 
-def attend_back_kernel(ids, da2, dac, wo, qkv, attn, lse, bias, cs, sn, w, x2, xc,
-                       dqkv, r_keep, r_send, gain_g, do, dk, dv):
+def attend_back_kernel(ids, da2, dac, wo, qkv, attn, lse, bias, cs, sn, w, normed, gains, gain_two, full,
+                       r_keep, r_send, dv_keep, a_keep, a_send, b_keep, b_send, do, dk, dv, dqkv, scratch, rows_g, qkv_g):
+    g, h, t = ids[0], ids[1], ids[2]
     for b in range(2):
         rows = slice(b * HALF, (b + 1) * HALF)
         do[rows] = dot_cols((da2 if b == 0 else dac)[...], wo[...]).astype(BF16)
@@ -609,7 +598,7 @@
             v = qkv[:, 2 * HT + i * HD:2 * HT + (i + 1) * HD]
             d = do[rows, lanes]
             delta = jnp.sum(d.astype(F32) * attn[rows, lanes], axis=-1, keepdims=True)
-            p = jnp.exp(dot_cols(q, k) * SCALE + bias[rows] - lse[rows, i:i + 1])
+            p = jnp.exp(dot_cols(q, k) * SCALE + bias[rows].astype(F32) - lse[rows, i:i + 1])
             ds = (p * (dot_cols(d, v) - delta)).astype(BF16)
             dqs.append(dot(ds, k))
             dki, dvi = dot_rows(ds, q), dot_rows(p.astype(BF16), d)
@@ -626,31 +615,25 @@
         dqkv[rows, HT:2 * HT] = (u * cs[rows] - swap_halves(u) * sn[rows]).astype(BF16)
         dqkv[rows, 2 * HT:] = (0.5 * dv[rows]).astype(BF16)
         dr = dot_cols(dqkv[rows], w[:, :3 * HT])
-        x = (x2 if b == 0 else xc)[:, :D].astype(F32)
-        gain_sum = gain_sum + jnp.sum(dr * (x * scale_of(x)), axis=0, keepdims=True)
+        gain_sum = gain_sum + jnp.sum(dr * normed[rows].astype(F32), axis=0, keepdims=True)
         if b == 0:
-            r_keep[...] = dr
+            r_keep[...] = dr.astype(BF16)
+            dv_keep[...] = dqkv[rows, 2 * HT:]
         else:
             r_send[:, :D] = dr.astype(BF16)
             r_send[:, D:] = dqkv[rows, 2 * HT:]
-    gain_g[...] = gain_sum
-
-
-def attend_weights_kernel(ids, normed, dqkv, gain_one, gain_two, full, da2, dac, a_keep, a_send, b_keep, b_send,
-                          scratch, rows_g, qkv):
-    g, h, t = ids[0], ids[1], ids[2]
     rows_g[...] = jnp.zeros_like(rows_g)
-    rows_g[0:1] = gain_one[...]
+    rows_g[0:1] = gain_sum / gains[0:1, :]
     rows_g[1:2] = gain_two[...]
     for k in range(4):
         lanes = aligned(g ^ k, HT)
-        qkv[:, :3 * HT] = dot_rows(normed[:, lanes], dqkv[...])
-        qkv[:, 3 * HT:] = dot_rows(rows_g[:, lanes].astype(BF16), eye(8, 128))
+        qkv_g[:, :3 * HT] = dot_rows(normed[:, lanes], dqkv[...])
+        qkv_g[:, 3 * HT:] = dot_rows(rows_g[:, lanes].astype(BF16), eye(8, 128))
         scratch[...] = dot_rows(full[:HALF, lanes], da2[...]) + dot_rows(full[HALF:, lanes], dac[...])
         for e in range(2):
             target, at = LEAVING[(k, e)]
             target = (a_keep, a_send, b_keep, b_send)[target]
-            target[at, :4 * ROWS] = qkv[aligned(h ^ e, 4 * ROWS)].astype(BF16)
+            target[at, :4 * ROWS] = qkv_g[aligned(h ^ e, 4 * ROWS)].astype(BF16)
             target[at, 4 * ROWS:] = line_tiles_in(scratch[aligned((h ^ e) * 4 + t, ROWS)]).astype(BF16)
 
 
@@ -728,7 +711,7 @@
 
 
 def result_kernel(keep, moved, after, own, send):
-    out = after[:M] + (keep[...] + moved[...].astype(F32))
+    out = after[...] + (keep[...] + moved[...].astype(F32))
     own[...] = out[:FAST_L].astype(BF16)
     send[...] = out[FAST_L:].astype(BF16)
 
@@ -800,7 +783,7 @@
     position = position.reshape(N) + g * N
     begin = jnp.max(jnp.where(starts[None, :] <= position[:, None], starts[None, :], 0), axis=1)
     visible = (begin[:, None] == begin[None, :]) & (position[None, :] <= position[:, None])
-    bias = jnp.where(visible, 0.0, NEG).astype(F32)
+    bias = jnp.where(visible, 0.0, NEG).astype(BF16)
     lane = jnp.arange(HT, dtype=jnp.int32)
     frequency = 10000.0 ** (-((lane % (HD // 2)).astype(F32) * 2.0 / HD))
     angles = (position - begin).astype(F32)[:, None] * frequency[None, :]
@@ -838,37 +821,34 @@
         [SMEM] + [VMEM] * 6 + [ANY] * 4, (ids, x_two, x_core, v_two, cs, sn, bias, *q_parts),
         [pltpu.SemaphoreType.DMA((32,))])
     a_two = jnp.concatenate([attn_low, to_z(after_these(attn_low, c_two))], axis=0)
-    a_core = to_core(after_these(a_two, c_core))
     o_two = jnp.concatenate([o_own, o_first], axis=0)
     o_core = to_core(after_these(o_two, attn_low))
     u_parts = (u_a, to_y(u_a), u_b, to_x(u_b))
     a_core = to_core(a_two)
     attn_full, after, normed_two, out_w = call(
-        after_kernel, (shape((N, D)), shape((N, D), F32), shape((N, D)), shape((HT, D))),
+        after_kernel, (shape((N, D)), shape((M, D), F32), shape((N, D)), shape((HT, D))),
         [SMEM] + [VMEM] * 5 + [ANY] * 2, (ids, x_two, x_core, a_two, a_core, gains, o_two, o_core),
         [pltpu.VMEM((D, D), BF16), pltpu.SemaphoreType.DMA((32,))])
-    hidden, dgu, out_keep, out_send, r_keep, r_send, gain_two_g, c_all = call(
-        feed_kernel,
-        (shape((N, FT)), shape((N, 2 * FT)), shape((HALF, D), F32), shape((HALF, D)), shape((HALF, D), F32), shape((HALF, D)),
-         shape((1, D), F32), shape((N, D))),
-        [SMEM] + [VMEM] * 4 + [ANY] * 4, (ids, normed_two, after, c_two, c_core, *u_parts),
+    block = (2, 6 * ROWS, 2 * FT)
+    out_keep, out_send, r_keep, r_send, gain_two_g, a_keep, a_send, b_keep, b_send = call(
+        feed_kernel, (shape((HALF, D)),) * 4 + (shape((1, D), F32),) + (shape(block),) * 4,
+        [SMEM] + [VMEM] * 4 + [ANY] * 4, (ids, normed_two, gains, c_two, c_core, *u_parts),
         [pltpu.VMEM((D, 2 * FT), BF16), pltpu.VMEM((8 * FROWS, D), BF16), pltpu.VMEM((8 * FROWS, D), F32), pltpu.VMEM((8, 2 * ROWS, 2 * FT), BF16),
-         pltpu.SemaphoreType.DMA((32,)), pltpu.SemaphoreType.DMA((8,))])
+         pltpu.VMEM((N, FT), BF16), pltpu.VMEM((N, 2 * FT), BF16), pltpu.VMEM((HT, 2 * FT), F32),
+         pltpu.SemaphoreType.DMA((32,)), pltpu.SemaphoreType.DMA((8,))], mib=48)
 
     r_core = to_core(r_send)
-    block = (2, 6 * ROWS, 2 * FT)
-    a_keep, a_send, b_keep, b_send = call(
-        feed_weights_kernel, (shape(block),) * 4, [SMEM] + [VMEM] * 4, (ids, normed_two, dgu, hidden, c_all),
-        [pltpu.VMEM((HT, 2 * FT), F32), pltpu.VMEM((8 * FROWS, D), F32)])
     u_sums = (a_keep, to_y(a_send), b_keep, to_x(b_send))
 
-    def middle(r_keep, r_core, after, gains, c_two):
+    def middle(r_keep, r_core, after, gains, c_two, out_keep, o_core):
         kept, sent = call(fold_kernel, (shape((M, D), F32), shape((M, D))), [VMEM] * 2, (r_keep, r_core))
         grad_after, branch = call(branch_kernel, (shape((M, D), F32), shape((M, D))), [VMEM] * 5, (kept, to_z(sent), after, gains, c_two))
         b_two = jnp.concatenate([branch, to_z(branch)], axis=0)
-        return grad_after, b_two, to_core(b_two)
-
-    grad_after, b_two, b_core = fenced(middle, r_keep, after_these(r_core, a_send), after, gains, c_two)
+        o_kept, o_sent = call(fold_kernel, (shape((M, D), F32), shape((M, D))), [VMEM] * 2, (out_keep, after_these(o_core, branch)))
+        return grad_after, b_two, to_core(b_two), o_kept, o_sent
+
+    grad_after, b_two, b_core, o_kept, o_sent = fenced(
+        middle, r_keep, after_these(r_core, a_send), after, gains, c_two, out_keep, to_core(out_send))
 
     def second_sum(a_own, a_send, b_own, b_send):
         return a_own, a_send, call(sum_second_kernel, shape(b_own.shape), [VMEM] * 2, (b_own, to_y(b_send)))
@@ -878,47 +858,44 @@
 
     u_sums = first_sum(lax.optimization_barrier(u_sums + (b_core,))[:4])
     b_core = after_these(b_core, u_sums[3])
-    def attend_back(*inputs):
-        return tuple(call(
-            attend_back_kernel,
-            (shape((N, 3 * HT)), shape((HALF, D), F32), shape((HALF, D + HT)), shape((1, D), F32)),
-            [SMEM] + [VMEM] * 12, (ids,) + inputs,
-            [pltpu.VMEM((N, HT), BF16), pltpu.VMEM((N, HT), F32), pltpu.VMEM((N, HT), F32)], mib=60))
-
-    dqkv, r_keep, r_send, gain_one_g = fenced(attend_back, b_two, b_core, out_w, qkv, attn, lse, bias, cs, sn, qkv_w, x_two, x_core)
+    def attend_back(o_sent, *inputs):
+        o_moved = to_z(o_sent)
+        block = (2, 4 * ROWS + 40, WQ)
+        return (o_moved,) + tuple(call(
+            attend_back_kernel, (shape((HALF, D)), shape((HALF, D + HT)), shape((HALF, HT))) + (shape(block),) * 4,
+            [SMEM] + [VMEM] * 14, (ids,) + inputs,
+            [pltpu.VMEM((N, HT), BF16), pltpu.VMEM((N, HT), F32), pltpu.VMEM((N, HT), F32), pltpu.VMEM((N, 3 * HT), BF16),
+             pltpu.VMEM((HT, D), F32), pltpu.VMEM((8, D), F32), pltpu.VMEM((HT, WQ), F32)], mib=60))
+
+    o_moved, r_keep, r_send, dv_keep, a_keep, a_send, b_keep, b_send = fenced(
+        attend_back, o_sent, b_two, b_core, out_w, qkv, attn, lse, bias, cs, sn, qkv_w, normed_one, gains, gain_two_g, attn_full)
     u_sums = second_sum(*u_sums)
     r_send = after_these(r_send, u_sums[2])
-    o_kept, o_sent = call(fold_kernel, (shape((M, D), F32), shape((M, D))), [VMEM] * 2,
-                          (out_keep, to_core(after_these(out_send, b_two))))
-    y_own, y_send = call(result_kernel, (shape((L, D)), shape((L, D))), [VMEM] * 3, (o_kept, to_z(o_sent), after))
+    y_own, y_send = call(result_kernel, (shape((L, D)), shape((L, D))), [VMEM] * 3, (o_kept, o_moved, after))
     layer_out = call(result_home_kernel, shape((2, L, D)), [SMEM] + [VMEM] * 2, (ids, y_own, to_h(y_send)))
-    dv_keep = dqkv[:HALF, 2 * HT:]
     r_core = to_core(r_send)
     kept, sent = call(fold_both_kernel, (shape((M, D), F32), shape((M, D + 2 * HT))), [VMEM] * 3, (r_keep, dv_keep, r_core))
-    block = (2, 4 * ROWS + 40, WQ)
-    a_keep, a_send, b_keep, b_send = call(
-        attend_weights_kernel, (shape(block),) * 4,
-        [SMEM] + [VMEM] * 7, (ids, normed_one, after_these(dqkv, sent), gain_one_g, gain_two_g, attn_full, b_two, b_core),
-        [pltpu.VMEM((HT, D), F32), pltpu.VMEM((8, D), F32), pltpu.VMEM((HT, WQ), F32)])
+    a_send, b_send, _ = lax.optimization_barrier((a_send, b_send, sent))
     q_sums = (a_keep, to_y(a_send), b_keep, to_x(b_send))
     own, sent = call(input_kernel, (shape((L, 2 * D)), shape((L, 2 * D))), [SMEM] + [VMEM] * 7,
                      (ids, kept, to_z(sent), x_two, gains, grad_after, dv_keep, r_core), [pltpu.VMEM((M, 2 * D), BF16)])
     home = to_h(sent)
     input_grad, v1_out = call(home_kernel, (shape((2, L, D), F32),) * 2, [SMEM] + [VMEM] * 3, (ids, own, home, v1_acc))
 
-    def finish(kernel, sums, rest, *first):
+    def finish(kernel, sums, rest, first=(), last=()):
         a_own, a_send, b_send = sums
         dims = a_own.shape
         kept, sent, rows = call(kernel, (shape((2, ROWS, dims[1])), shape((2, ROWS, dims[1])), shape(rest, F32)), [SMEM] + [VMEM] * 3,
                                 (ids, a_own, to_x(a_send), after_these(to_h(b_send), *first)), [pltpu.VMEM(dims, F32)])
         first = to_z(sent)
-        return (ids, kept, first, to_core(pair_of(kept, first))), rows
-
-    q_sums = second_sum(*first_sum(lax.optimization_barrier(q_sums + (sent,))[:4]))
+        return (ids, kept, first, to_core(pair_of(kept, after_these(first, *last)))), rows
+
+    a_own, a_send, b_own, b_send = first_sum(q_sums)
+    q_sums = second_sum(a_own, a_send, after_these(b_own, home), b_send)
     parts, down_g = finish(sum_hidden_kernel, u_sums, (FROWS, D))
     gate_g, up_g = call(join_hidden_kernel, (shape((ROWS, 4 * FT), F32),) * 2, [SMEM] + [VMEM] * 3, parts,
                         [pltpu.VMEM((4, ROWS, 2 * FT), F32)])
-    parts, out_g = finish(sum_qkv_kernel, q_sums, (ROWS, D), home, gate_g)
+    parts, out_g = finish(sum_qkv_kernel, q_sums, (ROWS, D), (gate_g,), (input_grad,))
     query_g, key_g, value_g, gain_g = call(
         join_qkv_kernel, (shape((ROWS, D), F32),) * 3 + (shape((ROWS, 128), F32),), [SMEM] + [VMEM] * 3, parts)
     return (layer_out, input_grad, v1_out, gain_g[:, 0], query_g, key_g, value_g, out_g, gain_g[:, 1], gate_g, up_g, down_g)

time: 252 us -> 243 us (0.964)
  waiting for transfers between devices: 116 us -> 105 us
  starting transfers between devices: 39.1 us -> 43.5 us
  Pallas kernels: 80.5 us -> 76.9 us
    ppermute x48, waiting for transfers between devices: 116 us -> 105 us  [send(): return lax.ppermute(array, ALL, pairs)]
    ppermute x48, starting transfers between devices: 39.1 us -> 43.5 us  [send(): return lax.ppermute(array, ALL, pairs)]
    pallas_call x33 -> x31, Pallas kernels: 80.5 us -> 76.9 us  [call(): pl.pallas_call(kernel, out_shape=outs, in_specs=specs, out_specs=jax.tree...]
    unnamed x77 -> x53, local copies, waits for them, and re-layouts: 5.97 us -> 7.73 us
  transfers between devices with their start and end apart: 48 -> 48, of which waited for: 21 -> 26; matrix products, arithmetic and copies ran while one was open for 3% -> 3% of each run, Pallas kernels for 20% -> 23%
where the time goes in v5:
time: 243 us; the launch traced here: 242 us
  waiting for transfers between devices  105 us (43%)
  Pallas kernels  76.9 us (32%)
  starting transfers between devices  43.5 us (18%)
  local copies, waits for them, and re-layouts  10 us (4%)
  other arithmetic  6.03 us (2%)
    ppermute x48, waiting for transfers between devices, send(): return lax.ppermute(array, ALL, pairs)  105 us
    pallas_call x31, Pallas kernels, call(): pl.pallas_call(kernel, out_shape=outs, in_specs=specs, out_specs=jax.tree...  76.9 us
    ppermute x48, starting transfers between devices, send(): return lax.ppermute(array, ALL, pairs)  43.5 us
    unnamed x53, local copies, waits for them, and re-layouts  7.73 us
  transfers between devices with their start and end apart: 48, of which 26 were waited for; matrix products, arithmetic and copies ran while one was open for 3% of the time, Pallas kernels for 23%

profile of v5, /device:TPU:0, one launch (start us, length us, event | category | flops | bytes accessed | tf_op | source)
XLA Modules:
  0.0 242.4 jit_solution(10232234856751877951)
XLA Ops:
  0.8 2.9 %shard_map.238 = (bf16[2,32,896]{2,1,0:T(8,128)(2,1)}, bf16[2,32,896]{2,1,0:T(8,128)(2,1)}, bf16[40,896]{1,0:T(8,128)(2,1)}, bf16[64,2048]{1,0:T(8,128)(2,1)}, bf16[64,1024]{1,0:T(8,128)(2,1)}) custom-call(s32[3]{0:T(128)S(1)} %pad_add_fusion.ids, bf16[1,32]{1,0:T(2,128)(2,1)} %bitcast.23, bf16[1,32]{1,0:T(2,128)(2,1)} %bitcast.24, bf16[32,1024]{1,0:T(8,128)(2,1)} %wq.1, ...), custom_call_target="tpu_custom_call" | custom-call | flops 1 | bytes 1 | tf_op jit(solution)/shard_map/pallas_call | solution.py:305
  3.7 3.1 %collective-permute-start.7 = (bf16[2,32,896]{2,1,0:T(8,128)(2,1)}, bf16[2,32,896]{2,1,0:T(8,128)(2,1)S(1)}, u32[]{:S(2)}, u32[]{:S(2)}) collective-permute-start(bf16[2,32,896]{2,1,0:T(8,128)(2,1)} %get-tuple-element.205), channel_id=1, source_target_pairs={{0,2},{1,3},{2,0},{3,1},{4,6},{5,7},{6,4},{7,5},{8,10},{9,11},{10,... | collective-permute-start | bytes 344072 | tf_op jit(solution)/shard_map/ppermute | solution.py:39
  21.4 3.1 %fusion = (f32[512,256]{1,0:T(8,128)}, f32[512,256]{1,0:T(8,128)}) fusion(f32[256]{0:T(256)S(1)} %get-tuple-element.307, f32[256]{0:T(256)S(1)} %get-tuple-element.308, f32[512]{0:T(512)S(1)} %subtract_convert_fusion), kind=kLoop, calls=%fused_computation.10 | loop fusion | flops 262144 | bytes 1052672 | tf_op jit(solution)/shard_map/mul | solution.py:791
  29.5 5.8 %collective-permute-done.9 = bf16[168,896]{1,0:T(8,128)(2,1)} collective-permute-done((bf16[168,896]{1,0:T(8,128)(2,1)S(1)}, bf16[168,896]{1,0:T(8,128)(2,1)}, u32[]{:S(2)}, u32[]{:S(2)}) %collective-permute-start.9) | collective-permute-done | bytes 301088 | tf_op jit(solution)/shard_map/ppermute | solution.py:39
  39.2 5.1 %collective-permute-done.5.moved = bf16[128,1536]{1,0:T(8,128)(2,1)S(1)} collective-permute-done((bf16[128,1536]{1,0:T(8,128)(2,1)}, bf16[128,1536]{1,0:T(8,128)(2,1)S(1)}, u32[]{:S(2)}, u32[]{:S(2)}) %collective-permute-start.5) | collective-permute-done | bytes 393248 | tf_op jit(solution)/shard_map/ppermute | solution.py:39
  49.2 14.2 %collective-permute-done.17 = bf16[192,1408]{1,0:T(8,128)(2,1)S(1)} collective-permute-done((bf16[192,1408]{1,0:T(8,128)(2,1)S(1)}, bf16[192,1408]{1,0:T(8,128)(2,1)S(1)}, u32[]{:S(2)}, u32[]{:S(2)}) %collective-permute-start.17) | collective-permute-done | bytes 540704 | tf_op jit(solution)/shard_map/ppermute | solution.py:39
  65.0 3.7 %collective-permute-start.23 = (bf16[256,1024]{1,0:T(8,128)(2,1)S(1)}, bf16[256,1024]{1,0:T(8,128)(2,1)S(1)}, u32[]{:S(2)}, u32[]{:S(2)}) collective-permute-start(bf16[256,1024]{1,0:T(8,128)(2,1)S(1)} %shard_map.246), channel_id=1, source_target_pairs={{0,2},{1,3},{2,0},{3,1},{4,6},{5,7},{6,4},{7,5},{8,10},{9,11},{10,... | collective-permute-start | bytes 1572872 | tf_op jit(solution)/shard_map/ppermute | solution.py:39
  68.7 5.4 %collective-permute-done.16 = bf16[192,1408]{1,0:T(8,128)(2,1)S(1)} collective-permute-done((bf16[192,1408]{1,0:T(8,128)(2,1)S(1)}, bf16[192,1408]{1,0:T(8,128)(2,1)S(1)}, u32[]{:S(2)}, u32[]{:S(2)}) %collective-permute-start.16) | collective-permute-done | bytes 540704 | tf_op jit(solution)/shard_map/ppermute | solution.py:39
  74.8 3.3 %collective-permute-done.18 = bf16[192,1408]{1,0:T(8,128)(2,1)S(1)} collective-permute-done((bf16[192,1408]{1,0:T(8,128)(2,1)S(1)}, bf16[192,1408]{1,0:T(8,128)(2,1)S(1)}, u32[]{:S(2)}, u32[]{:S(2)}) %collective-permute-start.18) | collective-permute-done | bytes 540704 | tf_op jit(solution)/shard_map/ppermute | solution.py:39
  79.6 9.7 %shard_map.247 = (bf16[1024,896]{1,0:T(8,128)(2,1)}, bf16[512,1024]{1,0:T(8,128)(2,1)}, bf16[512,768]{1,0:T(8,128)(2,1)}, f32[512,256]{1,0:T(8,128)}, bf16[512,2...) custom-call(s32[3]{0:T(128)S(1)} %pad_add_fusion.ids, bf16[256,1280]{1,0:T(8,128)(2,1)S(1)} %get-tuple-element.202.x2, ...), custom_call_target="tpu_custom_call" | custom-call | flops 1 | bytes 1 | tf_op jit(solution)/shard_map/pallas_call | solution.py:305
  89.9 8.5 %collective-permute-done.21 = bf16[512,256]{1,0:T(8,128)(2,1)S(1)} collective-permute-done((bf16[512,256]{1,0:T(8,128)(2,1)S(1)}, bf16[512,256]{1,0:T(8,128)(2,1)S(1)}, u32[]{:S(2)}, u32[]{:S(2)}) %collective-permute-start.21) | collective-permute-done | bytes 262176 | tf_op jit(solution)/shard_map/ppermute | solution.py:39
  100.4 6.7 %shard_map.248 = (bf16[512,1024]{1,0:T(8,128)(2,1)}, f32[128,1024]{1,0:T(8,128)}, bf16[512,1024]{1,0:T(8,128)(2,1)S(1)}, bf16[256,1024]{1,0:T(8,128)(2,1)}) custom-call(s32[3]{0:T(128)S(1)} %pad_add_fusion.ids, bf16[256,1280]{1,0:T(8,128)(2,1)S(1)} %get-tuple-element.202.x2, bf16[256,1280]{1,0:T(8,128)(2,1)S(1)} %collective-permute-done.6.xc, ...), custom_call_target="tpu_custom_call" | custom-call | flops 1 | bytes 1 | tf_op jit(solution)/shard_map/pallas_call | solution.py:305
  108.5 13.1 %shard_map.249 = (bf16[256,1024]{1,0:T(8,128)(2,1)}, bf16[256,1024]{1,0:T(8,128)(2,1)}, bf16[256,1024]{1,0:T(8,128)(2,1)}, bf16[256,1024]{1,0:T(8,128)(2,1)}, f3...) custom-call(s32[3]{0:T(128)S(1)} %pad_add_fusion.ids, ...), custom_call_target="tpu_custom_call" | custom-call | flops 1 | bytes 1 | tf_op jit(solution)/shard_map/pallas_call | solution.py:305
  126.3 21.5 %conditional.2 = (f32[128,1024]{1,0:T(8,128)}, bf16[256,1024]{1,0:T(8,128)(2,1)}, bf16[256,1024]{1,0:T(8,128)(2,1)}, f32[128,1024]{1,0:T(8,128)}, bf16[128,1024]{1,0:T(8,128)(2,1)}) conditional(s32[]{:T(128)} %convert_element_type.21, () %tuple.45, (bf16[256,1024]{1,0:T(8,128)(2,1)}, bf16[256,1024]{1,0:T(8,128)(2,1)}, f32[128,1024]{1,0:T(8,128)}, ...), branch_computations={%region_1.2_spmd, %region_2.3_spmd} | conditional | flops 3 | bytes 9437403 | solution.py:753
  129.1 7.0 %collective-permute-done.1.moved = bf16[128,1024]{1,0:T(8,128)(2,1)S(1)} collective-permute-done((bf16[128,1024]{1,0:T(8,128)(2,1)S(1)}, bf16[128,1024]{1,0:T(8,128)(2,1)S(1)}, u32[]{:S(2)}, u32[]{:S(2)}) %collective-permute-start.1) | collective-permute-done | bytes 262176 | tf_op jit(solution)/shard_map/cond/branch_1_fun/ppermute | solution.py:39
  139.3 5.5 %collective-permute-done.2 = bf16[128,1024]{1,0:T(8,128)(2,1)S(1)} collective-permute-done((bf16[128,1024]{1,0:T(8,128)(2,1)S(1)}, bf16[128,1024]{1,0:T(8,128)(2,1)S(1)}, u32[]{:S(2)}, u32[]{:S(2)}) %collective-permute-start.2) | collective-permute-done | bytes 262176 | tf_op jit(solution)/shard_map/cond/branch_1_fun/ppermute | solution.py:39
  153.5 16.3 %conditional.3 = (bf16[128,1024]{1,0:T(8,128)(2,1)}, bf16[256,1024]{1,0:T(8,128)(2,1)}, bf16[256,1280]{1,0:T(8,128)(2,1)}, bf16[256,256]{1,0:T(8,128)(2,1)S(1)},...) conditional(s32[]{:T(128)} %convert_element_type.21, () %tuple.60, ...), branch_computations={%region_3.4_spmd, %region_4.5_spmd} | conditional | flops 1 | bytes 3981392 | solution.py:753
  154.2 15.6 %branch_1_fun.7 = (bf16[256,1024]{1,0:T(8,128)(2,1)}, bf16[256,1280]{1,0:T(8,128)(2,1)}, bf16[256,256]{1,0:T(8,128)(2,1)S(1)}, bf16[2,168,896]{2,1,0:T(8,128)(2,...) custom-call(s32[3]{0:T(128)S(1)} %get-tuple-element.61.ids, ...), custom_call_target="tpu_custom_call" | custom-call | flops 1 | bytes 1 | tf_op jit(solution)/shard_map/cond/branch_1_fun/pallas_call | solution.py:305
  179.0 9.3 %collective-permute-done.37.a_moved = bf16[2,168,896]{2,1,0:T(8,128)(2,1)S(1)} collective-permute-done((bf16[2,168,896]{2,1,0:T(8,128)(2,1)}, bf16[2,168,896]{2,1,0:T(8,128)(2,1)S(1)}, u32[]{:S(2)}, u32[]{:S(2)}) %collective-permute-start.37) | collective-permute-done | bytes 602144 | tf_op jit(solution)/shard_map/ppermute | solution.py:39
  197.3 12.5 %collective-permute-done.43.moved = bf16[192,1408]{1,0:T(8,128)(2,1)S(1)} collective-permute-done((bf16[192,1408]{1,0:T(8,128)(2,1)S(1)}, bf16[192,1408]{1,0:T(8,128)(2,1)S(1)}, u32[]{:S(2)}, u32[]{:S(2)}) %collective-permute-start.43) | collective-permute-done | bytes 540704 | tf_op jit(solution)/shard_map/ppermute | solution.py:39
  215.9 3.9 %collective-permute-done.44.first = bf16[2,32,1408]{2,1,0:T(8,128)(2,1)S(1)} collective-permute-done((bf16[2,32,1408]{2,1,0:T(8,128)(2,1)S(1)}, bf16[2,32,1408]{2,1,0:T(8,128)(2,1)S(1)}, u32[]{:S(2)}, u32[]{:S(2)}) %collective-permute-start.44) | collective-permute-done | bytes 180256 | tf_op jit(solution)/shard_map/ppermute | solution.py:39
  223.4 5.3 %collective-permute-done.41.moved = bf16[168,896]{1,0:T(8,128)(2,1)S(1)} collective-permute-done((bf16[168,896]{1,0:T(8,128)(2,1)S(1)}, bf16[168,896]{1,0:T(8,128)(2,1)S(1)}, u32[]{:S(2)}, u32[]{:S(2)}) %collective-permute-start.41) | collective-permute-done | bytes 301088 | tf_op jit(solution)/shard_map/ppermute | solution.py:39
  231.1 2.7 %collective-permute-start.32 = (bf16[64,1024]{1,0:T(8,128)(2,1)S(1)}, bf16[64,1024]{1,0:T(8,128)(2,1)S(1)}, u32[]{:S(2)}, u32[]{:S(2)}) collective-permute-start(bf16[64,1024]{1,0:T(8,128)(2,1)S(1)} %get-tuple-element.263), channel_id=1, source_target_pairs={{0,4},{1,5},{2,6},{3,7},{4,0},{5,1},{6,2},{7,3},{8,12},{9,13},{10,... | collective-permute-start | bytes 393224 | tf_op jit(solution)/shard_map/ppermute | solution.py:39
  236.2 2.9 %collective-permute-done.32.moved = bf16[64,1024]{1,0:T(8,128)(2,1)S(1)} collective-permute-done((bf16[64,1024]{1,0:T(8,128)(2,1)S(1)}, bf16[64,1024]{1,0:T(8,128)(2,1)S(1)}, u32[]{:S(2)}, u32[]{:S(2)}) %collective-permute-start.32) | collective-permute-done | bytes 131104 | tf_op jit(solution)/shard_map/ppermute | solution.py:39
  (186 shorter events, 91.8 us)
Async XLA Ops:
  6.8 17.7 %collective-permute-start.4 = (bf16[64,2048]{1,0:T(8,128)(2,1)}, bf16[64,2048]{1,0:T(8,128)(2,1)}, u32[]{:S(2)}, u32[]{:S(2)}) collective-permute-start(bf16[64,2048]{1,0:T(8,128)(2,1)} %get-tuple-element.199), channel_id=1, source_target_pairs={{0,4},{1,5},{2,6},{3,7},{4,0},{5,1},{6,2},{7,3},{8,12},{9,13},{10,... | collective-permute-start | bytes 786440 | tf_op jit(solution)/shard_map/ppermute | solution.py:39
  17.3 20.9 %collective-permute-start.10 = (bf16[168,896]{1,0:T(8,128)(2,1)S(1)}, bf16[168,896]{1,0:T(8,128)(2,1)}, u32[]{:S(2)}, u32[]{:S(2)}) collective-permute-start(bf16[168,896]{1,0:T(8,128)(2,1)S(1)} %shard_map.242), channel_id=1, source_target_pairs={{0,8},{1,9},{2,10},{3,11},{4,12},{5,13},{6,14},{7,15},{8,0},{9,1},... | collective-permute-start | bytes 903176 | tf_op jit(solution)/shard_map/ppermute | solution.py:39
  18.8 16.5 %collective-permute-start.9 = (bf16[168,896]{1,0:T(8,128)(2,1)S(1)}, bf16[168,896]{1,0:T(8,128)(2,1)}, u32[]{:S(2)}, u32[]{:S(2)}) collective-permute-start(bf16[168,896]{1,0:T(8,128)(2,1)S(1)} %shard_map.242), channel_id=1, source_target_pairs={{0,4},{1,5},{2,6},{3,7},{4,0},{5,1},{6,2},{7,3},{8,12},{9,13},{10,... | collective-permute-start | bytes 903176 | tf_op jit(solution)/shard_map/ppermute | solution.py:39
  21.3 15.6 %collective-permute-start.15 = (bf16[2,32,1408]{2,1,0:T(8,128)(2,1)}, bf16[2,32,1408]{2,1,0:T(8,128)(2,1)}, u32[]{:S(2)}, u32[]{:S(2)}) collective-permute-start(bf16[2,32,1408]{2,1,0:T(8,128)(2,1)} %shard_map.244), channel_id=1, source_target_pairs={{0,1},{1,0},{2,3},{3,2},{4,5},{5,4},{6,7},{7,6},{8,9},{9,8},{10,11... | collective-permute-start | bytes 540680 | tf_op jit(solution)/shard_map/ppermute | solution.py:39
  26.9 17.3 %collective-permute-start.5 = (bf16[128,1536]{1,0:T(8,128)(2,1)}, bf16[128,1536]{1,0:T(8,128)(2,1)S(1)}, u32[]{:S(2)}, u32[]{:S(2)}) collective-permute-start(bf16[128,1536]{1,0:T(8,128)(2,1)} %get-tuple-element.200.mine), channel_id=1, source_target_pairs={{0,2},{1,3},{2,0},{3,1},{4,6},{5,7},{6,4},{7,5},{8,10},{9,11},{10,... | collective-permute-start | bytes 1179656 | tf_op jit(solution)/shard_map/ppermute | solution.py:39
  38.1 25.4 %collective-permute-start.17 = (bf16[192,1408]{1,0:T(8,128)(2,1)S(1)}, bf16[192,1408]{1,0:T(8,128)(2,1)S(1)}, u32[]{:S(2)}, u32[]{:S(2)}) collective-permute-start(bf16[192,1408]{1,0:T(8,128)(2,1)S(1)} %shard_map.245), channel_id=1, source_target_pairs={{0,4},{1,5},{2,6},{3,7},{4,0},{5,1},{6,2},{7,3},{8,12},{9,13},{10,... | collective-permute-start | bytes 1622024 | tf_op jit(solution)/shard_map/ppermute | solution.py:39
  45.4 18.6 %collective-permute-start.12 = (bf16[2,168,896]{2,1,0:T(8,128)(2,1)S(1)}, bf16[2,168,896]{2,1,0:T(8,128)(2,1)S(1)}, u32[]{:S(2)}, u32[]{:S(2)}) collective-permute-start(bf16[2,168,896]{2,1,0:T(8,128)(2,1)S(1)} %pad_maximum_fusion.3.b0), channel_id=1, source_target_pairs={{0,16},{1,17},{2,18},{3,19},{4,20},{5,21},{6,22},{7,23},{8,24},{9,... | collective-permute-start | bytes 1806344 | tf_op jit(solution)/shard_map/ppermute | solution.py:39
  47.2 16.9 %collective-permute-start.13 = (bf16[2,168,896]{2,1,0:T(8,128)(2,1)S(1)}, bf16[2,168,896]{2,1,0:T(8,128)(2,1)S(1)}, u32[]{:S(2)}, u32[]{:S(2)}) collective-permute-start(bf16[2,168,896]{2,1,0:T(8,128)(2,1)S(1)} %pad_maximum_fusion.4.b2), channel_id=1, source_target_pairs={{0,8},{1,9},{2,10},{3,11},{4,12},{5,13},{6,14},{7,15},{8,0},{9,1},... | collective-permute-start | bytes 1806344 | tf_op jit(solution)/shard_map/ppermute | solution.py:39
  48.6 25.5 %collective-permute-start.16 = (bf16[192,1408]{1,0:T(8,128)(2,1)S(1)}, bf16[192,1408]{1,0:T(8,128)(2,1)S(1)}, u32[]{:S(2)}, u32[]{:S(2)}) collective-permute-start(bf16[192,1408]{1,0:T(8,128)(2,1)S(1)} %shard_map.245), channel_id=1, source_target_pairs={{0,8},{1,9},{2,10},{3,11},{4,12},{5,13},{6,14},{7,15},{8,0},{9,1},... | collective-permute-start | bytes 1622024 | tf_op jit(solution)/shard_map/ppermute | solution.py:39
  65.0 24.4 %collective-permute-start.23 = (bf16[256,1024]{1,0:T(8,128)(2,1)S(1)}, bf16[256,1024]{1,0:T(8,128)(2,1)S(1)}, u32[]{:S(2)}, u32[]{:S(2)}) collective-permute-start(bf16[256,1024]{1,0:T(8,128)(2,1)S(1)} %shard_map.246), channel_id=1, source_target_pairs={{0,2},{1,3},{2,0},{3,1},{4,6},{5,7},{6,4},{7,5},{8,10},{9,11},{10,... | collective-permute-start | bytes 1572872 | tf_op jit(solution)/shard_map/ppermute | solution.py:39
  74.2 32.8 %collective-permute-start.26 = (bf16[2,192,1408]{2,1,0:T(8,128)(2,1)S(1)}, bf16[2,192,1408]{2,1,0:T(8,128)(2,1)S(1)}, u32[]{:S(2)}, u32[]{:S(2)}) collective-permute-start(bf16[2,192,1408]{2,1,0:T(8,128)(2,1)S(1)} %pad_maximum_fusion.u0), channel_id=1, source_target_pairs={{0,16},{1,17},{2,18},{3,19},{4,20},{5,21},{6,22},{7,23},{8,24},{9,... | collective-permute-start | bytes 3244040 | tf_op jit(solution)/shard_map/ppermute | solution.py:39
  74.7 14.9 %collective-permute-start.20 = (bf16[128,1024]{1,0:T(8,128)(2,1)S(1)}, bf16[128,1024]{1,0:T(8,128)(2,1)S(1)}, u32[]{:S(2)}, u32[]{:S(2)}) collective-permute-start(bf16[128,1024]{1,0:T(8,128)(2,1)S(1)} %pad_maximum_fusion.6), channel_id=1, source_target_pairs={{0,2},{1,3},{2,0},{3,1},{4,6},{5,7},{6,4},{7,5},{8,10},{9,11},{10,... | collective-permute-start | bytes 786440 | tf_op jit(solution)/shard_map/ppermute | solution.py:39
  78.2 28.9 %collective-permute-start.27 = (bf16[2,192,1408]{2,1,0:T(8,128)(2,1)S(1)}, bf16[2,192,1408]{2,1,0:T(8,128)(2,1)S(1)}, u32[]{:S(2)}, u32[]{:S(2)}) collective-permute-start(bf16[2,192,1408]{2,1,0:T(8,128)(2,1)S(1)} %pad_maximum_fusion.1.u2), channel_id=1, source_target_pairs={{0,8},{1,9},{2,10},{3,11},{4,12},{5,13},{6,14},{7,15},{8,0},{9,1},... | collective-permute-start | bytes 3244040 | tf_op jit(solution)/shard_map/ppermute | solution.py:39
  122.5 26.2 %collective-permute-start.31 = (bf16[2,192,1408]{2,1,0:T(8,128)(2,1)}, bf16[2,192,1408]{2,1,0:T(8,128)(2,1)}, u32[]{:S(2)}, u32[]{:S(2)}) collective-permute-start(bf16[2,192,1408]{2,1,0:T(8,128)(2,1)} %get-tuple-element.246), channel_id=1, source_target_pairs={{0,8},{1,9},{2,10},{3,11},{4,12},{5,13},{6,14},{7,15},{8,0},{9,1},... | collective-permute-start | bytes 3244040 | tf_op jit(solution)/shard_map/ppermute | solution.py:39
  123.2 25.7 %collective-permute-start.30 = (bf16[2,192,1408]{2,1,0:T(8,128)(2,1)S(1)}, bf16[2,192,1408]{2,1,0:T(8,128)(2,1)}, u32[]{:S(2)}, u32[]{:S(2)}) collective-permute-start(bf16[2,192,1408]{2,1,0:T(8,128)(2,1)S(1)} %get-tuple-element.235), channel_id=1, source_target_pairs={{0,16},{1,17},{2,18},{3,19},{4,20},{5,21},{6,22},{7,23},{8,24},{9,... | collective-permute-start | bytes 3244040 | tf_op jit(solution)/shard_map/ppermute | solution.py:39
  152.7 17.1 %collective-permute-start.33 = (bf16[192,1408]{1,0:T(8,128)(2,1)}, bf16[192,1408]{1,0:T(8,128)(2,1)S(1)}, u32[]{:S(2)}, u32[]{:S(2)}) collective-permute-start(bf16[192,1408]{1,0:T(8,128)(2,1)} %get-tuple-element.251), channel_id=1, source_target_pairs={{0,16},{1,17},{2,18},{3,19},{4,20},{5,21},{6,22},{7,23},{8,24},{9,... | collective-permute-start | bytes 1622024 | tf_op jit(solution)/shard_map/ppermute | solution.py:39
  153.5 16.3 %collective-permute-start = (bf16[128,1024]{1,0:T(8,128)(2,1)}, bf16[128,1024]{1,0:T(8,128)(2,1)}, u32[]{:S(2)}, u32[]{:S(2)}) collective-permute-start(bf16[128,1024]{1,0:T(8,128)(2,1)} %get-tuple-element.60), channel_id=1, source_target_pairs={{0,2},{1,3},{2,0},{3,1},{4,6},{5,7},{6,4},{7,5},{8,10},{9,11},{10,... | collective-permute-start | bytes 786440 | tf_op jit(solution)/shard_map/cond/branch_1_fun/ppermute | solution.py:39
  172.5 15.9 %collective-permute-start.37 = (bf16[2,168,896]{2,1,0:T(8,128)(2,1)}, bf16[2,168,896]{2,1,0:T(8,128)(2,1)S(1)}, u32[]{:S(2)}, u32[]{:S(2)}) collective-permute-start(bf16[2,168,896]{2,1,0:T(8,128)(2,1)} %get-tuple-element.279), channel_id=1, source_target_pairs={{0,16},{1,17},{2,18},{3,19},{4,20},{5,21},{6,22},{7,23},{8,24},{9,... | collective-permute-start | bytes 1806344 | tf_op jit(solution)/shard_map/ppermute | solution.py:39
  173.4 16.7 %collective-permute-start.38 = (bf16[2,168,896]{2,1,0:T(8,128)(2,1)}, bf16[2,168,896]{2,1,0:T(8,128)(2,1)S(1)}, u32[]{:S(2)}, u32[]{:S(2)}) collective-permute-start(bf16[2,168,896]{2,1,0:T(8,128)(2,1)} %get-tuple-element.281), channel_id=1, source_target_pairs={{0,8},{1,9},{2,10},{3,11},{4,12},{5,13},{6,14},{7,15},{8,0},{9,1},... | collective-permute-start | bytes 1806344 | tf_op jit(solution)/shard_map/ppermute | solution.py:39
  174.7 19.5 %collective-permute-start.35 = (bf16[128,1536]{1,0:T(8,128)(2,1)S(1)}, bf16[128,1536]{1,0:T(8,128)(2,1)S(1)}, u32[]{:S(2)}, u32[]{:S(2)}) collective-permute-start(bf16[128,1536]{1,0:T(8,128)(2,1)S(1)} %get-tuple-element.270), channel_id=1, source_target_pairs={{0,2},{1,3},{2,0},{3,1},{4,6},{5,7},{6,4},{7,5},{8,10},{9,11},{10,... | collective-permute-start | bytes 1179656 | tf_op jit(solution)/shard_map/ppermute | solution.py:39
  176.5 33.3 %collective-permute-start.43 = (bf16[192,1408]{1,0:T(8,128)(2,1)S(1)}, bf16[192,1408]{1,0:T(8,128)(2,1)S(1)}, u32[]{:S(2)}, u32[]{:S(2)}) collective-permute-start(bf16[192,1408]{1,0:T(8,128)(2,1)S(1)} %shard_map.253), channel_id=1, source_target_pairs={{0,4},{1,5},{2,6},{3,7},{4,0},{5,1},{6,2},{7,3},{8,12},{9,13},{10,... | collective-permute-start | bytes 1622024 | tf_op jit(solution)/shard_map/ppermute | solution.py:39
  178.3 31.5 %collective-permute-start.42 = (bf16[192,1408]{1,0:T(8,128)(2,1)S(1)}, bf16[192,1408]{1,0:T(8,128)(2,1)S(1)}, u32[]{:S(2)}, u32[]{:S(2)}) collective-permute-start(bf16[192,1408]{1,0:T(8,128)(2,1)S(1)} %get-tuple-element.288), channel_id=1, source_target_pairs={{0,8},{1,9},{2,10},{3,11},{4,12},{5,13},{6,14},{7,15},{8,0},{9,1},... | collective-permute-start | bytes 1622024 | tf_op jit(solution)/shard_map/ppermute | solution.py:39
  191.7 22.1 %collective-permute-start.40 = (bf16[168,896]{1,0:T(8,128)(2,1)S(1)}, bf16[168,896]{1,0:T(8,128)(2,1)S(1)}, u32[]{:S(2)}, u32[]{:S(2)}) collective-permute-start(bf16[168,896]{1,0:T(8,128)(2,1)S(1)} %get-tuple-element.286), channel_id=1, source_target_pairs={{0,16},{1,17},{2,18},{3,19},{4,20},{5,21},{6,22},{7,23},{8,24},{9,... | collective-permute-start | bytes 903176 | tf_op jit(solution)/shard_map/ppermute | solution.py:39
  195.1 18.7 %collective-permute-start.36 = (bf16[64,2048]{1,0:T(8,128)(2,1)S(1)}, bf16[64,2048]{1,0:T(8,128)(2,1)S(1)}, u32[]{:S(2)}, u32[]{:S(2)}) collective-permute-start(bf16[64,2048]{1,0:T(8,128)(2,1)S(1)} %get-tuple-element.273), channel_id=1, source_target_pairs={{0,4},{1,5},{2,6},{3,7},{4,0},{5,1},{6,2},{7,3},{8,12},{9,13},{10,... | collective-permute-start | bytes 786440 | tf_op jit(solution)/shard_map/ppermute | solution.py:39
  (52 other events, 434.9 us)

commit v6 on v5

--- a/solution.py
+++ b/solution.py
@@ -790,13 +790,6 @@
     cs = jnp.cos(angles)
     sn = jnp.sin(angles) * jnp.where(lane % HD < HD // 2, -1.0, 1.0)[None, :]
 
-    xv_out, v_keep = call(pack_second, (shape((M, D + 2 * HT)), shape((2, M, HT))), [SMEM] + [ANY] * 3,
-                          (ids, layer_in, first_layer_value, xv_moved), [pltpu.VMEM((M, D), BF16), pltpu.SemaphoreType.DMA((4,))], mib=63)
-    x_two, v_two = call(pack_third, (shape((HALF, D + HT)), shape((HALF, HT))), [VMEM] * 3, (xv_out, to_z(xv_out), v_keep))
-    x_core = to_core(x_two)
-    q_other, cs, sn, bias, _ = lax.optimization_barrier((q_other, cs, sn, bias, xv_out))
-    q_parts = spread(q_block, q_other, x_two)
-
     u_keep, u_send, d_block = call(
         pack_hidden, (shape((2, ROWS, 2 * FT)), shape((2, ROWS, 2 * FT)), shape((2 * ROWS, 2 * FT))), [SMEM] + [ANY] * 3,
         (after_these(ids, q_send), w_gate, w_up, w_down),
@@ -805,6 +798,14 @@
     u_first = to_z(u_send)
     u_last = to_core(pair_of(u_keep, after_these(u_first, q_block)))
     u_block = block_of(u_keep, u_first, u_last, d_block)
+
+    xv_out, v_keep = call(pack_second, (shape((M, D + 2 * HT)), shape((2, M, HT))), [SMEM] + [ANY] * 3,
+                          (after_these(ids, u_block), layer_in, first_layer_value, xv_moved), [pltpu.VMEM((M, D), BF16), pltpu.SemaphoreType.DMA((4,))], mib=63)
+    x_two, v_two = call(pack_third, (shape((HALF, D + HT)), shape((HALF, HT))), [VMEM] * 3, (xv_out, to_z(xv_out), v_keep))
+    x_core = to_core(x_two)
+    q_other, cs, sn, bias, _ = lax.optimization_barrier((q_other, cs, sn, bias, xv_out))
+    q_parts = spread(q_block, q_other, x_two)
+
     u_other = to_h(after_these(u_block, q_block))
     c_moved = to_h(after_these(c_send, u_other))
     u_a = jnp.stack([u_block, to_x(after_these(u_block, q_parts[2]))])

time: 243 us -> 242 us (level)
  starting transfers between devices: 43.5 us -> 46 us
    ppermute x48, starting transfers between devices: 43.5 us -> 46 us  [send(): return lax.ppermute(array, ALL, pairs)]
  transfers between devices with their start and end apart: 48 -> 48, of which waited for: 26 -> 23; matrix products, arithmetic and copies ran while one was open for 3% -> 3% of each run, Pallas kernels for 23% -> 23%
where the time goes in v6:
time: 242 us; the launch traced here: 241 us
  waiting for transfers between devices  103 us (43%)
  Pallas kernels  75.8 us (31%)
  starting transfers between devices  46 us (19%)
  local copies, waits for them, and re-layouts  8.94 us (4%)
  other arithmetic  6.03 us (2%)
    ppermute x48, waiting for transfers between devices, send(): return lax.ppermute(array, ALL, pairs)  103 us
    pallas_call x31, Pallas kernels, call(): pl.pallas_call(kernel, out_shape=outs, in_specs=specs, out_specs=jax.tree...  75.8 us
    ppermute x48, starting transfers between devices, send(): return lax.ppermute(array, ALL, pairs)  46 us
    unnamed x53, local copies, waits for them, and re-layouts  6.67 us
  transfers between devices with their start and end apart: 48, of which 23 were waited for; matrix products, arithmetic and copies ran while one was open for 3% of the time, Pallas kernels for 23%

profile of v6, /device:TPU:0, one launch (start us, length us, event | category | flops | bytes accessed | tf_op | source)
XLA Modules:
  0.0 241.2 jit_solution(6704910670571170016)
XLA Ops:
  0.8 2.9 %shard_map.238 = (bf16[2,32,896]{2,1,0:T(8,128)(2,1)}, bf16[2,32,896]{2,1,0:T(8,128)(2,1)}, bf16[40,896]{1,0:T(8,128)(2,1)}, bf16[64,2048]{1,0:T(8,128)(2,1)}, bf16[64,1024]{1,0:T(8,128)(2,1)}) custom-call(s32[3]{0:T(128)S(1)} %pad_add_fusion.ids, bf16[1,32]{1,0:T(2,128)(2,1)} %bitcast.23, bf16[1,32]{1,0:T(2,128)(2,1)} %bitcast.24, bf16[32,1024]{1,0:T(8,128)(2,1)} %wq.1, ...), custom_call_target="tpu_custom_call" | custom-call | flops 1 | bytes 1 | tf_op jit(solution)/shard_map/pallas_call | solution.py:305
  3.7 3.1 %collective-permute-start.5 = (bf16[2,32,896]{2,1,0:T(8,128)(2,1)}, bf16[2,32,896]{2,1,0:T(8,128)(2,1)S(1)}, u32[]{:S(2)}, u32[]{:S(2)}) collective-permute-start(bf16[2,32,896]{2,1,0:T(8,128)(2,1)} %get-tuple-element.200), channel_id=1, source_target_pairs={{0,2},{1,3},{2,0},{3,1},{4,6},{5,7},{6,4},{7,5},{8,10},{9,11},{10,... | collective-permute-start | bytes 344072 | tf_op jit(solution)/shard_map/ppermute | solution.py:39
  6.8 2.6 %collective-permute-start.8 = (bf16[64,2048]{1,0:T(8,128)(2,1)}, bf16[64,2048]{1,0:T(8,128)(2,1)}, u32[]{:S(2)}, u32[]{:S(2)}) collective-permute-start(bf16[64,2048]{1,0:T(8,128)(2,1)} %get-tuple-element.209), channel_id=1, source_target_pairs={{0,4},{1,5},{2,6},{3,7},{4,0},{5,1},{6,2},{7,3},{8,12},{9,13},{10,... | collective-permute-start | bytes 786440 | tf_op jit(solution)/shard_map/ppermute | solution.py:39
  9.4 2.7 %shard_map.239 = (bf16[2,32,1408]{2,1,0:T(8,128)(2,1)}, bf16[2,32,1408]{2,1,0:T(8,128)(2,1)}, bf16[64,1408]{1,0:T(8,128)(2,1)}) custom-call(s32[3]{0:T(128)S(1)} %pad_add_fusion.ids, bf16[32,2816]{1,0:T(8,128)(2,1)} %wg.1, bf16[32,2816]{1,0:T(8,128)(2,1)} %wu.1, bf16[88,1024]{1,0:T(8,128)(2,1)} %wd.1), custom_call_target="tpu_custom_call" | custom-call | flops 1 | bytes 1 | tf_op jit(solution)/shard_map/pallas_call | solution.py:305
  20.7 3.1 %fusion = (f32[512,256]{1,0:T(8,128)}, f32[512,256]{1,0:T(8,128)}) fusion(f32[256]{0:T(256)S(1)} %get-tuple-element.309, f32[256]{0:T(256)S(1)} %get-tuple-element.310, f32[512]{0:T(512)S(1)} %subtract_convert_fusion), kind=kLoop, calls=%fused_computation.10 | loop fusion | flops 262144 | bytes 1052672 | tf_op jit(solution)/shard_map/mul | solution.py:791
  29.6 5.7 %collective-permute-done.11 = bf16[168,896]{1,0:T(8,128)(2,1)} collective-permute-done((bf16[168,896]{1,0:T(8,128)(2,1)S(1)}, bf16[168,896]{1,0:T(8,128)(2,1)}, u32[]{:S(2)}, u32[]{:S(2)}) %collective-permute-start.11) | collective-permute-done | bytes 301088 | tf_op jit(solution)/shard_map/ppermute | solution.py:39
  37.9 7.0 %collective-permute-done.9.moved = bf16[128,1536]{1,0:T(8,128)(2,1)S(1)} collective-permute-done((bf16[128,1536]{1,0:T(8,128)(2,1)}, bf16[128,1536]{1,0:T(8,128)(2,1)S(1)}, u32[]{:S(2)}, u32[]{:S(2)}) %collective-permute-start.9) | collective-permute-done | bytes 393248 | tf_op jit(solution)/shard_map/ppermute | solution.py:39
  50.6 11.6 %collective-permute-done.17 = bf16[192,1408]{1,0:T(8,128)(2,1)S(1)} collective-permute-done((bf16[192,1408]{1,0:T(8,128)(2,1)S(1)}, bf16[192,1408]{1,0:T(8,128)(2,1)S(1)}, u32[]{:S(2)}, u32[]{:S(2)}) %collective-permute-start.17) | collective-permute-done | bytes 540704 | tf_op jit(solution)/shard_map/ppermute | solution.py:39
  67.6 7.9 %collective-permute-done.16 = bf16[192,1408]{1,0:T(8,128)(2,1)S(1)} collective-permute-done((bf16[192,1408]{1,0:T(8,128)(2,1)S(1)}, bf16[192,1408]{1,0:T(8,128)(2,1)S(1)}, u32[]{:S(2)}, u32[]{:S(2)}) %collective-permute-start.16) | collective-permute-done | bytes 540704 | tf_op jit(solution)/shard_map/ppermute | solution.py:39
  78.1 9.8 %shard_map.247 = (bf16[1024,896]{1,0:T(8,128)(2,1)}, bf16[512,1024]{1,0:T(8,128)(2,1)}, bf16[512,768]{1,0:T(8,128)(2,1)}, f32[512,256]{1,0:T(8,128)}, bf16[512,2...) custom-call(s32[3]{0:T(128)S(1)} %pad_add_fusion.ids, bf16[256,1280]{1,0:T(8,128)(2,1)S(1)} %get-tuple-element.212.x2, ...), custom_call_target="tpu_custom_call" | custom-call | flops 1 | bytes 1 | tf_op jit(solution)/shard_map/pallas_call | solution.py:305
  89.9 6.9 %collective-permute-done.21 = bf16[512,256]{1,0:T(8,128)(2,1)S(1)} collective-permute-done((bf16[512,256]{1,0:T(8,128)(2,1)S(1)}, bf16[512,256]{1,0:T(8,128)(2,1)S(1)}, u32[]{:S(2)}, u32[]{:S(2)}) %collective-permute-start.21) | collective-permute-done | bytes 262176 | tf_op jit(solution)/shard_map/ppermute | solution.py:39
  98.9 6.7 %shard_map.248 = (bf16[512,1024]{1,0:T(8,128)(2,1)}, f32[128,1024]{1,0:T(8,128)}, bf16[512,1024]{1,0:T(8,128)(2,1)S(1)}, bf16[256,1024]{1,0:T(8,128)(2,1)}) custom-call(s32[3]{0:T(128)S(1)} %pad_add_fusion.ids, bf16[256,1280]{1,0:T(8,128)(2,1)S(1)} %get-tuple-element.212.x2, bf16[256,1280]{1,0:T(8,128)(2,1)S(1)} %collective-permute-done.10.xc, ...), custom_call_target="tpu_custom_call" | custom-call | flops 1 | bytes 1 | tf_op jit(solution)/shard_map/pallas_call | solution.py:305
  107.0 13.1 %shard_map.249 = (bf16[256,1024]{1,0:T(8,128)(2,1)}, bf16[256,1024]{1,0:T(8,128)(2,1)}, bf16[256,1024]{1,0:T(8,128)(2,1)}, bf16[256,1024]{1,0:T(8,128)(2,1)}, f3...) custom-call(s32[3]{0:T(128)S(1)} %pad_add_fusion.ids, ...), custom_call_target="tpu_custom_call" | custom-call | flops 1 | bytes 1 | tf_op jit(solution)/shard_map/pallas_call | solution.py:305
  127.1 21.5 %conditional.2 = (f32[128,1024]{1,0:T(8,128)}, bf16[256,1024]{1,0:T(8,128)(2,1)}, bf16[256,1024]{1,0:T(8,128)(2,1)}, f32[128,1024]{1,0:T(8,128)}, bf16[128,1024]{1,0:T(8,128)(2,1)}) conditional(s32[]{:T(128)} %convert_element_type.21, () %tuple.46, (bf16[256,1024]{1,0:T(8,128)(2,1)}, bf16[256,1024]{1,0:T(8,128)(2,1)}, f32[128,1024]{1,0:T(8,128)}, ...), branch_computations={%region_1.2_spmd, %region_2.3_spmd} | conditional | flops 3 | bytes 9437403 | solution.py:753
  130.2 6.6 %collective-permute-done.1.moved = bf16[128,1024]{1,0:T(8,128)(2,1)S(1)} collective-permute-done((bf16[128,1024]{1,0:T(8,128)(2,1)S(1)}, bf16[128,1024]{1,0:T(8,128)(2,1)S(1)}, u32[]{:S(2)}, u32[]{:S(2)}) %collective-permute-start.1) | collective-permute-done | bytes 262176 | tf_op jit(solution)/shard_map/cond/branch_1_fun/ppermute | solution.py:39
  140.4 5.2 %collective-permute-done.2 = bf16[128,1024]{1,0:T(8,128)(2,1)S(1)} collective-permute-done((bf16[128,1024]{1,0:T(8,128)(2,1)S(1)}, bf16[128,1024]{1,0:T(8,128)(2,1)S(1)}, u32[]{:S(2)}, u32[]{:S(2)}) %collective-permute-start.2) | collective-permute-done | bytes 262176 | tf_op jit(solution)/shard_map/cond/branch_1_fun/ppermute | solution.py:39
  149.8 2.6 %shard_map.250 = (bf16[192,1408]{1,0:T(8,128)(2,1)S(1)}, bf16[192,1408]{1,0:T(8,128)(2,1)S(1)}, bf16[192,1408]{1,0:T(8,128)(2,1)S(1)}, bf16[192,1408]{1,0:T(8,128)(2,1)}) custom-call(bf16[2,192,1408]{2,1,0:T(8,128)(2,1)S(1)} %get-tuple-element.249.a_keep, bf16[2,192,1408]{2,1,0:T(8,128)(2,1)} %collective-permute-done.30.a_moved, ...), custom_call_target="tpu_custom_call" | custom-call | flops 1 | bytes 1 | tf_op jit(solution)/shard_map/pallas_call | solution.py:305
  153.6 17.3 %conditional.3 = (bf16[128,1024]{1,0:T(8,128)(2,1)}, bf16[256,1024]{1,0:T(8,128)(2,1)}, bf16[256,1280]{1,0:T(8,128)(2,1)}, bf16[256,256]{1,0:T(8,128)(2,1)S(1)},...) conditional(s32[]{:T(128)} %convert_element_type.21, () %tuple.62, ...), branch_computations={%region_3.4_spmd, %region_4.5_spmd} | conditional | flops 1 | bytes 3981392 | solution.py:753
  155.4 15.6 %branch_1_fun.7 = (bf16[256,1024]{1,0:T(8,128)(2,1)}, bf16[256,1280]{1,0:T(8,128)(2,1)}, bf16[256,256]{1,0:T(8,128)(2,1)S(1)}, bf16[2,168,896]{2,1,0:T(8,128)(2,...) custom-call(s32[3]{0:T(128)S(1)} %get-tuple-element.61.ids, ...), custom_call_target="tpu_custom_call" | custom-call | flops 1 | bytes 1 | tf_op jit(solution)/shard_map/cond/branch_1_fun/pallas_call | solution.py:305
  178.1 11.4 %collective-permute-done.37.a_moved = bf16[2,168,896]{2,1,0:T(8,128)(2,1)S(1)} collective-permute-done((bf16[2,168,896]{2,1,0:T(8,128)(2,1)}, bf16[2,168,896]{2,1,0:T(8,128)(2,1)S(1)}, u32[]{:S(2)}, u32[]{:S(2)}) %collective-permute-start.37) | collective-permute-done | bytes 602144 | tf_op jit(solution)/shard_map/ppermute | solution.py:39
  195.9 12.9 %collective-permute-done.43.moved = bf16[192,1408]{1,0:T(8,128)(2,1)S(1)} collective-permute-done((bf16[192,1408]{1,0:T(8,128)(2,1)S(1)}, bf16[192,1408]{1,0:T(8,128)(2,1)S(1)}, u32[]{:S(2)}, u32[]{:S(2)}) %collective-permute-start.43) | collective-permute-done | bytes 540704 | tf_op jit(solution)/shard_map/ppermute | solution.py:39
  214.9 3.4 %collective-permute-done.44.first = bf16[2,32,1408]{2,1,0:T(8,128)(2,1)S(1)} collective-permute-done((bf16[2,32,1408]{2,1,0:T(8,128)(2,1)S(1)}, bf16[2,32,1408]{2,1,0:T(8,128)(2,1)S(1)}, u32[]{:S(2)}, u32[]{:S(2)}) %collective-permute-start.44) | collective-permute-done | bytes 180256 | tf_op jit(solution)/shard_map/ppermute | solution.py:39
  221.9 5.7 %collective-permute-done.41.moved = bf16[168,896]{1,0:T(8,128)(2,1)S(1)} collective-permute-done((bf16[168,896]{1,0:T(8,128)(2,1)S(1)}, bf16[168,896]{1,0:T(8,128)(2,1)S(1)}, u32[]{:S(2)}, u32[]{:S(2)}) %collective-permute-start.41) | collective-permute-done | bytes 301088 | tf_op jit(solution)/shard_map/ppermute | solution.py:39
  235.2 2.7 %collective-permute-done.32.moved = bf16[64,1024]{1,0:T(8,128)(2,1)S(1)} collective-permute-done((bf16[64,1024]{1,0:T(8,128)(2,1)S(1)}, bf16[64,1024]{1,0:T(8,128)(2,1)S(1)}, u32[]{:S(2)}, u32[]{:S(2)}) %collective-permute-start.32) | collective-permute-done | bytes 131104 | tf_op jit(solution)/shard_map/ppermute | solution.py:39
  (186 shorter events, 91.0 us)
Async XLA Ops:
  6.8 17.8 %collective-permute-start.8 = (bf16[64,2048]{1,0:T(8,128)(2,1)}, bf16[64,2048]{1,0:T(8,128)(2,1)}, u32[]{:S(2)}, u32[]{:S(2)}) collective-permute-start(bf16[64,2048]{1,0:T(8,128)(2,1)} %get-tuple-element.209), channel_id=1, source_target_pairs={{0,4},{1,5},{2,6},{3,7},{4,0},{5,1},{6,2},{7,3},{8,12},{9,13},{10,... | collective-permute-start | bytes 786440 | tf_op jit(solution)/shard_map/ppermute | solution.py:39
  17.3 19.6 %collective-permute-start.12 = (bf16[168,896]{1,0:T(8,128)(2,1)S(1)}, bf16[168,896]{1,0:T(8,128)(2,1)}, u32[]{:S(2)}, u32[]{:S(2)}) collective-permute-start(bf16[168,896]{1,0:T(8,128)(2,1)S(1)} %shard_map.241), channel_id=1, source_target_pairs={{0,8},{1,9},{2,10},{3,11},{4,12},{5,13},{6,14},{7,15},{8,0},{9,1},... | collective-permute-start | bytes 903176 | tf_op jit(solution)/shard_map/ppermute | solution.py:39
  18.8 16.5 %collective-permute-start.11 = (bf16[168,896]{1,0:T(8,128)(2,1)S(1)}, bf16[168,896]{1,0:T(8,128)(2,1)}, u32[]{:S(2)}, u32[]{:S(2)}) collective-permute-start(bf16[168,896]{1,0:T(8,128)(2,1)S(1)} %shard_map.241), channel_id=1, source_target_pairs={{0,4},{1,5},{2,6},{3,7},{4,0},{5,1},{6,2},{7,3},{8,12},{9,13},{10,... | collective-permute-start | bytes 903176 | tf_op jit(solution)/shard_map/ppermute | solution.py:39
  27.1 17.9 %collective-permute-start.9 = (bf16[128,1536]{1,0:T(8,128)(2,1)}, bf16[128,1536]{1,0:T(8,128)(2,1)S(1)}, u32[]{:S(2)}, u32[]{:S(2)}) collective-permute-start(bf16[128,1536]{1,0:T(8,128)(2,1)} %get-tuple-element.210.mine), channel_id=1, source_target_pairs={{0,2},{1,3},{2,0},{3,1},{4,6},{5,7},{6,4},{7,5},{8,10},{9,11},{10,... | collective-permute-start | bytes 1179656 | tf_op jit(solution)/shard_map/ppermute | solution.py:39
  36.8 25.3 %collective-permute-start.17 = (bf16[192,1408]{1,0:T(8,128)(2,1)S(1)}, bf16[192,1408]{1,0:T(8,128)(2,1)S(1)}, u32[]{:S(2)}, u32[]{:S(2)}) collective-permute-start(bf16[192,1408]{1,0:T(8,128)(2,1)S(1)} %shard_map.243), channel_id=1, source_target_pairs={{0,4},{1,5},{2,6},{3,7},{4,0},{5,1},{6,2},{7,3},{8,12},{9,13},{10,... | collective-permute-start | bytes 1622024 | tf_op jit(solution)/shard_map/ppermute | solution.py:39
  46.0 16.7 %collective-permute-start.14 = (bf16[2,168,896]{2,1,0:T(8,128)(2,1)S(1)}, bf16[2,168,896]{2,1,0:T(8,128)(2,1)S(1)}, u32[]{:S(2)}, u32[]{:S(2)}) collective-permute-start(bf16[2,168,896]{2,1,0:T(8,128)(2,1)S(1)} %pad_maximum_fusion.3.b0), channel_id=1, source_target_pairs={{0,16},{1,17},{2,18},{3,19},{4,20},{5,21},{6,22},{7,23},{8,24},{9,... | collective-permute-start | bytes 1806344 | tf_op jit(solution)/shard_map/ppermute | solution.py:39
  48.6 16.5 %collective-permute-start.15 = (bf16[2,168,896]{2,1,0:T(8,128)(2,1)S(1)}, bf16[2,168,896]{2,1,0:T(8,128)(2,1)S(1)}, u32[]{:S(2)}, u32[]{:S(2)}) collective-permute-start(bf16[2,168,896]{2,1,0:T(8,128)(2,1)S(1)} %pad_maximum_fusion.4.b2), channel_id=1, source_target_pairs={{0,8},{1,9},{2,10},{3,11},{4,12},{5,13},{6,14},{7,15},{8,0},{9,1},... | collective-permute-start | bytes 1806344 | tf_op jit(solution)/shard_map/ppermute | solution.py:39
  50.1 25.4 %collective-permute-start.16 = (bf16[192,1408]{1,0:T(8,128)(2,1)S(1)}, bf16[192,1408]{1,0:T(8,128)(2,1)S(1)}, u32[]{:S(2)}, u32[]{:S(2)}) collective-permute-start(bf16[192,1408]{1,0:T(8,128)(2,1)S(1)} %shard_map.243), channel_id=1, source_target_pairs={{0,8},{1,9},{2,10},{3,11},{4,12},{5,13},{6,14},{7,15},{8,0},{9,1},... | collective-permute-start | bytes 1622024 | tf_op jit(solution)/shard_map/ppermute | solution.py:39
  62.7 15.3 %collective-permute-start.10 = (bf16[256,1280]{1,0:T(8,128)(2,1)S(1)}, bf16[256,1280]{1,0:T(8,128)(2,1)S(1)}, u32[]{:S(2)}, u32[]{:S(2)}) collective-permute-start(bf16[256,1280]{1,0:T(8,128)(2,1)S(1)} %get-tuple-element.212.x2), channel_id=1, source_target_pairs={{0,1},{1,0},{2,3},{3,2},{4,5},{5,4},{6,7},{7,6},{8,9},{9,8},{10,11... | collective-permute-start | bytes 1966088 | tf_op jit(solution)/shard_map/ppermute | solution.py:39
  65.9 22.0 %collective-permute-start.23 = (bf16[256,1024]{1,0:T(8,128)(2,1)S(1)}, bf16[256,1024]{1,0:T(8,128)(2,1)S(1)}, u32[]{:S(2)}, u32[]{:S(2)}) collective-permute-start(bf16[256,1024]{1,0:T(8,128)(2,1)S(1)} %shard_map.246), channel_id=1, source_target_pairs={{0,2},{1,3},{2,0},{3,1},{4,6},{5,7},{6,4},{7,5},{8,10},{9,11},{10,... | collective-permute-start | bytes 1572872 | tf_op jit(solution)/shard_map/ppermute | solution.py:39
  75.6 30.0 %collective-permute-start.26 = (bf16[2,192,1408]{2,1,0:T(8,128)(2,1)S(1)}, bf16[2,192,1408]{2,1,0:T(8,128)(2,1)S(1)}, u32[]{:S(2)}, u32[]{:S(2)}) collective-permute-start(bf16[2,192,1408]{2,1,0:T(8,128)(2,1)S(1)} %pad_maximum_fusion.u0), channel_id=1, source_target_pairs={{0,16},{1,17},{2,18},{3,19},{4,20},{5,21},{6,22},{7,23},{8,24},{9,... | collective-permute-start | bytes 3244040 | tf_op jit(solution)/shard_map/ppermute | solution.py:39
  76.6 29.0 %collective-permute-start.27 = (bf16[2,192,1408]{2,1,0:T(8,128)(2,1)S(1)}, bf16[2,192,1408]{2,1,0:T(8,128)(2,1)S(1)}, u32[]{:S(2)}, u32[]{:S(2)}) collective-permute-start(bf16[2,192,1408]{2,1,0:T(8,128)(2,1)S(1)} %pad_maximum_fusion.1.u2), channel_id=1, source_target_pairs={{0,8},{1,9},{2,10},{3,11},{4,12},{5,13},{6,14},{7,15},{8,0},{9,1},... | collective-permute-start | bytes 3244040 | tf_op jit(solution)/shard_map/ppermute | solution.py:39
  121.0 27.5 %collective-permute-start.31 = (bf16[2,192,1408]{2,1,0:T(8,128)(2,1)}, bf16[2,192,1408]{2,1,0:T(8,128)(2,1)}, u32[]{:S(2)}, u32[]{:S(2)}) collective-permute-start(bf16[2,192,1408]{2,1,0:T(8,128)(2,1)} %get-tuple-element.248), channel_id=1, source_target_pairs={{0,8},{1,9},{2,10},{3,11},{4,12},{5,13},{6,14},{7,15},{8,0},{9,1},... | collective-permute-start | bytes 3244040 | tf_op jit(solution)/shard_map/ppermute | solution.py:39
  122.4 26.2 %collective-permute-start.30 = (bf16[2,192,1408]{2,1,0:T(8,128)(2,1)S(1)}, bf16[2,192,1408]{2,1,0:T(8,128)(2,1)}, u32[]{:S(2)}, u32[]{:S(2)}) collective-permute-start(bf16[2,192,1408]{2,1,0:T(8,128)(2,1)S(1)} %get-tuple-element.237), channel_id=1, source_target_pairs={{0,16},{1,17},{2,18},{3,19},{4,20},{5,21},{6,22},{7,23},{8,24},{9,... | collective-permute-start | bytes 3244040 | tf_op jit(solution)/shard_map/ppermute | solution.py:39
  152.4 18.6 %collective-permute-start.33 = (bf16[192,1408]{1,0:T(8,128)(2,1)}, bf16[192,1408]{1,0:T(8,128)(2,1)S(1)}, u32[]{:S(2)}, u32[]{:S(2)}) collective-permute-start(bf16[192,1408]{1,0:T(8,128)(2,1)} %get-tuple-element.253), channel_id=1, source_target_pairs={{0,16},{1,17},{2,18},{3,19},{4,20},{5,21},{6,22},{7,23},{8,24},{9,... | collective-permute-start | bytes 1622024 | tf_op jit(solution)/shard_map/ppermute | solution.py:39
  153.6 17.3 %collective-permute-start = (bf16[128,1024]{1,0:T(8,128)(2,1)}, bf16[128,1024]{1,0:T(8,128)(2,1)}, u32[]{:S(2)}, u32[]{:S(2)}) collective-permute-start(bf16[128,1024]{1,0:T(8,128)(2,1)} %get-tuple-element.60), channel_id=1, source_target_pairs={{0,2},{1,3},{2,0},{3,1},{4,6},{5,7},{6,4},{7,5},{8,10},{9,11},{10,... | collective-permute-start | bytes 786440 | tf_op jit(solution)/shard_map/cond/branch_1_fun/ppermute | solution.py:39
  173.6 15.9 %collective-permute-start.37 = (bf16[2,168,896]{2,1,0:T(8,128)(2,1)}, bf16[2,168,896]{2,1,0:T(8,128)(2,1)S(1)}, u32[]{:S(2)}, u32[]{:S(2)}) collective-permute-start(bf16[2,168,896]{2,1,0:T(8,128)(2,1)} %get-tuple-element.281), channel_id=1, source_target_pairs={{0,16},{1,17},{2,18},{3,19},{4,20},{5,21},{6,22},{7,23},{8,24},{9,... | collective-permute-start | bytes 1806344 | tf_op jit(solution)/shard_map/ppermute | solution.py:39
  174.5 16.7 %collective-permute-start.38 = (bf16[2,168,896]{2,1,0:T(8,128)(2,1)}, bf16[2,168,896]{2,1,0:T(8,128)(2,1)S(1)}, u32[]{:S(2)}, u32[]{:S(2)}) collective-permute-start(bf16[2,168,896]{2,1,0:T(8,128)(2,1)} %get-tuple-element.283), channel_id=1, source_target_pairs={{0,8},{1,9},{2,10},{3,11},{4,12},{5,13},{6,14},{7,15},{8,0},{9,1},... | collective-permute-start | bytes 1806344 | tf_op jit(solution)/shard_map/ppermute | solution.py:39
  175.1 18.9 %collective-permute-start.35 = (bf16[128,1536]{1,0:T(8,128)(2,1)S(1)}, bf16[128,1536]{1,0:T(8,128)(2,1)S(1)}, u32[]{:S(2)}, u32[]{:S(2)}) collective-permute-start(bf16[128,1536]{1,0:T(8,128)(2,1)S(1)} %get-tuple-element.272), channel_id=1, source_target_pairs={{0,2},{1,3},{2,0},{3,1},{4,6},{5,7},{6,4},{7,5},{8,10},{9,11},{10,... | collective-permute-start | bytes 1179656 | tf_op jit(solution)/shard_map/ppermute | solution.py:39
  175.4 33.3 %collective-permute-start.43 = (bf16[192,1408]{1,0:T(8,128)(2,1)S(1)}, bf16[192,1408]{1,0:T(8,128)(2,1)S(1)}, u32[]{:S(2)}, u32[]{:S(2)}) collective-permute-start(bf16[192,1408]{1,0:T(8,128)(2,1)S(1)} %shard_map.253), channel_id=1, source_target_pairs={{0,4},{1,5},{2,6},{3,7},{4,0},{5,1},{6,2},{7,3},{8,12},{9,13},{10,... | collective-permute-start | bytes 1622024 | tf_op jit(solution)/shard_map/ppermute | solution.py:39
  177.1 31.6 %collective-permute-start.42 = (bf16[192,1408]{1,0:T(8,128)(2,1)S(1)}, bf16[192,1408]{1,0:T(8,128)(2,1)S(1)}, u32[]{:S(2)}, u32[]{:S(2)}) collective-permute-start(bf16[192,1408]{1,0:T(8,128)(2,1)S(1)} %get-tuple-element.290), channel_id=1, source_target_pairs={{0,8},{1,9},{2,10},{3,11},{4,12},{5,13},{6,14},{7,15},{8,0},{9,1},... | collective-permute-start | bytes 1622024 | tf_op jit(solution)/shard_map/ppermute | solution.py:39
  192.8 20.0 %collective-permute-start.40 = (bf16[168,896]{1,0:T(8,128)(2,1)S(1)}, bf16[168,896]{1,0:T(8,128)(2,1)S(1)}, u32[]{:S(2)}, u32[]{:S(2)}) collective-permute-start(bf16[168,896]{1,0:T(8,128)(2,1)S(1)} %get-tuple-element.288), channel_id=1, source_target_pairs={{0,16},{1,17},{2,18},{3,19},{4,20},{5,21},{6,22},{7,23},{8,24},{9,... | collective-permute-start | bytes 903176 | tf_op jit(solution)/shard_map/ppermute | solution.py:39
  195.0 17.8 %collective-permute-start.36 = (bf16[64,2048]{1,0:T(8,128)(2,1)S(1)}, bf16[64,2048]{1,0:T(8,128)(2,1)S(1)}, u32[]{:S(2)}, u32[]{:S(2)}) collective-permute-start(bf16[64,2048]{1,0:T(8,128)(2,1)S(1)} %get-tuple-element.275), channel_id=1, source_target_pairs={{0,4},{1,5},{2,6},{3,7},{4,0},{5,1},{6,2},{7,3},{8,12},{9,13},{10,... | collective-permute-start | bytes 786440 | tf_op jit(solution)/shard_map/ppermute | solution.py:39
  212.9 14.7 %collective-permute-start.41 = (bf16[168,896]{1,0:T(8,128)(2,1)S(1)}, bf16[168,896]{1,0:T(8,128)(2,1)S(1)}, u32[]{:S(2)}, u32[]{:S(2)}) collective-permute-start(bf16[168,896]{1,0:T(8,128)(2,1)S(1)} %shard_map.258), channel_id=1, source_target_pairs={{0,4},{1,5},{2,6},{3,7},{4,0},{5,1},{6,2},{7,3},{8,12},{9,13},{10,... | collective-permute-start | bytes 903176 | tf_op jit(solution)/shard_map/ppermute | solution.py:39
  (52 other events, 430.8 us)

commit v7 on v6

--- a/solution.py
+++ b/solution.py
@@ -466,24 +466,20 @@
             qkv[rows, i * HT:(i + 1) * HT] = (u * cs[rows] + swap_halves(u) * sn[rows]).astype(BF16)
         value = v2[...] if b == 0 else xc[:, D:]
         qkv[rows, 2 * HT:] = (0.5 * out[:, 2 * HT:] + 0.5 * value.astype(F32)).astype(BF16)
-    for b in range(2):
-        rows = slice(b * HALF, (b + 1) * HALF)
-        outs, tops = [], []
-        for i in range(4):
-            lanes = slice(i * HD, (i + 1) * HD)
-            q = qkv[rows, lanes]
-            k = qkv[:, HT + i * HD:HT + (i + 1) * HD]
-            v = qkv[:, 2 * HT + i * HD:2 * HT + (i + 1) * HD]
-            s = dot_cols(q, k) * SCALE + bias[rows].astype(F32)
-            top = jnp.max(s, axis=-1, keepdims=True)
-            p = jnp.exp(s - top)
-            total = jnp.sum(p, axis=-1, keepdims=True)
-            outs.append(dot(p.astype(BF16), v) / total)
-            tops.append(top + jnp.log(total))
-        o = jnp.concatenate(outs, axis=1)
-        attn[rows] = o
-        low[rows] = o.astype(BF16)
-        lse[rows] = jnp.concatenate(tops, axis=1)
+    outs, tops = [], []
+    mask = bias[...].astype(F32)
+    for i in range(4):
+        q, k, v = (qkv[:, n * HT + i * HD:n * HT + (i + 1) * HD] for n in range(3))
+        s = dot_cols(q, k) * SCALE + mask
+        top = jnp.max(s, axis=-1, keepdims=True)
+        p = jnp.exp(s - top)
+        total = jnp.sum(p, axis=-1, keepdims=True)
+        outs.append(dot(p.astype(BF16), v) / total)
+        tops.append(top + jnp.log(total))
+    o = jnp.concatenate(outs, axis=1)
+    attn[...] = o
+    low[...] = o.astype(BF16)
+    lse[...] = jnp.concatenate(tops, axis=1)
 
 
 def after_kernel(ids, x2, xc, o2, oc, gains, co2, coc, full, after, normed, own_w, w, sem):
@@ -588,26 +584,19 @@
     for b in range(2):
         rows = slice(b * HALF, (b + 1) * HALF)
         do[rows] = dot_cols((da2 if b == 0 else dac)[...], wo[...]).astype(BF16)
-    for b in range(2):
-        rows = slice(b * HALF, (b + 1) * HALF)
-        dqs = []
-        for i in range(4):
-            lanes = slice(i * HD, (i + 1) * HD)
-            q = qkv[rows, lanes]
-            k = qkv[:, HT + i * HD:HT + (i + 1) * HD]
-            v = qkv[:, 2 * HT + i * HD:2 * HT + (i + 1) * HD]
-            d = do[rows, lanes]
-            delta = jnp.sum(d.astype(F32) * attn[rows, lanes], axis=-1, keepdims=True)
-            p = jnp.exp(dot_cols(q, k) * SCALE + bias[rows].astype(F32) - lse[rows, i:i + 1])
-            ds = (p * (dot_cols(d, v) - delta)).astype(BF16)
-            dqs.append(dot(ds, k))
-            dki, dvi = dot_rows(ds, q), dot_rows(p.astype(BF16), d)
-            if b == 0:
-                dk[:, lanes], dv[:, lanes] = dki, dvi
-            else:
-                dk[:, lanes], dv[:, lanes] = dk[:, lanes] + dki, dv[:, lanes] + dvi
-        u = jnp.concatenate(dqs, axis=1) * SCALE
-        dqkv[rows, :HT] = (u * cs[rows] - swap_halves(u) * sn[rows]).astype(BF16)
+    dqs = []
+    mask = bias[...].astype(F32)
+    for i in range(4):
+        lanes = slice(i * HD, (i + 1) * HD)
+        q, k, v = (qkv[:, n * HT + i * HD:n * HT + (i + 1) * HD] for n in range(3))
+        d = do[:, lanes]
+        delta = jnp.sum(d.astype(F32) * attn[:, lanes], axis=-1, keepdims=True)
+        p = jnp.exp(dot_cols(q, k) * SCALE + mask - lse[:, i:i + 1])
+        ds = (p * (dot_cols(d, v) - delta)).astype(BF16)
+        dqs.append(dot(ds, k))
+        dk[:, lanes], dv[:, lanes] = dot_rows(ds, q), dot_rows(p.astype(BF16), d)
+    u = jnp.concatenate(dqs, axis=1) * SCALE
+    dqkv[:, :HT] = (u * cs[...] - swap_halves(u) * sn[...]).astype(BF16)
     gain_sum = jnp.zeros((1, D), F32)
     for b in range(2):
         rows = slice(b * HALF, (b + 1) * HALF)

time: 242 us -> 239 us (0.988)
  Pallas kernels: 75.8 us -> 73.1 us
    pallas_call x31, Pallas kernels: 75.8 us -> 73.1 us  [call(): pl.pallas_call(kernel, out_shape=outs, in_specs=specs, out_specs=jax.tree...]
  transfers between devices with their start and end apart: 48 -> 48, of which waited for: 23 -> 24; matrix products, arithmetic and copies ran while one was open for 3% -> 3% of each run, Pallas kernels for 23% -> 22%
where the time goes in v7:
time: 239 us
  waiting for transfers between devices  105 us (44%)
  Pallas kernels  73.1 us (31%)
  starting transfers between devices  44.6 us (19%)
  local copies, waits for them, and re-layouts  8.94 us (4%)
  other arithmetic  6.03 us (3%)
    ppermute x48, waiting for transfers between devices, send(): return lax.ppermute(array, ALL, pairs)  105 us
    pallas_call x31, Pallas kernels, call(): pl.pallas_call(kernel, out_shape=outs, in_specs=specs, out_specs=jax.tree...  73.1 us
    ppermute x48, starting transfers between devices, send(): return lax.ppermute(array, ALL, pairs)  44.6 us
    unnamed x53, local copies, waits for them, and re-layouts  6.67 us
  transfers between devices with their start and end apart: 48, of which 24 were waited for; matrix products, arithmetic and copies ran while one was open for 3% of the time, Pallas kernels for 22%

profile of v7, /device:TPU:0, one launch (start us, length us, event | category | flops | bytes accessed | tf_op | source)
XLA Modules:
  0.0 238.5 jit_solution(16943773161926042094)
XLA Ops:
  0.8 2.9 %shard_map.238 = (bf16[2,32,896]{2,1,0:T(8,128)(2,1)}, bf16[2,32,896]{2,1,0:T(8,128)(2,1)}, bf16[40,896]{1,0:T(8,128)(2,1)}, bf16[64,2048]{1,0:T(8,128)(2,1)}, bf16[64,1024]{1,0:T(8,128)(2,1)}) custom-call(s32[3]{0:T(128)S(1)} %pad_add_fusion.ids, bf16[1,32]{1,0:T(2,128)(2,1)} %bitcast.23, bf16[1,32]{1,0:T(2,128)(2,1)} %bitcast.24, bf16[32,1024]{1,0:T(8,128)(2,1)} %wq.1, ...), custom_call_target="tpu_custom_call" | custom-call | flops 1 | bytes 1 | tf_op jit(solution)/shard_map/pallas_call | solution.py:305
  3.7 3.1 %collective-permute-start.5 = (bf16[2,32,896]{2,1,0:T(8,128)(2,1)}, bf16[2,32,896]{2,1,0:T(8,128)(2,1)S(1)}, u32[]{:S(2)}, u32[]{:S(2)}) collective-permute-start(bf16[2,32,896]{2,1,0:T(8,128)(2,1)} %get-tuple-element.200), channel_id=1, source_target_pairs={{0,2},{1,3},{2,0},{3,1},{4,6},{5,7},{6,4},{7,5},{8,10},{9,11},{10,... | collective-permute-start | bytes 344072 | tf_op jit(solution)/shard_map/ppermute | solution.py:39
  6.8 2.6 %collective-permute-start.8 = (bf16[64,2048]{1,0:T(8,128)(2,1)}, bf16[64,2048]{1,0:T(8,128)(2,1)}, u32[]{:S(2)}, u32[]{:S(2)}) collective-permute-start(bf16[64,2048]{1,0:T(8,128)(2,1)} %get-tuple-element.209), channel_id=1, source_target_pairs={{0,4},{1,5},{2,6},{3,7},{4,0},{5,1},{6,2},{7,3},{8,12},{9,13},{10,... | collective-permute-start | bytes 786440 | tf_op jit(solution)/shard_map/ppermute | solution.py:39
  9.4 2.7 %shard_map.239 = (bf16[2,32,1408]{2,1,0:T(8,128)(2,1)}, bf16[2,32,1408]{2,1,0:T(8,128)(2,1)}, bf16[64,1408]{1,0:T(8,128)(2,1)}) custom-call(s32[3]{0:T(128)S(1)} %pad_add_fusion.ids, bf16[32,2816]{1,0:T(8,128)(2,1)} %wg.1, bf16[32,2816]{1,0:T(8,128)(2,1)} %wu.1, bf16[88,1024]{1,0:T(8,128)(2,1)} %wd.1), custom_call_target="tpu_custom_call" | custom-call | flops 1 | bytes 1 | tf_op jit(solution)/shard_map/pallas_call | solution.py:305
  20.7 3.1 %fusion = (f32[512,256]{1,0:T(8,128)}, f32[512,256]{1,0:T(8,128)}) fusion(f32[256]{0:T(256)S(1)} %get-tuple-element.309, f32[256]{0:T(256)S(1)} %get-tuple-element.310, f32[512]{0:T(512)S(1)} %subtract_convert_fusion), kind=kLoop, calls=%fused_computation.10 | loop fusion | flops 262144 | bytes 1052672 | tf_op jit(solution)/shard_map/mul | solution.py:780
  29.6 5.7 %collective-permute-done.11 = bf16[168,896]{1,0:T(8,128)(2,1)} collective-permute-done((bf16[168,896]{1,0:T(8,128)(2,1)S(1)}, bf16[168,896]{1,0:T(8,128)(2,1)}, u32[]{:S(2)}, u32[]{:S(2)}) %collective-permute-start.11) | collective-permute-done | bytes 301088 | tf_op jit(solution)/shard_map/ppermute | solution.py:39
  37.9 7.0 %collective-permute-done.9.moved = bf16[128,1536]{1,0:T(8,128)(2,1)S(1)} collective-permute-done((bf16[128,1536]{1,0:T(8,128)(2,1)}, bf16[128,1536]{1,0:T(8,128)(2,1)S(1)}, u32[]{:S(2)}, u32[]{:S(2)}) %collective-permute-start.9) | collective-permute-done | bytes 393248 | tf_op jit(solution)/shard_map/ppermute | solution.py:39
  50.6 11.6 %collective-permute-done.17 = bf16[192,1408]{1,0:T(8,128)(2,1)S(1)} collective-permute-done((bf16[192,1408]{1,0:T(8,128)(2,1)S(1)}, bf16[192,1408]{1,0:T(8,128)(2,1)S(1)}, u32[]{:S(2)}, u32[]{:S(2)}) %collective-permute-start.17) | collective-permute-done | bytes 540704 | tf_op jit(solution)/shard_map/ppermute | solution.py:39
  67.6 7.9 %collective-permute-done.16 = bf16[192,1408]{1,0:T(8,128)(2,1)S(1)} collective-permute-done((bf16[192,1408]{1,0:T(8,128)(2,1)S(1)}, bf16[192,1408]{1,0:T(8,128)(2,1)S(1)}, u32[]{:S(2)}, u32[]{:S(2)}) %collective-permute-start.16) | collective-permute-done | bytes 540704 | tf_op jit(solution)/shard_map/ppermute | solution.py:39
  78.1 8.1 %shard_map.247 = (bf16[1024,896]{1,0:T(8,128)(2,1)}, bf16[512,1024]{1,0:T(8,128)(2,1)}, bf16[512,768]{1,0:T(8,128)(2,1)}, f32[512,256]{1,0:T(8,128)}, bf16[512,2...) custom-call(s32[3]{0:T(128)S(1)} %pad_add_fusion.ids, bf16[256,1280]{1,0:T(8,128)(2,1)S(1)} %get-tuple-element.212.x2, ...), custom_call_target="tpu_custom_call" | custom-call | flops 1 | bytes 1 | tf_op jit(solution)/shard_map/pallas_call | solution.py:305
  88.3 6.9 %collective-permute-done.21 = bf16[512,256]{1,0:T(8,128)(2,1)S(1)} collective-permute-done((bf16[512,256]{1,0:T(8,128)(2,1)S(1)}, bf16[512,256]{1,0:T(8,128)(2,1)S(1)}, u32[]{:S(2)}, u32[]{:S(2)}) %collective-permute-start.21) | collective-permute-done | bytes 262176 | tf_op jit(solution)/shard_map/ppermute | solution.py:39
  97.3 6.7 %shard_map.248 = (bf16[512,1024]{1,0:T(8,128)(2,1)}, f32[128,1024]{1,0:T(8,128)}, bf16[512,1024]{1,0:T(8,128)(2,1)S(1)}, bf16[256,1024]{1,0:T(8,128)(2,1)}) custom-call(s32[3]{0:T(128)S(1)} %pad_add_fusion.ids, bf16[256,1280]{1,0:T(8,128)(2,1)S(1)} %get-tuple-element.212.x2, bf16[256,1280]{1,0:T(8,128)(2,1)S(1)} %collective-permute-done.10.xc, ...), custom_call_target="tpu_custom_call" | custom-call | flops 1 | bytes 1 | tf_op jit(solution)/shard_map/pallas_call | solution.py:305
  105.4 13.1 %shard_map.249 = (bf16[256,1024]{1,0:T(8,128)(2,1)}, bf16[256,1024]{1,0:T(8,128)(2,1)}, bf16[256,1024]{1,0:T(8,128)(2,1)}, bf16[256,1024]{1,0:T(8,128)(2,1)}, f3...) custom-call(s32[3]{0:T(128)S(1)} %pad_add_fusion.ids, ...), custom_call_target="tpu_custom_call" | custom-call | flops 1 | bytes 1 | tf_op jit(solution)/shard_map/pallas_call | solution.py:305
  125.4 21.5 %conditional.2 = (f32[128,1024]{1,0:T(8,128)}, bf16[256,1024]{1,0:T(8,128)(2,1)}, bf16[256,1024]{1,0:T(8,128)(2,1)}, f32[128,1024]{1,0:T(8,128)}, bf16[128,1024]{1,0:T(8,128)(2,1)}) conditional(s32[]{:T(128)} %convert_element_type.21, () %tuple.46, (bf16[256,1024]{1,0:T(8,128)(2,1)}, bf16[256,1024]{1,0:T(8,128)(2,1)}, f32[128,1024]{1,0:T(8,128)}, ...), branch_computations={%region_1.2_spmd, %region_2.3_spmd} | conditional | flops 3 | bytes 9437403 | solution.py:742
  128.6 6.6 %collective-permute-done.1.moved = bf16[128,1024]{1,0:T(8,128)(2,1)S(1)} collective-permute-done((bf16[128,1024]{1,0:T(8,128)(2,1)S(1)}, bf16[128,1024]{1,0:T(8,128)(2,1)S(1)}, u32[]{:S(2)}, u32[]{:S(2)}) %collective-permute-start.1) | collective-permute-done | bytes 262176 | tf_op jit(solution)/shard_map/cond/branch_1_fun/ppermute | solution.py:39
  138.8 5.2 %collective-permute-done.2 = bf16[128,1024]{1,0:T(8,128)(2,1)S(1)} collective-permute-done((bf16[128,1024]{1,0:T(8,128)(2,1)S(1)}, bf16[128,1024]{1,0:T(8,128)(2,1)S(1)}, u32[]{:S(2)}, u32[]{:S(2)}) %collective-permute-start.2) | collective-permute-done | bytes 262176 | tf_op jit(solution)/shard_map/cond/branch_1_fun/ppermute | solution.py:39
  148.2 2.6 %shard_map.250 = (bf16[192,1408]{1,0:T(8,128)(2,1)S(1)}, bf16[192,1408]{1,0:T(8,128)(2,1)S(1)}, bf16[192,1408]{1,0:T(8,128)(2,1)S(1)}, bf16[192,1408]{1,0:T(8,128)(2,1)}) custom-call(bf16[2,192,1408]{2,1,0:T(8,128)(2,1)S(1)} %get-tuple-element.249.a_keep, bf16[2,192,1408]{2,1,0:T(8,128)(2,1)} %collective-permute-done.30.a_moved, ...), custom_call_target="tpu_custom_call" | custom-call | flops 1 | bytes 1 | tf_op jit(solution)/shard_map/pallas_call | solution.py:305
  152.0 16.2 %conditional.3 = (bf16[128,1024]{1,0:T(8,128)(2,1)}, bf16[256,1024]{1,0:T(8,128)(2,1)}, bf16[256,1280]{1,0:T(8,128)(2,1)}, bf16[256,256]{1,0:T(8,128)(2,1)S(1)},...) conditional(s32[]{:T(128)} %convert_element_type.21, () %tuple.62, ...), branch_computations={%region_3.4_spmd, %region_4.5_spmd} | conditional | flops 1 | bytes 3981392 | solution.py:742
  153.7 14.5 %branch_1_fun.7 = (bf16[256,1024]{1,0:T(8,128)(2,1)}, bf16[256,1280]{1,0:T(8,128)(2,1)}, bf16[256,256]{1,0:T(8,128)(2,1)S(1)}, bf16[2,168,896]{2,1,0:T(8,128)(2,...) custom-call(s32[3]{0:T(128)S(1)} %get-tuple-element.61.ids, ...), custom_call_target="tpu_custom_call" | custom-call | flops 1 | bytes 1 | tf_op jit(solution)/shard_map/cond/branch_1_fun/pallas_call | solution.py:305
  175.3 11.4 %collective-permute-done.37.a_moved = bf16[2,168,896]{2,1,0:T(8,128)(2,1)S(1)} collective-permute-done((bf16[2,168,896]{2,1,0:T(8,128)(2,1)}, bf16[2,168,896]{2,1,0:T(8,128)(2,1)S(1)}, u32[]{:S(2)}, u32[]{:S(2)}) %collective-permute-start.37) | collective-permute-done | bytes 602144 | tf_op jit(solution)/shard_map/ppermute | solution.py:39
  193.1 13.0 %collective-permute-done.43.moved = bf16[192,1408]{1,0:T(8,128)(2,1)S(1)} collective-permute-done((bf16[192,1408]{1,0:T(8,128)(2,1)S(1)}, bf16[192,1408]{1,0:T(8,128)(2,1)S(1)}, u32[]{:S(2)}, u32[]{:S(2)}) %collective-permute-start.43) | collective-permute-done | bytes 540704 | tf_op jit(solution)/shard_map/ppermute | solution.py:39
  212.2 3.5 %collective-permute-done.44.first = bf16[2,32,1408]{2,1,0:T(8,128)(2,1)S(1)} collective-permute-done((bf16[2,32,1408]{2,1,0:T(8,128)(2,1)S(1)}, bf16[2,32,1408]{2,1,0:T(8,128)(2,1)S(1)}, u32[]{:S(2)}, u32[]{:S(2)}) %collective-permute-start.44) | collective-permute-done | bytes 180256 | tf_op jit(solution)/shard_map/ppermute | solution.py:39
  219.2 5.7 %collective-permute-done.41.moved = bf16[168,896]{1,0:T(8,128)(2,1)S(1)} collective-permute-done((bf16[168,896]{1,0:T(8,128)(2,1)S(1)}, bf16[168,896]{1,0:T(8,128)(2,1)S(1)}, u32[]{:S(2)}, u32[]{:S(2)}) %collective-permute-start.41) | collective-permute-done | bytes 301088 | tf_op jit(solution)/shard_map/ppermute | solution.py:39
  232.5 2.7 %collective-permute-done.32.moved = bf16[64,1024]{1,0:T(8,128)(2,1)S(1)} collective-permute-done((bf16[64,1024]{1,0:T(8,128)(2,1)S(1)}, bf16[64,1024]{1,0:T(8,128)(2,1)S(1)}, u32[]{:S(2)}, u32[]{:S(2)}) %collective-permute-start.32) | collective-permute-done | bytes 131104 | tf_op jit(solution)/shard_map/ppermute | solution.py:39
  (186 shorter events, 90.8 us)
Async XLA Ops:
  6.8 17.8 %collective-permute-start.8 = (bf16[64,2048]{1,0:T(8,128)(2,1)}, bf16[64,2048]{1,0:T(8,128)(2,1)}, u32[]{:S(2)}, u32[]{:S(2)}) collective-permute-start(bf16[64,2048]{1,0:T(8,128)(2,1)} %get-tuple-element.209), channel_id=1, source_target_pairs={{0,4},{1,5},{2,6},{3,7},{4,0},{5,1},{6,2},{7,3},{8,12},{9,13},{10,... | collective-permute-start | bytes 786440 | tf_op jit(solution)/shard_map/ppermute | solution.py:39
  17.3 19.6 %collective-permute-start.12 = (bf16[168,896]{1,0:T(8,128)(2,1)S(1)}, bf16[168,896]{1,0:T(8,128)(2,1)}, u32[]{:S(2)}, u32[]{:S(2)}) collective-permute-start(bf16[168,896]{1,0:T(8,128)(2,1)S(1)} %shard_map.241), channel_id=1, source_target_pairs={{0,8},{1,9},{2,10},{3,11},{4,12},{5,13},{6,14},{7,15},{8,0},{9,1},... | collective-permute-start | bytes 903176 | tf_op jit(solution)/shard_map/ppermute | solution.py:39
  18.8 16.5 %collective-permute-start.11 = (bf16[168,896]{1,0:T(8,128)(2,1)S(1)}, bf16[168,896]{1,0:T(8,128)(2,1)}, u32[]{:S(2)}, u32[]{:S(2)}) collective-permute-start(bf16[168,896]{1,0:T(8,128)(2,1)S(1)} %shard_map.241), channel_id=1, source_target_pairs={{0,4},{1,5},{2,6},{3,7},{4,0},{5,1},{6,2},{7,3},{8,12},{9,13},{10,... | collective-permute-start | bytes 903176 | tf_op jit(solution)/shard_map/ppermute | solution.py:39
  27.1 17.9 %collective-permute-start.9 = (bf16[128,1536]{1,0:T(8,128)(2,1)}, bf16[128,1536]{1,0:T(8,128)(2,1)S(1)}, u32[]{:S(2)}, u32[]{:S(2)}) collective-permute-start(bf16[128,1536]{1,0:T(8,128)(2,1)} %get-tuple-element.210.mine), channel_id=1, source_target_pairs={{0,2},{1,3},{2,0},{3,1},{4,6},{5,7},{6,4},{7,5},{8,10},{9,11},{10,... | collective-permute-start | bytes 1179656 | tf_op jit(solution)/shard_map/ppermute | solution.py:39
  36.8 25.3 %collective-permute-start.17 = (bf16[192,1408]{1,0:T(8,128)(2,1)S(1)}, bf16[192,1408]{1,0:T(8,128)(2,1)S(1)}, u32[]{:S(2)}, u32[]{:S(2)}) collective-permute-start(bf16[192,1408]{1,0:T(8,128)(2,1)S(1)} %shard_map.243), channel_id=1, source_target_pairs={{0,4},{1,5},{2,6},{3,7},{4,0},{5,1},{6,2},{7,3},{8,12},{9,13},{10,... | collective-permute-start | bytes 1622024 | tf_op jit(solution)/shard_map/ppermute | solution.py:39
  46.0 16.7 %collective-permute-start.14 = (bf16[2,168,896]{2,1,0:T(8,128)(2,1)S(1)}, bf16[2,168,896]{2,1,0:T(8,128)(2,1)S(1)}, u32[]{:S(2)}, u32[]{:S(2)}) collective-permute-start(bf16[2,168,896]{2,1,0:T(8,128)(2,1)S(1)} %pad_maximum_fusion.3.b0), channel_id=1, source_target_pairs={{0,16},{1,17},{2,18},{3,19},{4,20},{5,21},{6,22},{7,23},{8,24},{9,... | collective-permute-start | bytes 1806344 | tf_op jit(solution)/shard_map/ppermute | solution.py:39
  48.6 16.5 %collective-permute-start.15 = (bf16[2,168,896]{2,1,0:T(8,128)(2,1)S(1)}, bf16[2,168,896]{2,1,0:T(8,128)(2,1)S(1)}, u32[]{:S(2)}, u32[]{:S(2)}) collective-permute-start(bf16[2,168,896]{2,1,0:T(8,128)(2,1)S(1)} %pad_maximum_fusion.4.b2), channel_id=1, source_target_pairs={{0,8},{1,9},{2,10},{3,11},{4,12},{5,13},{6,14},{7,15},{8,0},{9,1},... | collective-permute-start | bytes 1806344 | tf_op jit(solution)/shard_map/ppermute | solution.py:39
  50.1 25.4 %collective-permute-start.16 = (bf16[192,1408]{1,0:T(8,128)(2,1)S(1)}, bf16[192,1408]{1,0:T(8,128)(2,1)S(1)}, u32[]{:S(2)}, u32[]{:S(2)}) collective-permute-start(bf16[192,1408]{1,0:T(8,128)(2,1)S(1)} %shard_map.243), channel_id=1, source_target_pairs={{0,8},{1,9},{2,10},{3,11},{4,12},{5,13},{6,14},{7,15},{8,0},{9,1},... | collective-permute-start | bytes 1622024 | tf_op jit(solution)/shard_map/ppermute | solution.py:39
  62.7 15.3 %collective-permute-start.10 = (bf16[256,1280]{1,0:T(8,128)(2,1)S(1)}, bf16[256,1280]{1,0:T(8,128)(2,1)S(1)}, u32[]{:S(2)}, u32[]{:S(2)}) collective-permute-start(bf16[256,1280]{1,0:T(8,128)(2,1)S(1)} %get-tuple-element.212.x2), channel_id=1, source_target_pairs={{0,1},{1,0},{2,3},{3,2},{4,5},{5,4},{6,7},{7,6},{8,9},{9,8},{10,11... | collective-permute-start | bytes 1966088 | tf_op jit(solution)/shard_map/ppermute | solution.py:39
  65.9 20.3 %collective-permute-start.23 = (bf16[256,1024]{1,0:T(8,128)(2,1)S(1)}, bf16[256,1024]{1,0:T(8,128)(2,1)S(1)}, u32[]{:S(2)}, u32[]{:S(2)}) collective-permute-start(bf16[256,1024]{1,0:T(8,128)(2,1)S(1)} %shard_map.246), channel_id=1, source_target_pairs={{0,2},{1,3},{2,0},{3,1},{4,6},{5,7},{6,4},{7,5},{8,10},{9,11},{10,... | collective-permute-start | bytes 1572872 | tf_op jit(solution)/shard_map/ppermute | solution.py:39
  75.6 28.3 %collective-permute-start.26 = (bf16[2,192,1408]{2,1,0:T(8,128)(2,1)S(1)}, bf16[2,192,1408]{2,1,0:T(8,128)(2,1)S(1)}, u32[]{:S(2)}, u32[]{:S(2)}) collective-permute-start(bf16[2,192,1408]{2,1,0:T(8,128)(2,1)S(1)} %pad_maximum_fusion.u0), channel_id=1, source_target_pairs={{0,16},{1,17},{2,18},{3,19},{4,20},{5,21},{6,22},{7,23},{8,24},{9,... | collective-permute-start | bytes 3244040 | tf_op jit(solution)/shard_map/ppermute | solution.py:39
  76.6 27.4 %collective-permute-start.27 = (bf16[2,192,1408]{2,1,0:T(8,128)(2,1)S(1)}, bf16[2,192,1408]{2,1,0:T(8,128)(2,1)S(1)}, u32[]{:S(2)}, u32[]{:S(2)}) collective-permute-start(bf16[2,192,1408]{2,1,0:T(8,128)(2,1)S(1)} %pad_maximum_fusion.1.u2), channel_id=1, source_target_pairs={{0,8},{1,9},{2,10},{3,11},{4,12},{5,13},{6,14},{7,15},{8,0},{9,1},... | collective-permute-start | bytes 3244040 | tf_op jit(solution)/shard_map/ppermute | solution.py:39
  119.4 27.5 %collective-permute-start.31 = (bf16[2,192,1408]{2,1,0:T(8,128)(2,1)}, bf16[2,192,1408]{2,1,0:T(8,128)(2,1)}, u32[]{:S(2)}, u32[]{:S(2)}) collective-permute-start(bf16[2,192,1408]{2,1,0:T(8,128)(2,1)} %get-tuple-element.248), channel_id=1, source_target_pairs={{0,8},{1,9},{2,10},{3,11},{4,12},{5,13},{6,14},{7,15},{8,0},{9,1},... | collective-permute-start | bytes 3244040 | tf_op jit(solution)/shard_map/ppermute | solution.py:39
  120.8 26.2 %collective-permute-start.30 = (bf16[2,192,1408]{2,1,0:T(8,128)(2,1)S(1)}, bf16[2,192,1408]{2,1,0:T(8,128)(2,1)}, u32[]{:S(2)}, u32[]{:S(2)}) collective-permute-start(bf16[2,192,1408]{2,1,0:T(8,128)(2,1)S(1)} %get-tuple-element.237), channel_id=1, source_target_pairs={{0,16},{1,17},{2,18},{3,19},{4,20},{5,21},{6,22},{7,23},{8,24},{9,... | collective-permute-start | bytes 3244040 | tf_op jit(solution)/shard_map/ppermute | solution.py:39
  150.8 17.5 %collective-permute-start.33 = (bf16[192,1408]{1,0:T(8,128)(2,1)}, bf16[192,1408]{1,0:T(8,128)(2,1)S(1)}, u32[]{:S(2)}, u32[]{:S(2)}) collective-permute-start(bf16[192,1408]{1,0:T(8,128)(2,1)} %get-tuple-element.253), channel_id=1, source_target_pairs={{0,16},{1,17},{2,18},{3,19},{4,20},{5,21},{6,22},{7,23},{8,24},{9,... | collective-permute-start | bytes 1622024 | tf_op jit(solution)/shard_map/ppermute | solution.py:39
  152.0 16.2 %collective-permute-start = (bf16[128,1024]{1,0:T(8,128)(2,1)}, bf16[128,1024]{1,0:T(8,128)(2,1)}, u32[]{:S(2)}, u32[]{:S(2)}) collective-permute-start(bf16[128,1024]{1,0:T(8,128)(2,1)} %get-tuple-element.60), channel_id=1, source_target_pairs={{0,2},{1,3},{2,0},{3,1},{4,6},{5,7},{6,4},{7,5},{8,10},{9,11},{10,... | collective-permute-start | bytes 786440 | tf_op jit(solution)/shard_map/cond/branch_1_fun/ppermute | solution.py:39
  170.9 15.9 %collective-permute-start.37 = (bf16[2,168,896]{2,1,0:T(8,128)(2,1)}, bf16[2,168,896]{2,1,0:T(8,128)(2,1)S(1)}, u32[]{:S(2)}, u32[]{:S(2)}) collective-permute-start(bf16[2,168,896]{2,1,0:T(8,128)(2,1)} %get-tuple-element.281), channel_id=1, source_target_pairs={{0,16},{1,17},{2,18},{3,19},{4,20},{5,21},{6,22},{7,23},{8,24},{9,... | collective-permute-start | bytes 1806344 | tf_op jit(solution)/shard_map/ppermute | solution.py:39
  171.7 16.7 %collective-permute-start.38 = (bf16[2,168,896]{2,1,0:T(8,128)(2,1)}, bf16[2,168,896]{2,1,0:T(8,128)(2,1)S(1)}, u32[]{:S(2)}, u32[]{:S(2)}) collective-permute-start(bf16[2,168,896]{2,1,0:T(8,128)(2,1)} %get-tuple-element.283), channel_id=1, source_target_pairs={{0,8},{1,9},{2,10},{3,11},{4,12},{5,13},{6,14},{7,15},{8,0},{9,1},... | collective-permute-start | bytes 1806344 | tf_op jit(solution)/shard_map/ppermute | solution.py:39
  172.4 18.9 %collective-permute-start.35 = (bf16[128,1536]{1,0:T(8,128)(2,1)S(1)}, bf16[128,1536]{1,0:T(8,128)(2,1)S(1)}, u32[]{:S(2)}, u32[]{:S(2)}) collective-permute-start(bf16[128,1536]{1,0:T(8,128)(2,1)S(1)} %get-tuple-element.272), channel_id=1, source_target_pairs={{0,2},{1,3},{2,0},{3,1},{4,6},{5,7},{6,4},{7,5},{8,10},{9,11},{10,... | collective-permute-start | bytes 1179656 | tf_op jit(solution)/shard_map/ppermute | solution.py:39
  172.9 33.3 %collective-permute-start.43 = (bf16[192,1408]{1,0:T(8,128)(2,1)S(1)}, bf16[192,1408]{1,0:T(8,128)(2,1)S(1)}, u32[]{:S(2)}, u32[]{:S(2)}) collective-permute-start(bf16[192,1408]{1,0:T(8,128)(2,1)S(1)} %shard_map.253), channel_id=1, source_target_pairs={{0,4},{1,5},{2,6},{3,7},{4,0},{5,1},{6,2},{7,3},{8,12},{9,13},{10,... | collective-permute-start | bytes 1622024 | tf_op jit(solution)/shard_map/ppermute | solution.py:39
  174.4 31.8 %collective-permute-start.42 = (bf16[192,1408]{1,0:T(8,128)(2,1)S(1)}, bf16[192,1408]{1,0:T(8,128)(2,1)S(1)}, u32[]{:S(2)}, u32[]{:S(2)}) collective-permute-start(bf16[192,1408]{1,0:T(8,128)(2,1)S(1)} %get-tuple-element.290), channel_id=1, source_target_pairs={{0,8},{1,9},{2,10},{3,11},{4,12},{5,13},{6,14},{7,15},{8,0},{9,1},... | collective-permute-start | bytes 1622024 | tf_op jit(solution)/shard_map/ppermute | solution.py:39
  190.0 20.2 %collective-permute-start.40 = (bf16[168,896]{1,0:T(8,128)(2,1)S(1)}, bf16[168,896]{1,0:T(8,128)(2,1)S(1)}, u32[]{:S(2)}, u32[]{:S(2)}) collective-permute-start(bf16[168,896]{1,0:T(8,128)(2,1)S(1)} %get-tuple-element.288), channel_id=1, source_target_pairs={{0,16},{1,17},{2,18},{3,19},{4,20},{5,21},{6,22},{7,23},{8,24},{9,... | collective-permute-start | bytes 903176 | tf_op jit(solution)/shard_map/ppermute | solution.py:39
  192.2 18.0 %collective-permute-start.36 = (bf16[64,2048]{1,0:T(8,128)(2,1)S(1)}, bf16[64,2048]{1,0:T(8,128)(2,1)S(1)}, u32[]{:S(2)}, u32[]{:S(2)}) collective-permute-start(bf16[64,2048]{1,0:T(8,128)(2,1)S(1)} %get-tuple-element.275), channel_id=1, source_target_pairs={{0,4},{1,5},{2,6},{3,7},{4,0},{5,1},{6,2},{7,3},{8,12},{9,13},{10,... | collective-permute-start | bytes 786440 | tf_op jit(solution)/shard_map/ppermute | solution.py:39
  210.3 14.6 %collective-permute-start.41 = (bf16[168,896]{1,0:T(8,128)(2,1)S(1)}, bf16[168,896]{1,0:T(8,128)(2,1)S(1)}, u32[]{:S(2)}, u32[]{:S(2)}) collective-permute-start(bf16[168,896]{1,0:T(8,128)(2,1)S(1)} %shard_map.258), channel_id=1, source_target_pairs={{0,4},{1,5},{2,6},{3,7},{4,0},{5,1},{6,2},{7,3},{8,12},{9,13},{10,... | collective-permute-start | bytes 903176 | tf_op jit(solution)/shard_map/ppermute | solution.py:39
  (52 other events, 427.4 us)

commit v8 on v7

--- a/solution.py
+++ b/solution.py
@@ -656,14 +656,16 @@
     out[...] = line_tiles_out(total[4 * ROWS:])
 
 
-def join_qkv_kernel(ids, kept, first, last, q, k, v, gains):
+def join_qkv_kernel(ids, kept, first, last, q, k, v, gain_one, gain_two):
     t = ids[2]
     parts = (kept[0], first[0], last[0], last[1])
     for s, part in zip(ORDER, parts):
         for i, ref in enumerate((q, k, v)):
             ref[:, aligned(t ^ s, HT)] = part[:, i * HT:(i + 1) * HT].astype(F32)
     low = [part[:, 3 * HT:].astype(F32) for part in parts]
-    gains[...] = (low[0] + low[1]) + (low[2] + low[3])
+    total = jnp.transpose((low[0] + low[1]) + (low[2] + low[3]))
+    gain_one[...] = total[0:1]
+    gain_two[...] = total[1:2]
 
 
 def join_hidden_kernel(ids, kept, first, last, gate, up, nat):
@@ -886,9 +888,9 @@
     gate_g, up_g = call(join_hidden_kernel, (shape((ROWS, 4 * FT), F32),) * 2, [SMEM] + [VMEM] * 3, parts,
                         [pltpu.VMEM((4, ROWS, 2 * FT), F32)])
     parts, out_g = finish(sum_qkv_kernel, q_sums, (ROWS, D), (gate_g,), (input_grad,))
-    query_g, key_g, value_g, gain_g = call(
-        join_qkv_kernel, (shape((ROWS, D), F32),) * 3 + (shape((ROWS, 128), F32),), [SMEM] + [VMEM] * 3, parts)
-    return (layer_out, input_grad, v1_out, gain_g[:, 0], query_g, key_g, value_g, out_g, gain_g[:, 1], gate_g, up_g, down_g)
+    query_g, key_g, value_g, gain_one_g, gain_two_g = call(
+        join_qkv_kernel, (shape((ROWS, D), F32),) * 3 + (shape((1, ROWS), F32),) * 2, [SMEM] + [VMEM] * 3, parts)
+    return (layer_out, input_grad, v1_out, gain_one_g.reshape(ROWS), query_g, key_g, value_g, out_g, gain_two_g.reshape(ROWS), gate_g, up_g, down_g)
 
 
 def local(plan, layer_in, *rest):

time: 239 us -> 238 us (level)
  no operation moved by 1% of the time
where the time goes in v8:
time: 238 us
  waiting for transfers between devices  105 us (44%)
  Pallas kernels  73.1 us (31%)
  starting transfers between devices  44.6 us (19%)
  local copies, waits for them, and re-layouts  8.3 us (3%)
  other arithmetic  6.03 us (3%)
    ppermute x48, waiting for transfers between devices, send(): return lax.ppermute(array, ALL, pairs)  105 us
    pallas_call x31, Pallas kernels, call(): pl.pallas_call(kernel, out_shape=outs, in_specs=specs, out_specs=jax.tree...  73.1 us
    ppermute x48, starting transfers between devices, send(): return lax.ppermute(array, ALL, pairs)  44.6 us
    unnamed x53, local copies, waits for them, and re-layouts  6.71 us
  transfers between devices with their start and end apart: 48, of which 24 were waited for; matrix products, arithmetic and copies ran while one was open for 3% of the time, Pallas kernels for 22%

profile of v8, /device:TPU:0, one launch (start us, length us, event | category | flops | bytes accessed | tf_op | source)
XLA Modules:
  0.0 237.8 jit_solution(16397747795793567884)
XLA Ops:
  0.8 2.9 %shard_map.238 = (bf16[2,32,896]{2,1,0:T(8,128)(2,1)}, bf16[2,32,896]{2,1,0:T(8,128)(2,1)}, bf16[40,896]{1,0:T(8,128)(2,1)}, bf16[64,2048]{1,0:T(8,128)(2,1)}, bf16[64,1024]{1,0:T(8,128)(2,1)}) custom-call(s32[3]{0:T(128)S(1)} %pad_add_fusion.ids, bf16[1,32]{1,0:T(2,128)(2,1)} %bitcast.25, bf16[1,32]{1,0:T(2,128)(2,1)} %bitcast.26, bf16[32,1024]{1,0:T(8,128)(2,1)} %wq.1, ...), custom_call_target="tpu_custom_call" | custom-call | flops 1 | bytes 1 | tf_op jit(solution)/shard_map/pallas_call | solution.py:305
  3.7 3.1 %collective-permute-start.5 = (bf16[2,32,896]{2,1,0:T(8,128)(2,1)}, bf16[2,32,896]{2,1,0:T(8,128)(2,1)S(1)}, u32[]{:S(2)}, u32[]{:S(2)}) collective-permute-start(bf16[2,32,896]{2,1,0:T(8,128)(2,1)} %get-tuple-element.201), channel_id=1, source_target_pairs={{0,2},{1,3},{2,0},{3,1},{4,6},{5,7},{6,4},{7,5},{8,10},{9,11},{10,... | collective-permute-start | bytes 344072 | tf_op jit(solution)/shard_map/ppermute | solution.py:39
  6.8 2.6 %collective-permute-start.8 = (bf16[64,2048]{1,0:T(8,128)(2,1)}, bf16[64,2048]{1,0:T(8,128)(2,1)}, u32[]{:S(2)}, u32[]{:S(2)}) collective-permute-start(bf16[64,2048]{1,0:T(8,128)(2,1)} %get-tuple-element.210), channel_id=1, source_target_pairs={{0,4},{1,5},{2,6},{3,7},{4,0},{5,1},{6,2},{7,3},{8,12},{9,13},{10,... | collective-permute-start | bytes 786440 | tf_op jit(solution)/shard_map/ppermute | solution.py:39
  9.4 2.7 %shard_map.239 = (bf16[2,32,1408]{2,1,0:T(8,128)(2,1)}, bf16[2,32,1408]{2,1,0:T(8,128)(2,1)}, bf16[64,1408]{1,0:T(8,128)(2,1)}) custom-call(s32[3]{0:T(128)S(1)} %pad_add_fusion.ids, bf16[32,2816]{1,0:T(8,128)(2,1)} %wg.1, bf16[32,2816]{1,0:T(8,128)(2,1)} %wu.1, bf16[88,1024]{1,0:T(8,128)(2,1)} %wd.1), custom_call_target="tpu_custom_call" | custom-call | flops 1 | bytes 1 | tf_op jit(solution)/shard_map/pallas_call | solution.py:305
  20.7 3.1 %fusion = (f32[512,256]{1,0:T(8,128)}, f32[512,256]{1,0:T(8,128)}) fusion(f32[256]{0:T(256)S(1)} %get-tuple-element.309, f32[256]{0:T(256)S(1)} %get-tuple-element.310, f32[512]{0:T(512)S(1)} %subtract_convert_fusion), kind=kLoop, calls=%fused_computation.10 | loop fusion | flops 262144 | bytes 1052672 | tf_op jit(solution)/shard_map/mul | solution.py:782
  29.6 5.7 %collective-permute-done.11 = bf16[168,896]{1,0:T(8,128)(2,1)} collective-permute-done((bf16[168,896]{1,0:T(8,128)(2,1)S(1)}, bf16[168,896]{1,0:T(8,128)(2,1)}, u32[]{:S(2)}, u32[]{:S(2)}) %collective-permute-start.11) | collective-permute-done | bytes 301088 | tf_op jit(solution)/shard_map/ppermute | solution.py:39
  37.9 7.0 %collective-permute-done.9.moved = bf16[128,1536]{1,0:T(8,128)(2,1)S(1)} collective-permute-done((bf16[128,1536]{1,0:T(8,128)(2,1)}, bf16[128,1536]{1,0:T(8,128)(2,1)S(1)}, u32[]{:S(2)}, u32[]{:S(2)}) %collective-permute-start.9) | collective-permute-done | bytes 393248 | tf_op jit(solution)/shard_map/ppermute | solution.py:39
  50.6 11.6 %collective-permute-done.17 = bf16[192,1408]{1,0:T(8,128)(2,1)S(1)} collective-permute-done((bf16[192,1408]{1,0:T(8,128)(2,1)S(1)}, bf16[192,1408]{1,0:T(8,128)(2,1)S(1)}, u32[]{:S(2)}, u32[]{:S(2)}) %collective-permute-start.17) | collective-permute-done | bytes 540704 | tf_op jit(solution)/shard_map/ppermute | solution.py:39
  67.6 7.9 %collective-permute-done.16 = bf16[192,1408]{1,0:T(8,128)(2,1)S(1)} collective-permute-done((bf16[192,1408]{1,0:T(8,128)(2,1)S(1)}, bf16[192,1408]{1,0:T(8,128)(2,1)S(1)}, u32[]{:S(2)}, u32[]{:S(2)}) %collective-permute-start.16) | collective-permute-done | bytes 540704 | tf_op jit(solution)/shard_map/ppermute | solution.py:39
  78.1 8.1 %shard_map.247 = (bf16[1024,896]{1,0:T(8,128)(2,1)}, bf16[512,1024]{1,0:T(8,128)(2,1)}, bf16[512,768]{1,0:T(8,128)(2,1)}, f32[512,256]{1,0:T(8,128)}, bf16[512,2...) custom-call(s32[3]{0:T(128)S(1)} %pad_add_fusion.ids, bf16[256,1280]{1,0:T(8,128)(2,1)S(1)} %get-tuple-element.213.x2, ...), custom_call_target="tpu_custom_call" | custom-call | flops 1 | bytes 1 | tf_op jit(solution)/shard_map/pallas_call | solution.py:305
  88.3 6.9 %collective-permute-done.21 = bf16[512,256]{1,0:T(8,128)(2,1)S(1)} collective-permute-done((bf16[512,256]{1,0:T(8,128)(2,1)S(1)}, bf16[512,256]{1,0:T(8,128)(2,1)S(1)}, u32[]{:S(2)}, u32[]{:S(2)}) %collective-permute-start.21) | collective-permute-done | bytes 262176 | tf_op jit(solution)/shard_map/ppermute | solution.py:39
  97.3 6.7 %shard_map.248 = (bf16[512,1024]{1,0:T(8,128)(2,1)}, f32[128,1024]{1,0:T(8,128)}, bf16[512,1024]{1,0:T(8,128)(2,1)S(1)}, bf16[256,1024]{1,0:T(8,128)(2,1)}) custom-call(s32[3]{0:T(128)S(1)} %pad_add_fusion.ids, bf16[256,1280]{1,0:T(8,128)(2,1)S(1)} %get-tuple-element.213.x2, bf16[256,1280]{1,0:T(8,128)(2,1)S(1)} %collective-permute-done.10.xc, ...), custom_call_target="tpu_custom_call" | custom-call | flops 1 | bytes 1 | tf_op jit(solution)/shard_map/pallas_call | solution.py:305
  105.4 13.1 %shard_map.249 = (bf16[256,1024]{1,0:T(8,128)(2,1)}, bf16[256,1024]{1,0:T(8,128)(2,1)}, bf16[256,1024]{1,0:T(8,128)(2,1)}, bf16[256,1024]{1,0:T(8,128)(2,1)}, f3...) custom-call(s32[3]{0:T(128)S(1)} %pad_add_fusion.ids, ...), custom_call_target="tpu_custom_call" | custom-call | flops 1 | bytes 1 | tf_op jit(solution)/shard_map/pallas_call | solution.py:305
  125.4 21.5 %conditional.2 = (f32[128,1024]{1,0:T(8,128)}, bf16[256,1024]{1,0:T(8,128)(2,1)}, bf16[256,1024]{1,0:T(8,128)(2,1)}, f32[128,1024]{1,0:T(8,128)}, bf16[128,1024]{1,0:T(8,128)(2,1)}) conditional(s32[]{:T(128)} %convert_element_type.21, () %tuple.46, (bf16[256,1024]{1,0:T(8,128)(2,1)}, bf16[256,1024]{1,0:T(8,128)(2,1)}, f32[128,1024]{1,0:T(8,128)}, ...), branch_computations={%region_1.2_spmd, %region_2.3_spmd} | conditional | flops 3 | bytes 9437403 | solution.py:744
  128.6 6.6 %collective-permute-done.1.moved = bf16[128,1024]{1,0:T(8,128)(2,1)S(1)} collective-permute-done((bf16[128,1024]{1,0:T(8,128)(2,1)S(1)}, bf16[128,1024]{1,0:T(8,128)(2,1)S(1)}, u32[]{:S(2)}, u32[]{:S(2)}) %collective-permute-start.1) | collective-permute-done | bytes 262176 | tf_op jit(solution)/shard_map/cond/branch_1_fun/ppermute | solution.py:39
  138.8 5.2 %collective-permute-done.2 = bf16[128,1024]{1,0:T(8,128)(2,1)S(1)} collective-permute-done((bf16[128,1024]{1,0:T(8,128)(2,1)S(1)}, bf16[128,1024]{1,0:T(8,128)(2,1)S(1)}, u32[]{:S(2)}, u32[]{:S(2)}) %collective-permute-start.2) | collective-permute-done | bytes 262176 | tf_op jit(solution)/shard_map/cond/branch_1_fun/ppermute | solution.py:39
  148.2 2.6 %shard_map.250 = (bf16[192,1408]{1,0:T(8,128)(2,1)S(1)}, bf16[192,1408]{1,0:T(8,128)(2,1)S(1)}, bf16[192,1408]{1,0:T(8,128)(2,1)S(1)}, bf16[192,1408]{1,0:T(8,128)(2,1)}) custom-call(bf16[2,192,1408]{2,1,0:T(8,128)(2,1)S(1)} %get-tuple-element.250.a_keep, bf16[2,192,1408]{2,1,0:T(8,128)(2,1)} %collective-permute-done.30.a_moved, ...), custom_call_target="tpu_custom_call" | custom-call | flops 1 | bytes 1 | tf_op jit(solution)/shard_map/pallas_call | solution.py:305
  152.0 16.2 %conditional.3 = (bf16[128,1024]{1,0:T(8,128)(2,1)}, bf16[256,1024]{1,0:T(8,128)(2,1)}, bf16[256,1280]{1,0:T(8,128)(2,1)}, bf16[256,256]{1,0:T(8,128)(2,1)S(1)},...) conditional(s32[]{:T(128)} %convert_element_type.21, () %tuple.62, ...), branch_computations={%region_3.4_spmd, %region_4.5_spmd} | conditional | flops 1 | bytes 3981392 | solution.py:744
  153.8 14.5 %branch_1_fun.7 = (bf16[256,1024]{1,0:T(8,128)(2,1)}, bf16[256,1280]{1,0:T(8,128)(2,1)}, bf16[256,256]{1,0:T(8,128)(2,1)S(1)}, bf16[2,168,896]{2,1,0:T(8,128)(2,...) custom-call(s32[3]{0:T(128)S(1)} %get-tuple-element.61.ids, ...), custom_call_target="tpu_custom_call" | custom-call | flops 1 | bytes 1 | tf_op jit(solution)/shard_map/cond/branch_1_fun/pallas_call | solution.py:305
  175.4 11.5 %collective-permute-done.37.a_moved = bf16[2,168,896]{2,1,0:T(8,128)(2,1)S(1)} collective-permute-done((bf16[2,168,896]{2,1,0:T(8,128)(2,1)}, bf16[2,168,896]{2,1,0:T(8,128)(2,1)S(1)}, u32[]{:S(2)}, u32[]{:S(2)}) %collective-permute-start.37) | collective-permute-done | bytes 602144 | tf_op jit(solution)/shard_map/ppermute | solution.py:39
  193.2 13.1 %collective-permute-done.43.moved = bf16[192,1408]{1,0:T(8,128)(2,1)S(1)} collective-permute-done((bf16[192,1408]{1,0:T(8,128)(2,1)S(1)}, bf16[192,1408]{1,0:T(8,128)(2,1)S(1)}, u32[]{:S(2)}, u32[]{:S(2)}) %collective-permute-start.43) | collective-permute-done | bytes 540704 | tf_op jit(solution)/shard_map/ppermute | solution.py:39
  212.2 3.5 %collective-permute-done.44.first = bf16[2,32,1408]{2,1,0:T(8,128)(2,1)S(1)} collective-permute-done((bf16[2,32,1408]{2,1,0:T(8,128)(2,1)S(1)}, bf16[2,32,1408]{2,1,0:T(8,128)(2,1)S(1)}, u32[]{:S(2)}, u32[]{:S(2)}) %collective-permute-start.44) | collective-permute-done | bytes 180256 | tf_op jit(solution)/shard_map/ppermute | solution.py:39
  219.3 5.7 %collective-permute-done.41.moved = bf16[168,896]{1,0:T(8,128)(2,1)S(1)} collective-permute-done((bf16[168,896]{1,0:T(8,128)(2,1)S(1)}, bf16[168,896]{1,0:T(8,128)(2,1)S(1)}, u32[]{:S(2)}, u32[]{:S(2)}) %collective-permute-start.41) | collective-permute-done | bytes 301088 | tf_op jit(solution)/shard_map/ppermute | solution.py:39
  232.5 2.7 %collective-permute-done.32.moved = bf16[64,1024]{1,0:T(8,128)(2,1)S(1)} collective-permute-done((bf16[64,1024]{1,0:T(8,128)(2,1)S(1)}, bf16[64,1024]{1,0:T(8,128)(2,1)S(1)}, u32[]{:S(2)}, u32[]{:S(2)}) %collective-permute-start.32) | collective-permute-done | bytes 131104 | tf_op jit(solution)/shard_map/ppermute | solution.py:39
  (185 shorter events, 90.0 us)
Async XLA Ops:
  6.8 17.8 %collective-permute-start.8 = (bf16[64,2048]{1,0:T(8,128)(2,1)}, bf16[64,2048]{1,0:T(8,128)(2,1)}, u32[]{:S(2)}, u32[]{:S(2)}) collective-permute-start(bf16[64,2048]{1,0:T(8,128)(2,1)} %get-tuple-element.210), channel_id=1, source_target_pairs={{0,4},{1,5},{2,6},{3,7},{4,0},{5,1},{6,2},{7,3},{8,12},{9,13},{10,... | collective-permute-start | bytes 786440 | tf_op jit(solution)/shard_map/ppermute | solution.py:39
  17.3 19.6 %collective-permute-start.12 = (bf16[168,896]{1,0:T(8,128)(2,1)S(1)}, bf16[168,896]{1,0:T(8,128)(2,1)}, u32[]{:S(2)}, u32[]{:S(2)}) collective-permute-start(bf16[168,896]{1,0:T(8,128)(2,1)S(1)} %shard_map.241), channel_id=1, source_target_pairs={{0,8},{1,9},{2,10},{3,11},{4,12},{5,13},{6,14},{7,15},{8,0},{9,1},... | collective-permute-start | bytes 903176 | tf_op jit(solution)/shard_map/ppermute | solution.py:39
  18.8 16.5 %collective-permute-start.11 = (bf16[168,896]{1,0:T(8,128)(2,1)S(1)}, bf16[168,896]{1,0:T(8,128)(2,1)}, u32[]{:S(2)}, u32[]{:S(2)}) collective-permute-start(bf16[168,896]{1,0:T(8,128)(2,1)S(1)} %shard_map.241), channel_id=1, source_target_pairs={{0,4},{1,5},{2,6},{3,7},{4,0},{5,1},{6,2},{7,3},{8,12},{9,13},{10,... | collective-permute-start | bytes 903176 | tf_op jit(solution)/shard_map/ppermute | solution.py:39
  27.1 17.9 %collective-permute-start.9 = (bf16[128,1536]{1,0:T(8,128)(2,1)}, bf16[128,1536]{1,0:T(8,128)(2,1)S(1)}, u32[]{:S(2)}, u32[]{:S(2)}) collective-permute-start(bf16[128,1536]{1,0:T(8,128)(2,1)} %get-tuple-element.211.mine), channel_id=1, source_target_pairs={{0,2},{1,3},{2,0},{3,1},{4,6},{5,7},{6,4},{7,5},{8,10},{9,11},{10,... | collective-permute-start | bytes 1179656 | tf_op jit(solution)/shard_map/ppermute | solution.py:39
  36.8 25.3 %collective-permute-start.17 = (bf16[192,1408]{1,0:T(8,128)(2,1)S(1)}, bf16[192,1408]{1,0:T(8,128)(2,1)S(1)}, u32[]{:S(2)}, u32[]{:S(2)}) collective-permute-start(bf16[192,1408]{1,0:T(8,128)(2,1)S(1)} %shard_map.243), channel_id=1, source_target_pairs={{0,4},{1,5},{2,6},{3,7},{4,0},{5,1},{6,2},{7,3},{8,12},{9,13},{10,... | collective-permute-start | bytes 1622024 | tf_op jit(solution)/shard_map/ppermute | solution.py:39
  46.0 16.7 %collective-permute-start.14 = (bf16[2,168,896]{2,1,0:T(8,128)(2,1)S(1)}, bf16[2,168,896]{2,1,0:T(8,128)(2,1)S(1)}, u32[]{:S(2)}, u32[]{:S(2)}) collective-permute-start(bf16[2,168,896]{2,1,0:T(8,128)(2,1)S(1)} %pad_maximum_fusion.3.b0), channel_id=1, source_target_pairs={{0,16},{1,17},{2,18},{3,19},{4,20},{5,21},{6,22},{7,23},{8,24},{9,... | collective-permute-start | bytes 1806344 | tf_op jit(solution)/shard_map/ppermute | solution.py:39
  48.6 16.5 %collective-permute-start.15 = (bf16[2,168,896]{2,1,0:T(8,128)(2,1)S(1)}, bf16[2,168,896]{2,1,0:T(8,128)(2,1)S(1)}, u32[]{:S(2)}, u32[]{:S(2)}) collective-permute-start(bf16[2,168,896]{2,1,0:T(8,128)(2,1)S(1)} %pad_maximum_fusion.4.b2), channel_id=1, source_target_pairs={{0,8},{1,9},{2,10},{3,11},{4,12},{5,13},{6,14},{7,15},{8,0},{9,1},... | collective-permute-start | bytes 1806344 | tf_op jit(solution)/shard_map/ppermute | solution.py:39
  50.1 25.4 %collective-permute-start.16 = (bf16[192,1408]{1,0:T(8,128)(2,1)S(1)}, bf16[192,1408]{1,0:T(8,128)(2,1)S(1)}, u32[]{:S(2)}, u32[]{:S(2)}) collective-permute-start(bf16[192,1408]{1,0:T(8,128)(2,1)S(1)} %shard_map.243), channel_id=1, source_target_pairs={{0,8},{1,9},{2,10},{3,11},{4,12},{5,13},{6,14},{7,15},{8,0},{9,1},... | collective-permute-start | bytes 1622024 | tf_op jit(solution)/shard_map/ppermute | solution.py:39
  62.7 15.4 %collective-permute-start.10 = (bf16[256,1280]{1,0:T(8,128)(2,1)S(1)}, bf16[256,1280]{1,0:T(8,128)(2,1)S(1)}, u32[]{:S(2)}, u32[]{:S(2)}) collective-permute-start(bf16[256,1280]{1,0:T(8,128)(2,1)S(1)} %get-tuple-element.213.x2), channel_id=1, source_target_pairs={{0,1},{1,0},{2,3},{3,2},{4,5},{5,4},{6,7},{7,6},{8,9},{9,8},{10,11... | collective-permute-start | bytes 1966088 | tf_op jit(solution)/shard_map/ppermute | solution.py:39
  65.9 20.4 %collective-permute-start.23 = (bf16[256,1024]{1,0:T(8,128)(2,1)S(1)}, bf16[256,1024]{1,0:T(8,128)(2,1)S(1)}, u32[]{:S(2)}, u32[]{:S(2)}) collective-permute-start(bf16[256,1024]{1,0:T(8,128)(2,1)S(1)} %shard_map.246), channel_id=1, source_target_pairs={{0,2},{1,3},{2,0},{3,1},{4,6},{5,7},{6,4},{7,5},{8,10},{9,11},{10,... | collective-permute-start | bytes 1572872 | tf_op jit(solution)/shard_map/ppermute | solution.py:39
  75.6 28.4 %collective-permute-start.26 = (bf16[2,192,1408]{2,1,0:T(8,128)(2,1)S(1)}, bf16[2,192,1408]{2,1,0:T(8,128)(2,1)S(1)}, u32[]{:S(2)}, u32[]{:S(2)}) collective-permute-start(bf16[2,192,1408]{2,1,0:T(8,128)(2,1)S(1)} %pad_maximum_fusion.u0), channel_id=1, source_target_pairs={{0,16},{1,17},{2,18},{3,19},{4,20},{5,21},{6,22},{7,23},{8,24},{9,... | collective-permute-start | bytes 3244040 | tf_op jit(solution)/shard_map/ppermute | solution.py:39
  76.6 27.4 %collective-permute-start.27 = (bf16[2,192,1408]{2,1,0:T(8,128)(2,1)S(1)}, bf16[2,192,1408]{2,1,0:T(8,128)(2,1)S(1)}, u32[]{:S(2)}, u32[]{:S(2)}) collective-permute-start(bf16[2,192,1408]{2,1,0:T(8,128)(2,1)S(1)} %pad_maximum_fusion.1.u2), channel_id=1, source_target_pairs={{0,8},{1,9},{2,10},{3,11},{4,12},{5,13},{6,14},{7,15},{8,0},{9,1},... | collective-permute-start | bytes 3244040 | tf_op jit(solution)/shard_map/ppermute | solution.py:39
  119.4 27.5 %collective-permute-start.31 = (bf16[2,192,1408]{2,1,0:T(8,128)(2,1)}, bf16[2,192,1408]{2,1,0:T(8,128)(2,1)}, u32[]{:S(2)}, u32[]{:S(2)}) collective-permute-start(bf16[2,192,1408]{2,1,0:T(8,128)(2,1)} %get-tuple-element.249), channel_id=1, source_target_pairs={{0,8},{1,9},{2,10},{3,11},{4,12},{5,13},{6,14},{7,15},{8,0},{9,1},... | collective-permute-start | bytes 3244040 | tf_op jit(solution)/shard_map/ppermute | solution.py:39
  120.8 26.2 %collective-permute-start.30 = (bf16[2,192,1408]{2,1,0:T(8,128)(2,1)S(1)}, bf16[2,192,1408]{2,1,0:T(8,128)(2,1)}, u32[]{:S(2)}, u32[]{:S(2)}) collective-permute-start(bf16[2,192,1408]{2,1,0:T(8,128)(2,1)S(1)} %get-tuple-element.238), channel_id=1, source_target_pairs={{0,16},{1,17},{2,18},{3,19},{4,20},{5,21},{6,22},{7,23},{8,24},{9,... | collective-permute-start | bytes 3244040 | tf_op jit(solution)/shard_map/ppermute | solution.py:39
  150.8 17.5 %collective-permute-start.33 = (bf16[192,1408]{1,0:T(8,128)(2,1)}, bf16[192,1408]{1,0:T(8,128)(2,1)S(1)}, u32[]{:S(2)}, u32[]{:S(2)}) collective-permute-start(bf16[192,1408]{1,0:T(8,128)(2,1)} %get-tuple-element.254), channel_id=1, source_target_pairs={{0,16},{1,17},{2,18},{3,19},{4,20},{5,21},{6,22},{7,23},{8,24},{9,... | collective-permute-start | bytes 1622024 | tf_op jit(solution)/shard_map/ppermute | solution.py:39
  152.0 16.2 %collective-permute-start = (bf16[128,1024]{1,0:T(8,128)(2,1)}, bf16[128,1024]{1,0:T(8,128)(2,1)}, u32[]{:S(2)}, u32[]{:S(2)}) collective-permute-start(bf16[128,1024]{1,0:T(8,128)(2,1)} %get-tuple-element.60), channel_id=1, source_target_pairs={{0,2},{1,3},{2,0},{3,1},{4,6},{5,7},{6,4},{7,5},{8,10},{9,11},{10,... | collective-permute-start | bytes 786440 | tf_op jit(solution)/shard_map/cond/branch_1_fun/ppermute | solution.py:39
  170.9 15.9 %collective-permute-start.37 = (bf16[2,168,896]{2,1,0:T(8,128)(2,1)}, bf16[2,168,896]{2,1,0:T(8,128)(2,1)S(1)}, u32[]{:S(2)}, u32[]{:S(2)}) collective-permute-start(bf16[2,168,896]{2,1,0:T(8,128)(2,1)} %get-tuple-element.282), channel_id=1, source_target_pairs={{0,16},{1,17},{2,18},{3,19},{4,20},{5,21},{6,22},{7,23},{8,24},{9,... | collective-permute-start | bytes 1806344 | tf_op jit(solution)/shard_map/ppermute | solution.py:39
  171.7 16.7 %collective-permute-start.38 = (bf16[2,168,896]{2,1,0:T(8,128)(2,1)}, bf16[2,168,896]{2,1,0:T(8,128)(2,1)S(1)}, u32[]{:S(2)}, u32[]{:S(2)}) collective-permute-start(bf16[2,168,896]{2,1,0:T(8,128)(2,1)} %get-tuple-element.284), channel_id=1, source_target_pairs={{0,8},{1,9},{2,10},{3,11},{4,12},{5,13},{6,14},{7,15},{8,0},{9,1},... | collective-permute-start | bytes 1806344 | tf_op jit(solution)/shard_map/ppermute | solution.py:39
  172.4 18.9 %collective-permute-start.35 = (bf16[128,1536]{1,0:T(8,128)(2,1)S(1)}, bf16[128,1536]{1,0:T(8,128)(2,1)S(1)}, u32[]{:S(2)}, u32[]{:S(2)}) collective-permute-start(bf16[128,1536]{1,0:T(8,128)(2,1)S(1)} %get-tuple-element.273), channel_id=1, source_target_pairs={{0,2},{1,3},{2,0},{3,1},{4,6},{5,7},{6,4},{7,5},{8,10},{9,11},{10,... | collective-permute-start | bytes 1179656 | tf_op jit(solution)/shard_map/ppermute | solution.py:39
  172.9 33.3 %collective-permute-start.43 = (bf16[192,1408]{1,0:T(8,128)(2,1)S(1)}, bf16[192,1408]{1,0:T(8,128)(2,1)S(1)}, u32[]{:S(2)}, u32[]{:S(2)}) collective-permute-start(bf16[192,1408]{1,0:T(8,128)(2,1)S(1)} %shard_map.253), channel_id=1, source_target_pairs={{0,4},{1,5},{2,6},{3,7},{4,0},{5,1},{6,2},{7,3},{8,12},{9,13},{10,... | collective-permute-start | bytes 1622024 | tf_op jit(solution)/shard_map/ppermute | solution.py:39
  174.4 31.8 %collective-permute-start.42 = (bf16[192,1408]{1,0:T(8,128)(2,1)S(1)}, bf16[192,1408]{1,0:T(8,128)(2,1)S(1)}, u32[]{:S(2)}, u32[]{:S(2)}) collective-permute-start(bf16[192,1408]{1,0:T(8,128)(2,1)S(1)} %get-tuple-element.291), channel_id=1, source_target_pairs={{0,8},{1,9},{2,10},{3,11},{4,12},{5,13},{6,14},{7,15},{8,0},{9,1},... | collective-permute-start | bytes 1622024 | tf_op jit(solution)/shard_map/ppermute | solution.py:39
  190.0 20.2 %collective-permute-start.40 = (bf16[168,896]{1,0:T(8,128)(2,1)S(1)}, bf16[168,896]{1,0:T(8,128)(2,1)S(1)}, u32[]{:S(2)}, u32[]{:S(2)}) collective-permute-start(bf16[168,896]{1,0:T(8,128)(2,1)S(1)} %get-tuple-element.289), channel_id=1, source_target_pairs={{0,16},{1,17},{2,18},{3,19},{4,20},{5,21},{6,22},{7,23},{8,24},{9,... | collective-permute-start | bytes 903176 | tf_op jit(solution)/shard_map/ppermute | solution.py:39
  192.3 18.0 %collective-permute-start.36 = (bf16[64,2048]{1,0:T(8,128)(2,1)S(1)}, bf16[64,2048]{1,0:T(8,128)(2,1)S(1)}, u32[]{:S(2)}, u32[]{:S(2)}) collective-permute-start(bf16[64,2048]{1,0:T(8,128)(2,1)S(1)} %get-tuple-element.276), channel_id=1, source_target_pairs={{0,4},{1,5},{2,6},{3,7},{4,0},{5,1},{6,2},{7,3},{8,12},{9,13},{10,... | collective-permute-start | bytes 786440 | tf_op jit(solution)/shard_map/ppermute | solution.py:39
  210.4 14.6 %collective-permute-start.41 = (bf16[168,896]{1,0:T(8,128)(2,1)S(1)}, bf16[168,896]{1,0:T(8,128)(2,1)S(1)}, u32[]{:S(2)}, u32[]{:S(2)}) collective-permute-start(bf16[168,896]{1,0:T(8,128)(2,1)S(1)} %shard_map.258), channel_id=1, source_target_pairs={{0,4},{1,5},{2,6},{3,7},{4,0},{5,1},{6,2},{7,3},{8,12},{9,13},{10,... | collective-permute-start | bytes 903176 | tf_op jit(solution)/shard_map/ppermute | solution.py:39
  (52 other events, 427.5 us)
